TPU v7x, 32 devices: a whole 2x2x4 slice. The times are simulated.
32 devices in a mesh: crop: 4 (over y, x), img: 8 (over z, core).
Axes of the slice: x: 2, y: 2, z: 4, core: 2. Of those that a mesh axis runs over, the one named last changes fastest.
Arguments:
- pixels: bfloat16 [4, 8, 784, 2016], P('crop', 'img'), may hold values from -6 to 6
- counts: int32 [8, 4], P('img'), may hold values from 1 to 10, 32 in all within a row
- slot_order: int32 [8, 32], P('img'), may hold values from 0 to 31, each once within a row
- w_in: bfloat16 [2016, 2016], replicated, may hold values from -0.125 to 0.125
- kernel: bfloat16 [9, 36, 56, 56], replicated, may hold values from -0.25 to 0.25
- w_red: bfloat16 [2016, 504], replicated, may hold values from -0.125 to 0.125
- b_red: float32 [504], replicated, may hold values from -3 to 3
- w_exp: bfloat16 [504, 2016], replicated, may hold values from -0.25 to 0.25
- b_exp: float32 [2016], replicated, may hold values from -3 to 3
- w_out: bfloat16 [2016, 2016], replicated, may hold values from -0.125 to 0.125
- gain_one: float32 [2016], replicated, may hold values from 0.5 to 1.5
- shift_one: float32 [2016], replicated, may hold values from -1.8 to 1.8
- gain_two: float32 [2016], replicated, may hold values from 0.5 to 1.5
- shift_two: float32 [2016], replicated, may hold values from -1.8 to 1.8
- gain_three: float32 [2016], replicated, may hold values from 0.5 to 1.5
- shift_three: float32 [2016], replicated, may hold values from -1.8 to 1.8
- protos: bfloat16 [2016, 3000], replicated, may hold values from -1.1953125 to 1.1953125
Outputs:
- loss: float32 [], replicated
- block_out: bfloat16 [4, 8, 784, 2016], P('crop', 'img')
- grad_pixels: float32 [4, 8, 784, 2016], P('crop', 'img')
- grad_w_in: float32 [4064256], P('img')
- grad_kernel: float32 [1016064], P('img')
- grad_w_red: float32 [1016064], P('img')
- grad_w_exp: float32 [1016064], P('img')
- grad_w_out: float32 [4064256], P('img')
- grad_protos: float32 [6048000], P('img')
- grad_b_red: float32 [504], replicated
- grad_b_exp: float32 [2016], replicated
- grad_gain_one: float32 [2016], replicated
- grad_shift_one: float32 [2016], replicated
- grad_gain_two: float32 [2016], replicated
- grad_shift_two: float32 [2016], replicated
- grad_gain_three: float32 [2016], replicated
- grad_shift_three: float32 [2016], replicated
Inputs may be any that keep to these rules, and one draw needn't show every extreme that they name: `counts`: each row sums to 32 and its largest entry is 10. `slot_order`: each row is a permutation.
All inputs are finite; a program needn't handle non-finite values.
Results may differ from a plain program's by a relative error of at most 0.015.
Values sent between devices are 32-bit elements; how exact they have to be, the bound alone decides.
No kernel may reach another device: no remote copies, remote signals or barrier semaphores. Data moves between devices by JAX's collectives and lax.ppermute only.
A program may use at most 448 MiB of HBM per device.

v0:
```python
import jax
import jax.numpy as jnp
from jax import lax
from jax.sharding import PartitionSpec as P

IMG_DEV = 4
SIDE = 14
SMALL_SIDE = 7


norm_epsilon = 1e-05
length_epsilon = 1e-06
sharpening_divisor = 0.1
sharpness = 0.05
exact_mode = lax.Precision.HIGHEST


def from_partner(value, axis, stride):
    mask = 2**stride
    pairs = [(source, source ^ mask) for source in range(lax.axis_size(axis))]
    return lax.ppermute(value, axis, pairs)


def smooth_gate(values):
    return values * jax.nn.sigmoid(values)


def smooth_slope(values):
    sigma_values = jax.nn.sigmoid(values)
    return sigma_values * (1.0 + values * (1.0 - sigma_values))


def exact_dot(left, right):
    return jnp.dot(left, right, precision=exact_mode, preferred_element_type=jnp.float32)


def conv_forward(field_rows, kernel, crop_count, edge_cells):
    group_count = kernel.shape[1]
    group_width = kernel.shape[2]
    grid_view = field_rows.reshape(crop_count, edge_cells, edge_cells, group_count, group_width)
    padded = jnp.pad(grid_view, ((0, 0), (1, 1), (1, 1), (0, 0), (0, 0)))
    summed = jnp.zeros(grid_view.shape, jnp.float32)
    for offset_index in range(9):
        row_shift = offset_index // 3
        col_shift = offset_index % 3
        window = padded[:, row_shift : row_shift + edge_cells, col_shift : col_shift + edge_cells]
        summed = summed + jnp.einsum(
            "nhwgc,gcd->nhwgd", window, kernel[offset_index], preferred_element_type=jnp.float32
        )
    return summed.reshape(field_rows.shape[0], group_count * group_width)


def conv_backward(field_rows, grad_rows, kernel, crop_count, edge_cells):
    group_count = kernel.shape[1]
    group_width = kernel.shape[2]
    grid_view = field_rows.reshape(crop_count, edge_cells, edge_cells, group_count, group_width)
    grad_view = grad_rows.reshape(crop_count, edge_cells, edge_cells, group_count, group_width)
    padded_in = jnp.pad(grid_view, ((0, 0), (1, 1), (1, 1), (0, 0), (0, 0)))
    padded_grad = jnp.pad(grad_view, ((0, 0), (1, 1), (1, 1), (0, 0), (0, 0)))
    grad_field = jnp.zeros(grid_view.shape, jnp.float32)
    kernel_parts = []
    for offset_index in range(9):
        row_shift = offset_index // 3
        col_shift = offset_index % 3
        window = padded_in[
            :, row_shift : row_shift + edge_cells, col_shift : col_shift + edge_cells
        ]
        kernel_parts.append(
            jnp.einsum("nhwgc,nhwgd->gcd", window, grad_view, preferred_element_type=jnp.float32)
        )
        back_window = padded_grad[
            :,
            2 - row_shift : 2 - row_shift + edge_cells,
            2 - col_shift : 2 - col_shift + edge_cells,
        ]
        grad_field = grad_field + jnp.einsum(
            "nhwgd,gcd->nhwgc",
            back_window,
            kernel[offset_index],
            preferred_element_type=jnp.float32,
        )
    return (
        grad_field.reshape(field_rows.shape[0], group_count * group_width),
        jnp.stack(kernel_parts),
    )


def shards(
    pixels,
    counts,
    slot_order,
    w_in,
    kernel,
    w_red,
    b_red,
    w_exp,
    b_exp,
    w_out,
    gain_one,
    shift_one,
    gain_two,
    shift_two,
    gain_three,
    shift_three,
    protos,
):
    row_count = pixels.shape[2]
    feature_width = pixels.shape[3]
    proto_count = protos.shape[1]
    seg_count = row_count // (SMALL_SIDE * SMALL_SIDE)
    slot_total = slot_order.shape[1]
    img_devices = lax.axis_size("img")
    crop_index = lax.axis_index("crop")
    is_global = crop_index < 2
    stream_rows = 2.0 * img_devices * row_count
    couple_number = 2.0 * img_devices * (IMG_DEV + slot_total)
    inputs = pixels.reshape(row_count, feature_width)
    row_ids = jnp.arange(row_count, dtype=jnp.int32)
    seg_of_row = jnp.where(
        is_global, row_ids // (SIDE * SIDE), row_ids // (SMALL_SIDE * SMALL_SIDE)
    )
    member = (seg_of_row[None, :] == jnp.arange(seg_count, dtype=jnp.int32)[:, None]).astype(
        jnp.float32
    )
    member_rows = member.T
    crop_pixels = jnp.where(is_global, float(SIDE * SIDE), float(SMALL_SIDE * SMALL_SIDE))

    def normalize(hidden, gain, shift):
        local_sums = jnp.stack([jnp.sum(hidden, axis=0), jnp.sum(hidden * hidden, axis=0)])
        within = lax.psum(local_sums, "img")
        stream_sums = within + from_partner(within, "crop", 0)
        average = stream_sums[0] / stream_rows
        scale_inv = lax.rsqrt(stream_sums[1] / stream_rows - average * average + norm_epsilon)
        centred = (hidden - average) * scale_inv
        return (centred, scale_inv, centred * gain + shift)

    def norm_back(grad_act, centred, scale_inv, gain):
        local_sums = jnp.stack([jnp.sum(grad_act, axis=0), jnp.sum(grad_act * centred, axis=0)])
        within = lax.psum(local_sums, "img")
        stream_sums = within + from_partner(within, "crop", 0)
        grad_hidden = (
            gain
            * scale_inv
            * (grad_act - stream_sums[0] / stream_rows - centred * stream_sums[1] / stream_rows)
        )
        return (grad_hidden, local_sums)

    def conv_global(field_rows, kernel_now):
        return conv_forward(field_rows, kernel_now, IMG_DEV, SIDE)

    def conv_small(field_rows, kernel_now):
        return conv_forward(field_rows, kernel_now, seg_count, SMALL_SIDE)

    def back_global(field_rows, grad_rows, kernel_now):
        return conv_backward(field_rows, grad_rows, kernel_now, IMG_DEV, SIDE)

    def back_small(field_rows, grad_rows, kernel_now):
        return conv_backward(field_rows, grad_rows, kernel_now, seg_count, SMALL_SIDE)

    hidden_one = jnp.dot(inputs, w_in, preferred_element_type=jnp.float32)
    centred_one, inv_one, pre_one = normalize(hidden_one, gain_one, shift_one)
    act_one = smooth_gate(pre_one).astype(jnp.bfloat16)
    hidden_two = lax.cond(is_global, conv_global, conv_small, act_one, kernel)
    centred_two, inv_two, pre_two = normalize(hidden_two, gain_two, shift_two)
    act_two = smooth_gate(pre_two)
    red_float = w_red.astype(jnp.float32)
    exp_float = w_exp.astype(jnp.float32)
    pooled = exact_dot(member, act_two) / crop_pixels
    reduce_pre = exact_dot(pooled, red_float) + b_red
    reduced = smooth_gate(reduce_pre)
    gate_values = jax.nn.sigmoid(exact_dot(reduced, exp_float) + b_exp)
    gate_rows = exact_dot(member_rows, gate_values)
    excited = (act_two * gate_rows).astype(jnp.bfloat16)
    hidden_three = jnp.dot(excited, w_out, preferred_element_type=jnp.float32)
    centred_three, inv_three, branch = normalize(hidden_three, gain_three, shift_three)
    summed_in = inputs.astype(jnp.float32) + branch
    output = smooth_gate(summed_in)
    pooled_out = exact_dot(member, output) / crop_pixels
    length_inv = lax.rsqrt(jnp.sum(pooled_out * pooled_out, axis=1, keepdims=True) + length_epsilon)
    unit_rows = (pooled_out * length_inv).astype(jnp.bfloat16)
    match_matrix = jnp.dot(unit_rows, protos, preferred_element_type=jnp.float32)
    plan_rows = jnp.exp(match_matrix[:IMG_DEV] / sharpness)
    for sweep_index in range(3):
        plan_rows = plan_rows / lax.psum(jnp.sum(plan_rows, axis=0), "img")
        plan_rows = plan_rows / jnp.sum(plan_rows, axis=1, keepdims=True)
    all_codes = lax.all_gather(plan_rows, "crop", axis=0, tiled=True)
    first_codes = all_codes[:IMG_DEV]
    second_codes = all_codes[IMG_DEV : 2 * IMG_DEV]
    partner = jnp.where(crop_index == 0, second_codes, first_codes)
    wide_target = jnp.concatenate(
        [partner, jnp.zeros((seg_count - IMG_DEV, proto_count), jnp.float32)], axis=0
    )
    ends = jnp.cumsum(counts[0])
    first_slot = jnp.maximum(crop_index - 2, 0) * seg_count
    order_here = lax.dynamic_slice_in_dim(slot_order[0], first_slot, seg_count)
    owner = jnp.sum((order_here[:, None] >= ends[None, :]).astype(jnp.int32), axis=1)
    picks = (owner[:, None] == jnp.arange(IMG_DEV, dtype=jnp.int32)[None, :]).astype(jnp.float32)
    narrow_target = exact_dot(picks, first_codes + second_codes)
    target = jnp.where(is_global, wide_target, narrow_target)
    sharpened = match_matrix / sharpening_divisor
    shifted = sharpened - jnp.max(sharpened, axis=1, keepdims=True)
    log_probs = shifted - jnp.log(jnp.sum(jnp.exp(shifted), axis=1, keepdims=True))
    loss_here = -jnp.sum(target * log_probs) / couple_number
    grad_scores = (
        (jnp.exp(log_probs) * jnp.sum(target, axis=1, keepdims=True) - target)
        / (sharpening_divisor * couple_number)
    ).astype(jnp.bfloat16)
    grad_protos = jnp.einsum(
        "sw,sk->wk", unit_rows, grad_scores, preferred_element_type=jnp.float32
    )
    grad_unit = jnp.einsum("sk,wk->sw", grad_scores, protos, preferred_element_type=jnp.float32)
    inner_term = jnp.sum(pooled_out * grad_unit, axis=1, keepdims=True)
    grad_pooled_out = (
        length_inv * grad_unit - pooled_out * length_inv * length_inv * length_inv * inner_term
    )
    grad_output = exact_dot(member_rows, grad_pooled_out / crop_pixels)
    grad_summed = grad_output * smooth_slope(summed_in)
    grad_hidden_three, sums_three = norm_back(grad_summed, centred_three, inv_three, gain_three)
    grad_three_low = grad_hidden_three.astype(jnp.bfloat16)
    grad_w_out = jnp.einsum(
        "rw,rv->wv", excited, grad_three_low, preferred_element_type=jnp.float32
    )
    grad_excited = jnp.einsum(
        "rv,wv->rw", grad_three_low, w_out, preferred_element_type=jnp.float32
    )
    grad_gate = exact_dot(member, grad_excited * act_two)
    grad_gate_pre = grad_gate * gate_values * (1.0 - gate_values)
    grad_w_exp = exact_dot(reduced.T, grad_gate_pre)
    grad_reduce_pre = exact_dot(grad_gate_pre, exp_float.T) * smooth_slope(reduce_pre)
    grad_w_red = exact_dot(pooled.T, grad_reduce_pre)
    grad_pooled = exact_dot(grad_reduce_pre, red_float.T)
    grad_act_two = grad_excited * gate_rows + exact_dot(member_rows, grad_pooled / crop_pixels)
    grad_hidden_two, sums_two = norm_back(
        grad_act_two * smooth_slope(pre_two), centred_two, inv_two, gain_two
    )
    grad_two_low = grad_hidden_two.astype(jnp.bfloat16)
    grad_act_one, grad_kernel = lax.cond(
        is_global, back_global, back_small, act_one, grad_two_low, kernel
    )
    grad_hidden_one, sums_one = norm_back(
        grad_act_one * smooth_slope(pre_one), centred_one, inv_one, gain_one
    )
    grad_one_low = grad_hidden_one.astype(jnp.bfloat16)
    grad_w_in = jnp.einsum("rw,rv->wv", inputs, grad_one_low, preferred_element_type=jnp.float32)
    grad_inputs = (
        jnp.einsum("rv,wv->rw", grad_one_low, w_in, preferred_element_type=jnp.float32)
        + grad_summed
    )
    local_norm_sums = jnp.stack([sums_one, sums_two, sums_three])
    loss_total, grad_b_red, grad_b_exp, norm_sums = lax.psum(
        (
            loss_here,
            jnp.sum(grad_reduce_pre, axis=0),
            jnp.sum(grad_gate_pre, axis=0),
            local_norm_sums,
        ),
        ("crop", "img"),
    )
    flat_in = grad_w_in.reshape(-1)
    flat_kernel = grad_kernel.reshape(-1)
    flat_red = grad_w_red.reshape(-1)
    flat_exp = grad_w_exp.reshape(-1)
    flat_out = grad_w_out.reshape(-1)
    flat_protos = grad_protos.reshape(-1)
    shares = (
        lax.psum_scatter(flat_in, "img", scatter_dimension=0, tiled=True),
        lax.psum_scatter(flat_kernel, "img", scatter_dimension=0, tiled=True),
        lax.psum_scatter(flat_red, "img", scatter_dimension=0, tiled=True),
        lax.psum_scatter(flat_exp, "img", scatter_dimension=0, tiled=True),
        lax.psum_scatter(flat_out, "img", scatter_dimension=0, tiled=True),
        lax.psum_scatter(flat_protos, "img", scatter_dimension=0, tiled=True),
    )
    shares = lax.psum((shares[0], shares[1], shares[2], shares[3], shares[4], shares[5]), "crop")
    return (
        loss_total,
        output.astype(jnp.bfloat16).reshape(pixels.shape),
        grad_inputs.reshape(pixels.shape),
        shares[0],
        shares[1],
        shares[2],
        shares[3],
        shares[4],
        shares[5],
        grad_b_red,
        grad_b_exp,
        norm_sums[0, 1],
        norm_sums[0, 0],
        norm_sums[1, 1],
        norm_sums[1, 0],
        norm_sums[2, 1],
        norm_sums[2, 0],
    )


def solution(mesh):
    return jax.shard_map(
        shards,
        mesh=mesh,
        in_specs=(
            P("crop", "img", None, None),
            P("img", None),
            P("img", None),
            P(),
            P(),
            P(),
            P(),
            P(),
            P(),
            P(),
            P(),
            P(),
            P(),
            P(),
            P(),
            P(),
            P(),
        ),
        out_specs=(
            P(),
            P("crop", "img", None, None),
            P("crop", "img", None, None),
            P("img"),
            P("img"),
            P("img"),
            P("img"),
            P("img"),
            P("img"),
            P(),
            P(),
            P(),
            P(),
            P(),
            P(),
            P(),
            P(),
        ),
        check_vma=False,
    )
```

profile of v0, /device:TPU:0, one launch (start us, length us, event | category | flops | bytes accessed | tf_op | source)
XLA Modules:
  0.0 2633.5 jit_solution(7908694971802427046)
XLA Ops:
  19.3 30.3 %psum.133 = f32[2,2016]{1,0:T(2,128)S(1)} all-reduce(f32[2,2016]{1,0:T(2,128)S(1)} %pad_maximum_fusion.1), channel_id=1, replica_groups=mesh['crop'=4,'img'=8] {'img'}, use_global_device_ids=true, to_apply=%region_2.3 | all-reduce | flops 4032 | bytes 32256 | tf_op jit(solution)/shard_map/psum | solution.py:130
  59.1 211.3 %conditional.2 = (f32[784,2016]{1,0:T(8,128)}) conditional(s32[]{:T(128)} %convert_element_type.47, (bf16[784,2016]{1,0:T(8,128)(2,1)}, bf16[9,36,56,56]{3,2,1,0:T(8,128)(2,1)}) %tuple.22, (bf16[784,2016]{1,0:T(8,128)(2,1)}, bf16[9,36,56,56]{3,2,1,0:T(8,128)(2,1)}) %tuple.22), branch_computations={%region_3.4_spmd, %region_4.5_spmd} | conditional | flops 1605832704 | bytes 254722080 | solution.py:163
  123.1 22.8 fusion.41
  191.7 49.0 %bitcast_add_fusion.5 = f32[4,14,14,36,56]{4,2,1,0,3:T(8,128)} fusion(f32[36,4,14,14,56]{4,3,2,1,0:T(8,128)} %fusion.35, f32[36,4,14,14,56]{4,3,2,1,0:T(8,128)} %fusion.37, f32[36,4,14,14,56]{4,3,2,1,0:T(8,128)} %fusion.39, f32[36,4,14,14,56]{4,3,2,1,0:T(8,128)} %fusion.41, f32[36,56,4,14,14]{1,4,3,2,0:T(8,128)} %fusion.62, ...), kind=kOutput, calls=%fused_computation.40 | convolution fusion | flops 189665280 | bytes 60576768 | tf_op jit(solution)/shard_map/cond/branch_1_fun/nhwgc,gcd->nhwgd/dot_general | solution.py:47
  240.7 16.6 copy.120
  274.2 25.9 psum.134
  327.9 26.1 psum.135
  374.6 25.9 psum.136
  400.8 25.9 psum.137
  427.0 25.9 psum.138
  478.7 26.1 psum.140
  515.4 26.4 %reshape.205 = f32[6048000]{0:T(1024)} reshape(f32[2016,3000]{1,0:T(8,128)} %fusion.405) | data formatting | bytes 48384000 | tf_op jit(solution)/shard_map/reshape | solution.py:264
  559.7 13.9 fusion.426
  591.7 26.1 psum.141
  632.5 327.0 %conditional.3 = (f32[784,2016]{1,0:T(8,128)}, f32[9,36,56,56]{3,2,1,0:T(8,128)}) conditional(s32[]{:T(128)} %convert_element_type.47, (bf16[784,2016]{1,0:T(8,128)(2,1)}, bf16[9,36,56,56]{3,2,1,0:T(8,128)(2,1)}, bf16[784,2016]{1,0:T(8,128)(2,1)}) %tuple.23, (bf16[784,2016]{1,0:T(8,128)(2,1)}, bf16[9,36,56,56]{3,2,1,0:T(8,128)(2,1)}, ...), branch_computations={%region_35.36_spmd, %region_36.37_spmd} | conditional | flops 3199021056 | bytes 463998976 | solution.py:237
  753.5 49.7 %bitcast_add_fusion.15 = f32[4,14,14,36,56]{4,2,1,0,3:T(8,128)} fusion(f32[36,4,14,14,56]{4,3,2,1,0:T(8,128)} %fusion.173, f32[36,4,14,14,56]{4,3,2,1,0:T(8,128)} %fusion.175, f32[36,4,14,14,56]{4,3,2,1,0:T(8,128)} %fusion.177, f32[36,4,14,14,56]{4,3,2,1,0:T(8,128)} %fusion.179, f32[36,56,4,14,14]{1,4,3,2,0:T(8,128)} %fusion.306, ...), kind=kOutput, calls=%fused_computation.173 | convolution fusion | flops 189665280 | bytes 147216384 | tf_op jit(solution)/shard_map/cond/branch_1_fun/nhwgd,gcd->nhwgc/dot_general | solution.py:76
  803.2 16.7 copy.137
  967.8 25.9 psum.142
  1011.6 19.0 reshape.204
  1061.2 17.6 copy.149
  1078.8 19.3 reshape.200
  1101.3 1316.3 %all-reduce.19.cloned.1.call-done = (f32[4064256]{0:T(1024)}, f32[1016064]{0:T(1024)}, f32[1016064]{0:T(1024)}, f32[1016064]{0:T(1024)}, f32[4064256]{0:T(1024)}, /*index=5*/f32[6048000]{0:T(1024)}) async-done(((f32[4064256]{0:T(1024)}, f32[1016064]{0:T(1024)}, f32[1016064]{0:T(1024)}, f32[1016064]{0:T(1024)}, f32[4064256]{0:T(1024)}, /*index=5*/f32[6048000]{0:T(1024)}), (f32[4064256]{0:T(1024)}, ...) | async-done | bytes 68898832
  2435.7 41.2 %all-reduce.13 = (f32[]{:T(128)}, f32[504]{0:T(512)}, f32[2016]{0:T(1024)}, f32[3,2,2016]{2,1,0:T(2,128)S(1)}) all-reduce(f32[]{:T(128)S(6)} %div.192, f32[504]{0:T(512)S(1)} %copy-done.33, f32[2016]{0:T(1024)S(1)} %copy-done.34, f32[3,2,2016]{2,1,0:T(2,128)S(1)} %pad_maximum_fusion), channel_id=1, replica_groups=mesh['crop'=4,'img'=8] {'crop','img'}, use_global_device_ids=true, to_apply=%region_26.27 | all-reduce | flops 14617 | bytes 116936 | tf_op jit(solution)/shard_map/psum | solution.py:250
  2491.2 123.0 %all-reduce.21.cloned.1.call-done = (f32[508032]{0:T(1024)}, f32[127008]{0:T(1024)}, f32[127008]{0:T(1024)}, f32[127008]{0:T(1024)}, f32[508032]{0:T(1024)}, /*index=5*/f32[756000]{0:T(1024)}) async-done(((f32[508032]{0:T(1024)}, f32[127008]{0:T(1024)}, f32[127008]{0:T(1024)}, f32[127008]{0:T(1024)}, f32[508032]{0:T(1024)}, /*index=5*/f32[756000]{0:T(1024)}), (f32[508032]{0:T(1024)}, f32[127008]{0:T(1024)}, ...) | async-done | bytes 8612368 | tf_op jit(solution)/shard_map/psum | solution.py:273
  (237 shorter events, 622.1 us)
Async XLA Ops:
  7.2 304.1 %copy-start = (bf16[504,2016]{1,0:T(8,128)(2,1)S(1)}, bf16[504,2016]{1,0:T(8,128)(2,1)}, u32[]{:S(2)}) copy-start(bf16[504,2016]{1,0:T(8,128)(2,1)} %param.28) | copy-start | bytes 6096388
  7.2 46.7 %copy-start.26 = (f32[2016]{0:T(1024)S(1)}, f32[2016]{0:T(1024)}, u32[]{:S(2)}) copy-start(f32[2016]{0:T(1024)} %param.32) | copy-start | bytes 24196
  7.2 46.7 %copy-start.20 = (f32[2016]{0:T(1024)S(1)}, f32[2016]{0:T(1024)}, u32[]{:S(2)}) copy-start(f32[2016]{0:T(1024)} %param.31) | copy-start | bytes 24196
  7.2 2410.3 %all-reduce.19.cloned.1.call-start = ((), (), s32[]{:S(2)}) async-start(), calls=%async_computation | async-start | bytes 137822208
  49.5 3.7 collective-permute-start
  59.1 242.5 %copy-start.37 = (s32[1,32]{1,0:T(1,128)S(1)}, s32[1,32]{1,0:T(1,128)}, u32[]{:S(2)}) copy-start(s32[1,32]{1,0:T(1,128)} %param.23) | copy-start | bytes 388
  59.1 244.8 %copy-start.29 = (s32[784]{0:T(1024)S(1)}, s32[784]{0:T(1024)}, u32[]{:S(2)}) copy-start(s32[784]{0:T(1024)} %fusion.396) | copy-start | bytes 9412
  59.1 244.8 %copy-start.32 = (f32[2016]{0:T(1024)S(1)}, f32[2016]{0:T(1024)}, u32[]{:S(2)}) copy-start(f32[2016]{0:T(1024)} %param.33) | copy-start | bytes 24196
  300.1 3.7 collective-permute-start.1
  311.3 267.3 %copy-start.11 = (f32[16,504]{1,0:T(8,128)}, f32[16,504]{1,0:T(8,128)S(1)}, u32[]{:S(2)}) copy-start(f32[16,504]{1,0:T(8,128)S(1)} %convolution_add_fusion.1) | copy-start | bytes 96772
  319.0 36.5 %copy-start.16 = (f32[1,2016]{1,0:T(1,128)S(1)}, f32[1,2016]{1,0:T(1,128)}, u32[]{:S(2)}) copy-start(f32[1,2016]{1,0:T(1,128)} %copy-done.15) | copy-start | bytes 24196
  319.0 36.5 %copy-start.21 = (f32[2016]{0:T(1024)S(1)}, f32[2016]{0:T(1024)}, u32[]{:S(2)}) copy-start(f32[2016]{0:T(1024)} %param.31) | copy-start | bytes 24196
  319.1 38.7 %copy-start.28 = (f32[2016]{0:T(1024)S(1)}, f32[2016]{0:T(1024)}, u32[]{:S(2)}) copy-start(f32[2016]{0:T(1024)} %param.35) | copy-start | bytes 24196
  319.1 38.7 %copy-start.31 = (f32[2016]{0:T(1024)S(1)}, f32[2016]{0:T(1024)}, u32[]{:S(2)}) copy-start(f32[2016]{0:T(1024)} %param.36) | copy-start | bytes 24196
  354.0 3.7 collective-permute-start.2
  504.8 37.0 %collective-permute-start.3 = (f32[2,2016]{1,0:T(2,128)S(1)}, f32[2,2016]{1,0:T(2,128)S(1)}, u32[]{:S(2)}, u32[]{:S(2)}) collective-permute-start(f32[2,2016]{1,0:T(2,128)S(1)} %psum.140), channel_id=1, source_target_pairs={{0,8},{8,0},{16,24},{24,16},{1,9},{9,1},{17,25},{25,17},{2,10},{10... | collective-permute-start | bytes 48392 | tf_op jit(solution)/shard_map/ppermute | solution.py:21
  617.8 6.5 collective-permute-start.4
  632.5 327.1 %copy-start.17 = (f32[1,2016]{1,0:T(1,128)S(1)}, f32[1,2016]{1,0:T(1,128)}, u32[]{:S(2)}) copy-start(f32[1,2016]{1,0:T(1,128)} %copy-done.15) | copy-start | bytes 24196
  632.5 327.1 %copy-start.19 = (f32[1,2016]{1,0:T(1,128)S(1)}, f32[1,2016]{1,0:T(1,128)}, u32[]{:S(2)}) copy-start(f32[1,2016]{1,0:T(1,128)} %copy-done.18) | copy-start | bytes 24196
  632.5 327.1 %copy-start.22 = (f32[2016]{0:T(1024)S(1)}, f32[2016]{0:T(1024)}, u32[]{:S(2)}) copy-start(f32[2016]{0:T(1024)} %param.31) | copy-start | bytes 24196
  632.5 327.1 %copy-start.27 = (f32[2016]{0:T(1024)S(1)}, f32[2016]{0:T(1024)}, u32[]{:S(2)}) copy-start(f32[2016]{0:T(1024)} %param.32) | copy-start | bytes 24196
  959.6 34.6 %copy-start.12 = (f32[16,504]{1,0:T(8,128)S(1)}, f32[16,504]{1,0:T(8,128)}, u32[]{:S(2)}) copy-start(f32[16,504]{1,0:T(8,128)} %copy-done.11) | copy-start | bytes 96772
  993.7 47.6 %collective-permute-start.5 = (f32[2,2016]{1,0:T(2,128)S(1)}, f32[2,2016]{1,0:T(2,128)S(1)}, u32[]{:S(2)}, u32[]{:S(2)}) collective-permute-start(f32[2,2016]{1,0:T(2,128)S(1)} %psum.142), channel_id=1, source_target_pairs={{0,8},{8,0},{16,24},{24,16},{1,9},{9,1},{17,25},{25,17},{2,10},{10... | collective-permute-start | bytes 48392 | tf_op jit(solution)/shard_map/ppermute | solution.py:21
  1098.1 1516.1 %all-reduce.21.cloned.1.call-start = ((), (), s32[]{:S(2)}) async-start(), calls=%async_computation.1 | async-start | bytes 17268736 | tf_op jit(solution)/shard_map/psum | solution.py:273
  (34 other events, 372.1 us)
Sparse Core Ops, SparseCore 0:
  1098.2 1319.2 all-reduce.18
  2435.1 179.0 all-reduce.20
where the time goes:
time: 2640 us; the launch traced here: 2630 us
  waiting for transfers between devices  1440 us (55%)
  matrix products  544 us (21%)
  blocking collectives  288 us (11%)
  local copies, waits for them, and re-layouts  259 us (10%)
  other arithmetic  49.5 us (2%)
    unnamed x3, waiting for transfers between devices  1320 us
    dot_general x9, matrix products, conv_forward(): jnp.einsum('nhwgc,gcd->nhwgd', window, kernel[offset_index], preferred_el...  152 us
    dot_general x9, matrix products, conv_backward(): jnp.einsum('nhwgd,gcd->nhwgc', back_window, kernel[offset_index], preferr...  141 us
    psum x1, waiting for transfers between devices, shards(): lax.psum((shares[0], shares[1], shares[2], shares[3], shares[4], shares[5...  123 us
    dot_general x9, matrix products, conv_backward(): jnp.einsum('nhwgc,nhwgd->gcd', window, grad_view, preferred_element_type=...  102 us
    psum x3, blocking collectives, normalize(): within = lax.psum(local_sums, 'img')  82.3 us
    psum x3, blocking collectives, norm_back(): within = lax.psum(local_sums, 'img')  78.1 us
    psum x3, blocking collectives, shards(): plan_rows = plan_rows / lax.psum(jnp.sum(plan_rows, axis=0), 'img')  77.7 us
  transfers between devices with their start and end apart: 8, of which 5 were waited for; matrix products, arithmetic and copies ran while one was open for 4% of the time, Pallas kernels for 0%

commit v1 on v0

v1 whole, which is shorter than its diff:
```python
import functools
import jax
import jax.numpy as jnp
from jax import lax
from jax.experimental import pallas as pl
from jax.experimental.pallas import tpu as pltpu

VMEM_LIMIT = 56 * 1024 * 1024
PACK = 4


def window_of(block, width):
    start = block * width
    base = jnp.minimum(start // 128, 13) * 128
    return pl.multiple_of(base, 128), start - base


def take_window(ref, block, width, cast=None):
    base, offset = window_of(block, width)
    value = ref[:, pl.ds(base, 384)]
    if value.dtype != jnp.float32:
        value = value.astype(jnp.float32)
    moved = pltpu.roll(value, jnp.where(offset == 0, 0, 384 - offset), 1)[:, :256]
    lanes = lax.broadcasted_iota(jnp.int32, moved.shape, 1)
    return jnp.where(lanes < width, moved, 0.0)


def put_window(ref, block, width, value):
    base, offset = window_of(block, width)
    wide = jnp.concatenate([value, jnp.zeros((value.shape[0], 128), jnp.float32)], axis=1)
    moved = pltpu.roll(wide, offset, 1)
    lanes = lax.broadcasted_iota(jnp.int32, moved.shape, 1)
    old = ref[:, pl.ds(base, 384)]
    ref[:, pl.ds(base, 384)] = jnp.where(lanes >= offset, moved.astype(ref.dtype), old)


def shift_rows(value, step):
    rows = value.shape[0]
    return pltpu.roll(value, (-step) % rows, 0)


def bn_act(h, p_ref, block, width):
    par = take_window(p_ref, block, width)
    return h * par[0:1] + par[1:2], par


def stack_cols(act, mask_ref, dest):
    dest[:, 0:256] = (shift_rows(act, -1) * mask_ref[0]).astype(jnp.bfloat16)
    dest[:, 256:512] = act.astype(jnp.bfloat16)
    dest[:, 512:768] = (shift_rows(act, 1) * mask_ref[1]).astype(jnp.bfloat16)


def stack_rows(grad, mask_ref, dest, side):
    dest[:, 0:256] = (shift_rows(grad, side) * mask_ref[3]).astype(jnp.bfloat16)
    dest[:, 256:512] = grad.astype(jnp.bfloat16)
    dest[:, 512:768] = (shift_rows(grad, -side) * mask_ref[2]).astype(jnp.bfloat16)


def fwd_kernel(width, sides, glob_ref, h_ref, p_ref, mask_ref, k_ref, out_ref, st_ref, stack):
    block = pl.program_id(0)
    h = take_window(h_ref, block, width)
    pre, _ = bn_act(h, p_ref, block, width)
    act = pre * jax.nn.sigmoid(pre)
    stack_cols(act.astype(jnp.bfloat16).astype(jnp.float32), mask_ref, stack)
    y = jnp.dot(stack[...], k_ref[0], preferred_element_type=jnp.float32)

    def finish(side):
        total = (
            y[:, 256:512]
            + shift_rows(y[:, 0:256], -side) * mask_ref[2]
            + shift_rows(y[:, 512:768], side) * mask_ref[3]
        )
        put_window(out_ref, block, width, total)
        sums = jnp.concatenate(
            [
                jnp.sum(total, axis=0, keepdims=True),
                jnp.sum(total * total, axis=0, keepdims=True),
                jnp.zeros((6, 256), jnp.float32),
            ],
            axis=0,
        )
        put_window(st_ref, block, width, sums)

    @pl.when(glob_ref[0] == 1)
    def _():
        finish(sides[0])

    @pl.when(glob_ref[0] == 0)
    def _():
        finish(sides[1])


def dgrad_kernel(width, sides, glob_ref, g_ref, h_ref, p_ref, mask_ref, k_ref, out_ref, st_ref, stack):
    block = pl.program_id(0)
    grad = take_window(g_ref, block, width)

    @pl.when(glob_ref[0] == 1)
    def _():
        stack_rows(grad, mask_ref, stack, sides[0])

    @pl.when(glob_ref[0] == 0)
    def _():
        stack_rows(grad, mask_ref, stack, sides[1])

    z = lax.dot_general(
        stack[...], k_ref[0], (((1,), (1,)), ((), ())), preferred_element_type=jnp.float32
    )
    total = (
        z[:, 256:512]
        + shift_rows(z[:, 0:256], 1) * mask_ref[1]
        + shift_rows(z[:, 512:768], -1) * mask_ref[0]
    )
    h = take_window(h_ref, block, width)
    pre, par = bn_act(h, p_ref, block, width)
    sig = jax.nn.sigmoid(pre)
    ga = total * (sig * (1.0 + pre * (1.0 - sig)))
    xhat = h * par[2:3] + par[3:4]
    put_window(out_ref, block, width, ga)
    sums = jnp.concatenate(
        [
            jnp.sum(ga, axis=0, keepdims=True),
            jnp.sum(ga * xhat, axis=0, keepdims=True),
            jnp.zeros((6, 256), jnp.float32),
        ],
        axis=0,
    )
    put_window(st_ref, block, width, sums)


def wgrad_kernel(width, sides, glob_ref, g_ref, h_ref, p_ref, mask_ref, out_ref, cols, rows):
    block = pl.program_id(0)
    h = take_window(h_ref, block, width)
    pre, _ = bn_act(h, p_ref, block, width)
    stack_cols((pre * jax.nn.sigmoid(pre)).astype(jnp.bfloat16).astype(jnp.float32), mask_ref, cols)
    grad = take_window(g_ref, block, width)

    @pl.when(glob_ref[0] == 1)
    def _():
        stack_rows(grad, mask_ref, rows, sides[0])

    @pl.when(glob_ref[0] == 0)
    def _():
        stack_rows(grad, mask_ref, rows, sides[1])

    gw = width // PACK
    for dx in range(3):
        acc = lax.dot_general(
            cols[:, 256 * dx : 256 * dx + 256],
            rows[...],
            (((0,), (0,)), ((), ())),
            preferred_element_type=jnp.float32,
        )
        lanes = lax.broadcasted_iota(jnp.int32, (gw, 256), 1)
        for dy in range(3):
            small = jnp.zeros((gw, 256), jnp.float32)
            for g in range(PACK):
                piece = acc[gw * g : gw * g + gw, 256 * dy : 256 * dy + 256]
                small = jnp.where((lanes >= gw * g) & (lanes < gw * g + gw), piece, small)
            out_ref[3 * dy + dx, 0] = small


def pack_kernel(gw, kc_ref, out_ref):
    lanes = lax.broadcasted_iota(jnp.int32, (gw, 256), 1)
    for dy in range(3):
        for dx in range(3):
            small = kc_ref[3 * dy + dx, 0].astype(jnp.float32)
            parts = [
                jnp.where((lanes >= gw * g) & (lanes < gw * g + gw), small, 0.0)
                for g in range(PACK)
            ]
            parts.append(jnp.zeros((256 - PACK * gw, 256), jnp.float32))
            out_ref[0, 256 * dx : 256 * dx + 256, 256 * dy : 256 * dy + 256] = jnp.concatenate(
                parts, axis=0
            ).astype(jnp.bfloat16)


def params():
    return pltpu.CompilerParams(vmem_limit_bytes=VMEM_LIMIT)


def pack_blocks(kernel):
    taps, groups, gw, _ = kernel.shape
    blocks = groups // PACK
    kc = kernel.reshape(taps, blocks, PACK, gw, gw).transpose(0, 1, 3, 2, 4).reshape(taps, blocks, gw, PACK * gw)
    kc = jnp.pad(kc, ((0, 0), (0, 0), (0, 0), (0, 256 - PACK * gw)))
    return pl.pallas_call(
        functools.partial(pack_kernel, gw),
        grid=(blocks,),
        in_specs=[pl.BlockSpec((taps, 1, gw, 256), lambda b: (0, b, 0, 0))],
        out_specs=pl.BlockSpec((1, 768, 768), lambda b: (b, 0, 0)),
        out_shape=jax.ShapeDtypeStruct((blocks, 768, 768), jnp.bfloat16),
        compiler_params=params(),
        name="pack",
    )(kc)


def conv_specs(rows):
    whole = lambda r: pl.BlockSpec((r, 2048), lambda b, s: (0, 0))
    mask = pl.BlockSpec((4, rows, 256), lambda b, s: (0, 0, 0))
    kern = pl.BlockSpec((1, 768, 768), lambda b, s: (b, 0, 0))
    return whole, mask, kern


def conv_fwd(glob, h, par, masks, packed, width, sides):
    rows, chans = h.shape
    whole, mask, kern = conv_specs(rows)
    return pl.pallas_call(
        functools.partial(fwd_kernel, width, sides),
        grid_spec=pltpu.PrefetchScalarGridSpec(
            num_scalar_prefetch=1,
            grid=(packed.shape[0],),
            in_specs=[whole(rows), whole(8), mask, kern],
            out_specs=[whole(rows), whole(8)],
            scratch_shapes=[pltpu.VMEM((rows, 768), jnp.bfloat16)],
        ),
        out_shape=[
            jax.ShapeDtypeStruct((rows, chans), jnp.float32),
            jax.ShapeDtypeStruct((8, chans), jnp.float32),
        ],
        compiler_params=params(),
        name="conv_fwd",
    )(glob, h, par, masks, packed)


def conv_dgrad(glob, grad, h, par, masks, packed, width, sides):
    rows, chans = h.shape
    whole, mask, kern = conv_specs(rows)
    return pl.pallas_call(
        functools.partial(dgrad_kernel, width, sides),
        grid_spec=pltpu.PrefetchScalarGridSpec(
            num_scalar_prefetch=1,
            grid=(packed.shape[0],),
            in_specs=[whole(rows), whole(rows), whole(8), mask, kern],
            out_specs=[whole(rows), whole(8)],
            scratch_shapes=[pltpu.VMEM((rows, 768), jnp.bfloat16)],
        ),
        out_shape=[
            jax.ShapeDtypeStruct((rows, chans), jnp.float32),
            jax.ShapeDtypeStruct((8, chans), jnp.float32),
        ],
        compiler_params=params(),
        name="conv_dgrad",
    )(glob, grad, h, par, masks, packed)


def conv_wgrad(glob, grad, h, par, masks, blocks, width, sides):
    rows, chans = h.shape
    whole, mask, kern = conv_specs(rows)
    gw = width // PACK
    return pl.pallas_call(
        functools.partial(wgrad_kernel, width, sides),
        grid_spec=pltpu.PrefetchScalarGridSpec(
            num_scalar_prefetch=1,
            grid=(blocks,),
            in_specs=[whole(rows), whole(rows), whole(8), mask],
            out_specs=pl.BlockSpec((9, 1, gw, 256), lambda b, s: (0, b, 0, 0)),
            scratch_shapes=[pltpu.VMEM((rows, 768), jnp.bfloat16)] * 2,
        ),
        out_shape=jax.ShapeDtypeStruct((9, blocks, gw, 256), jnp.float32),
        compiler_params=params(),
        name="conv_wgrad",
    )(glob, grad, h, par, masks)


from jax.sharding import PartitionSpec as P

IMG_DEV = 4
SIDE = 14
SMALL_SIDE = 7

norm_epsilon = 1e-05
length_epsilon = 1e-06
sharpening_divisor = 0.1
sharpness = 0.05
exact_mode = lax.Precision.HIGHEST


def swap(value, axis, mask):
    pairs = [(source, source ^ mask) for source in range(lax.axis_size(axis))]
    return lax.ppermute(value, axis, pairs)


def smooth_gate(values):
    return values * jax.nn.sigmoid(values)


def smooth_slope(values):
    sigma_values = jax.nn.sigmoid(values)
    return sigma_values * (1.0 + values * (1.0 - sigma_values))


def exact_dot(left, right):
    return jnp.dot(left, right, precision=exact_mode, preferred_element_type=jnp.float32)


def bits_of(size):
    return [1 << bit for bit in range(size.bit_length() - 1)]


def img_sum(value):
    for mask in bits_of(lax.axis_size("img")):
        value = value + swap(value, "img", mask)
    return value


def stream_sum(value):
    value = value + swap(value, "crop", 1)
    return img_sum(value)


def pick(value, index, axis):
    return lax.dynamic_index_in_dim(value, index, axis, keepdims=False)


def slab_rows(width, devices):
    return -(-(width // devices) // 8) * 8


def slab_offset(index, width, devices):
    share = width // devices
    return 2 * share * (index // 2) + (index % 2) * (2 * share - slab_rows(width, devices))


def slab_kernel(core_ref, left_ref, right_ref, out_ref):
    out_ref[0] = lax.dot_general(
        left_ref[0], right_ref[...], (((0,), (0,)), ((), ())), preferred_element_type=jnp.float32
    )


def slab_product(core, left, right):
    slabs, rows, height = left.shape
    wide = right.shape[1]
    return pl.pallas_call(
        slab_kernel,
        grid_spec=pltpu.PrefetchScalarGridSpec(
            num_scalar_prefetch=1,
            grid=(slabs // 2,),
            in_specs=[
                pl.BlockSpec((1, rows, height), lambda z, c: (2 * z + c[0], 0, 0)),
                pl.BlockSpec((rows, wide), lambda z, c: (0, 0)),
            ],
            out_specs=pl.BlockSpec((1, height, wide), lambda z, c: (z, 0, 0)),
        ),
        out_shape=jax.ShapeDtypeStruct((slabs // 2, height, wide), jnp.float32),
        compiler_params=pltpu.CompilerParams(vmem_limit_bytes=32 * 1024 * 1024),
        name="slab_product",
    )(core, left, right)


def share_kernel(left_ref, right_ref, out_ref):
    out_ref[...] = lax.dot_general(
        left_ref[...].astype(jnp.bfloat16),
        right_ref[...].astype(jnp.bfloat16),
        (((0,), (0,)), ((), ())),
        preferred_element_type=jnp.float32,
    )


def share_product(left, right):
    return pl.pallas_call(
        share_kernel,
        out_shape=jax.ShapeDtypeStruct((left.shape[1], right.shape[1]), jnp.float32),
        compiler_params=pltpu.CompilerParams(vmem_limit_bytes=32 * 1024 * 1024),
        name="share_product",
    )(left, right)


def make_slabs(value, devices):
    width = value.shape[1]
    height = slab_rows(width, devices)
    return jnp.stack(
        [
            lax.slice_in_dim(value, start, start + height, axis=1)
            for start in (slab_offset(i, width, devices) for i in range(devices))
        ]
    )


def crop_scatter(value):
    lead, rows, cols = value.shape
    crop = lax.axis_index("crop")
    bits = (crop & 1, crop >> 1)
    whole = value.reshape(lead, 2, 2, 2, rows // 8, cols)
    parts = []
    for half, order in ((0, (0, 1)), (1, (1, 0))):
        part = whole[:, half]
        for axis in order:
            part = pick(part, bits[axis], 1) + swap(pick(part, 1 - bits[axis], 1), "crop", 1 << axis)
        parts.append(part)
    return parts


def crop_gather(parts):
    crop = lax.axis_index("crop")
    bits = (crop & 1, crop >> 1)
    halves = []
    for part, order in zip(parts, ((1, 0), (0, 1))):
        for axis in order:
            other = swap(part, "crop", 1 << axis)
            upper = bits[axis] == 1
            part = jnp.stack(
                [jnp.where(upper, other, part), jnp.where(upper, part, other)], axis=1
            ) if part.ndim == 3 else jnp.stack(
                [jnp.where(upper, other, part), jnp.where(upper, part, other)], axis=1
            )
        halves.append(part)
    both = jnp.stack(halves, axis=1)
    lead, cols = both.shape[0], both.shape[-1]
    return both.reshape(lead, -1, cols)


def chip_scatter(value):
    chip = lax.axis_index("img") // 2
    for mask in bits_of(value.shape[0]):
        bit = (chip // mask) % 2
        value = value.reshape((value.shape[0] // 2, 2) + value.shape[1:])
        value = pick(value, bit, 1) + swap(pick(value, 1 - bit, 1), "img", 2 * mask)
    return value[0]


def shards(
    pixels,
    counts,
    slot_order,
    w_in,
    kernel,
    w_red,
    b_red,
    w_exp,
    b_exp,
    w_out,
    gain_one,
    shift_one,
    gain_two,
    shift_two,
    gain_three,
    shift_three,
    protos,
):
    row_count = pixels.shape[2]
    width = pixels.shape[3]
    proto_count = protos.shape[1]
    squeeze = w_red.shape[1]
    seg_count = row_count // (SMALL_SIDE * SMALL_SIDE)
    slot_total = slot_order.shape[1]
    devices = lax.axis_size("img")
    img_index = lax.axis_index("img")
    crop_index = lax.axis_index("crop")
    core = img_index % 2
    fast = width % devices == 0 and (2 * width // devices) % 8 == 0
    is_global = crop_index < 2
    glob = is_global.astype(jnp.int32).reshape(1)
    stream_rows = 2.0 * devices * row_count
    couple_number = 2.0 * devices * (IMG_DEV + slot_total)
    inputs = pixels.reshape(row_count, width)
    row_ids = jnp.arange(row_count, dtype=jnp.int32)
    side = jnp.where(is_global, SIDE, SMALL_SIDE)
    seg_of_row = row_ids // (side * side)
    across = row_ids % side
    down = (row_ids // side) % side
    masks = jnp.stack([across > 0, across < side - 1, down > 0, down < side - 1])
    masks = jnp.broadcast_to(masks.astype(jnp.float32)[:, :, None], (4, row_count, 256))
    member = (seg_of_row[None, :] == jnp.arange(seg_count, dtype=jnp.int32)[:, None]).astype(
        jnp.float32
    )
    member_rows = member.T
    crop_pixels = jnp.where(is_global, float(SIDE * SIDE), float(SMALL_SIDE * SMALL_SIDE))
    block_width = PACK * kernel.shape[2]
    block_count = kernel.shape[1] // PACK
    sides = (SIDE, SMALL_SIDE)

    def norm_rows(local_sums, gain, shift):
        sums = stream_sum(local_sums)
        average = sums[0] / stream_rows
        inv = lax.rsqrt(sums[1] / stream_rows - average * average + norm_epsilon)
        return average, inv

    def back_rows(local_sums, gain, inv):
        sums = stream_sum(local_sums)
        return sums, gain * inv, sums[0] / stream_rows, sums[1] / stream_rows

    hidden_one = jnp.dot(inputs, w_in, preferred_element_type=jnp.float32)
    sums = jnp.stack([jnp.sum(hidden_one, axis=0), jnp.sum(hidden_one * hidden_one, axis=0)])
    mean_one, inv_one = norm_rows(sums, gain_one, shift_one)
    packed = pack_blocks(kernel)
    zero_row = jnp.zeros((width,), jnp.float32)
    scale_one = gain_one * inv_one
    par = jnp.stack(
        [scale_one, shift_one - mean_one * scale_one, inv_one, -mean_one * inv_one] + [zero_row] * 4
    )
    hidden_two, sums = conv_fwd(glob, hidden_one, par, masks, packed, block_width, sides)
    mean_two, inv_two = norm_rows(sums[:2], gain_two, shift_two)
    centred_two = (hidden_two - mean_two) * inv_two
    pre_two = centred_two * gain_two + shift_two
    act_two = smooth_gate(pre_two)
    red_float = w_red.astype(jnp.float32)
    exp_float = w_exp.astype(jnp.float32)
    pooled = exact_dot(member, act_two) / crop_pixels
    reduce_pre = exact_dot(pooled, red_float) + b_red
    reduced = smooth_gate(reduce_pre)
    gate_values = jax.nn.sigmoid(exact_dot(reduced, exp_float) + b_exp)
    gate_rows = exact_dot(member_rows, gate_values)
    excited = (act_two * gate_rows).astype(jnp.bfloat16)
    hidden_three = jnp.dot(excited, w_out, preferred_element_type=jnp.float32)
    sums = jnp.stack([jnp.sum(hidden_three, axis=0), jnp.sum(hidden_three * hidden_three, axis=0)])
    mean_three, inv_three = norm_rows(sums, gain_three, shift_three)
    centred_three = (hidden_three - mean_three) * inv_three
    summed_in = inputs.astype(jnp.float32) + centred_three * gain_three + shift_three
    output = smooth_gate(summed_in)
    pooled_out = exact_dot(member, output) / crop_pixels
    length_inv = lax.rsqrt(jnp.sum(pooled_out * pooled_out, axis=1, keepdims=True) + length_epsilon)
    unit_wide = pooled_out * length_inv
    unit_rows = unit_wide.astype(jnp.bfloat16)
    match_matrix = jnp.dot(unit_rows, protos, preferred_element_type=jnp.float32)

    every = match_matrix[:IMG_DEV]
    for mask in bits_of(devices):
        every = jnp.concatenate([every, swap(every, "img", mask)], axis=0)
    plan_rows = jnp.exp(every / sharpness)
    for sweep_index in range(3):
        plan_rows = plan_rows / jnp.sum(plan_rows, axis=0, keepdims=True)
        plan_rows = plan_rows / jnp.sum(plan_rows, axis=1, keepdims=True)
    codes = plan_rows[:IMG_DEV]
    partner = lax.ppermute(codes, "crop", [(0, 1), (1, 0)])
    both_codes = lax.ppermute(codes, "crop", [(0, 2), (1, 3)]) + lax.ppermute(
        codes, "crop", [(0, 3), (1, 2)]
    )
    wide_target = jnp.concatenate(
        [partner, jnp.zeros((seg_count - IMG_DEV, proto_count), jnp.float32)], axis=0
    )
    ends = [jnp.sum(counts[0, : i + 1]) for i in range(IMG_DEV)]
    first_slot = jnp.maximum(crop_index - 2, 0) * seg_count
    order_here = lax.dynamic_slice_in_dim(slot_order[0], first_slot, seg_count)
    owner = sum((order_here >= end).astype(jnp.int32) for end in ends)
    narrow_target = jnp.zeros((seg_count, proto_count), jnp.float32)
    for i in range(IMG_DEV):
        narrow_target = jnp.where(owner[:, None] == i, both_codes[i : i + 1], narrow_target)
    target = jnp.where(is_global, wide_target, narrow_target)
    sharpened = match_matrix / sharpening_divisor
    shifted = sharpened - jnp.max(sharpened, axis=1, keepdims=True)
    log_probs = shifted - jnp.log(jnp.sum(jnp.exp(shifted), axis=1, keepdims=True))
    loss_here = -jnp.sum(target * log_probs) / couple_number
    scores_wide = (jnp.exp(log_probs) * jnp.sum(target, axis=1, keepdims=True) - target) / (
        sharpening_divisor * couple_number
    )
    grad_scores = scores_wide.astype(jnp.bfloat16)

    grad_unit = jnp.einsum("sk,wk->sw", grad_scores, protos, preferred_element_type=jnp.float32)
    inner_term = jnp.sum(pooled_out * grad_unit, axis=1, keepdims=True)
    grad_pooled_out = (
        length_inv * grad_unit - pooled_out * length_inv * length_inv * length_inv * inner_term
    )
    grad_output = exact_dot(member_rows, grad_pooled_out / crop_pixels)
    grad_summed = grad_output * smooth_slope(summed_in)
    sums_three, scale_three, first, second = back_rows(
        jnp.stack([jnp.sum(grad_summed, axis=0), jnp.sum(grad_summed * centred_three, axis=0)]),
        gain_three,
        inv_three,
    )
    grad_three_low = (scale_three * (grad_summed - first - centred_three * second)).astype(
        jnp.bfloat16
    )
    grad_excited = jnp.einsum(
        "rv,wv->rw", grad_three_low, w_out, preferred_element_type=jnp.float32
    )
    grad_gate = exact_dot(member, grad_excited * act_two)
    grad_gate_pre = grad_gate * gate_values * (1.0 - gate_values)
    grad_reduce_pre = exact_dot(grad_gate_pre, exp_float.T) * smooth_slope(reduce_pre)
    grad_pooled = exact_dot(grad_reduce_pre, red_float.T)
    grad_act_two = grad_excited * gate_rows + exact_dot(member_rows, grad_pooled / crop_pixels)
    grad_pre_two = grad_act_two * smooth_slope(pre_two)
    bias_row = jnp.concatenate(
        [
            jnp.sum(grad_reduce_pre, axis=0),
            loss_here.reshape(1),
            jnp.zeros((width - squeeze - 1,), jnp.float32),
        ]
    )
    sums_two, scale_two, first, second = back_rows(
        jnp.stack(
            [
                jnp.sum(grad_pre_two, axis=0),
                jnp.sum(grad_pre_two * centred_two, axis=0),
                jnp.sum(grad_gate_pre, axis=0),
                bias_row,
            ]
        ),
        gain_two,
        inv_two,
    )
    grad_two_low = (scale_two * (grad_pre_two - first - centred_two * second)).astype(jnp.bfloat16)
    grad_pre_one, sums = conv_dgrad(
        glob, grad_two_low, hidden_one, par, masks, packed, block_width, sides
    )
    sums_one, scale_one, first, second = back_rows(sums[:2], gain_one, inv_one)
    small_kernel = conv_wgrad(
        glob, grad_two_low, hidden_one, par, masks, block_count, block_width, sides
    )
    centred_one = (hidden_one - mean_one) * inv_one
    grad_one_low = (scale_one * (grad_pre_one - first - centred_one * second)).astype(jnp.bfloat16)
    grad_inputs = (
        jnp.einsum("rv,wv->rw", grad_one_low, w_in, preferred_element_type=jnp.float32)
        + grad_summed
    )

    last = jnp.concatenate([sums_one, sums_two, sums_three], axis=0)
    last = last + swap(last, "crop", 2)
    tail = (
        last[5, :squeeze],
        last[4],
        last[1],
        last[0],
        last[3],
        last[2],
        last[7],
        last[6],
    )
    loss_total = last[5, squeeze]

    if fast:
        share = width // devices
        near = core.reshape(1)
        far = (1 - core).reshape(1)

        def kept(value):
            skip = core * (value.shape[0] - share)
            return lax.dynamic_slice_in_dim(value, skip, share, axis=0)

        def my_columns(value):
            count = value.shape[1] // devices
            return lax.dynamic_slice_in_dim(value, img_index * count, count, axis=1)

        seen = lax.all_gather(
            jnp.concatenate([unit_wide, scores_wide], axis=1), "img", tiled=True
        )
        share_protos = share_product(my_columns(seen[:, :width]), seen[:, width:])
        seen = lax.all_gather(
            jnp.concatenate([pooled, reduced, grad_reduce_pre, grad_gate_pre], axis=1),
            "img",
            tiled=True,
        )
        share_red = exact_dot(
            my_columns(seen[:, :width]).T, seen[:, width + squeeze : width + 2 * squeeze]
        )
        share_exp = exact_dot(
            my_columns(seen[:, width : width + squeeze]).T, seen[:, width + 2 * squeeze :]
        )

        def pad_rows(value):
            rows = -(-value.shape[0] // 64) * 64
            return jnp.pad(value, ((0, rows - value.shape[0]), (0, 0)))

        slabs = make_slabs(excited, devices)
        own = slab_product(near, slabs, grad_three_low)
        own = own + swap(slab_product(far, slabs, grad_three_low), "img", 1)
        share_out = chip_scatter(own)
        pieces = [share_out, share_protos, share_red, share_exp]
        summed = [crop_gather(crop_scatter(pad_rows(piece)[None]))[0] for piece in pieces]
        flat_out = kept(summed[0][: share_out.shape[0]]).reshape(-1)
        flat_protos = summed[1][: share_protos.shape[0]].reshape(-1)
        flat_red = summed[2][: share_red.shape[0]].reshape(-1)
        flat_exp = summed[3][: share_exp.shape[0]].reshape(-1)

        slabs = make_slabs(inputs, devices)
        own = slab_product(near, slabs, grad_one_low)
        own = own + swap(slab_product(far, slabs, grad_one_low), "img", 1)
        parts = [chip_scatter(part)[None] for part in crop_scatter(own)]
        flat_in = kept(crop_gather(parts)[0]).reshape(-1)

        gw = kernel.shape[2]
        units = small_kernel.reshape(9 * block_count, gw, 256)
        total = kernel.size // devices
        unit_size = gw * gw * PACK
        span = -(-total // unit_size) + 1
        firsts = [min(total * i // unit_size, units.shape[0] - span) for i in range(devices)]
        slabs = jnp.stack([units[f : f + span] for f in firsts])
        mine = lax.psum_scatter(slabs, "img", scatter_dimension=0, tiled=False)
        mine = lax.psum(mine, "crop")
        mine = mine[:, :, : PACK * gw].reshape(span, gw, PACK, gw).transpose(0, 2, 1, 3).reshape(-1)
        skips = jnp.asarray([total * i - unit_size * f for i, f in enumerate(firsts)], jnp.int32)
        flat_kernel = lax.dynamic_slice_in_dim(mine, skips[img_index], total)
        shares = (flat_in, flat_kernel, flat_red, flat_exp, flat_out, flat_protos)
    else:
        gw = kernel.shape[2]
        grads = (
            jnp.einsum("rw,rv->wv", inputs, grad_one_low, preferred_element_type=jnp.float32),
            small_kernel[..., : PACK * gw]
            .reshape(9, block_count, gw, PACK, gw)
            .transpose(0, 1, 3, 2, 4),
            exact_dot(pooled.T, grad_reduce_pre),
            exact_dot(reduced.T, grad_gate_pre),
            jnp.einsum("rw,rv->wv", excited, grad_three_low, preferred_element_type=jnp.float32),
            jnp.einsum("sw,sk->wk", unit_rows, grad_scores, preferred_element_type=jnp.float32),
        )
        shares = tuple(
            lax.psum(
                lax.psum_scatter(grad.reshape(-1), "img", scatter_dimension=0, tiled=True), "crop"
            )
            for grad in grads
        )
    return (
        loss_total,
        output.astype(jnp.bfloat16).reshape(pixels.shape),
        grad_inputs.reshape(pixels.shape),
        *shares,
        *tail,
    )


def solution(mesh):
    return jax.shard_map(
        shards,
        mesh=mesh,
        in_specs=(P("crop", "img", None, None), P("img", None), P("img", None)) + (P(),) * 14,
        out_specs=(P(), P("crop", "img", None, None), P("crop", "img", None, None))
        + (P("img"),) * 6
        + (P(),) * 8,
        check_vma=False,
    )
```

time: 2640 us -> 933 us (0.35)
  waiting for transfers between devices: 1440 us -> 270 us
  matrix products: 544 us -> 114 us
  blocking collectives: 288 us -> 0 us
  Pallas kernels: 0 us -> 123 us
  starting transfers between devices: 7.09 us -> 111 us
  local copies, waits for them, and re-layouts: 259 us -> 186 us
  other arithmetic: 49.5 us -> 104 us
    unnamed x3 -> x4, waiting for transfers between devices: 1320 us -> 0.07 us
    dot_general x30 -> x0, matrix products: 430 us -> none  [the longest x9 152 us: conv_forward(): jnp.einsum('nhwgc,gcd->nhwgd', window, kernel[offset_index], preferred_el...]
    psum x10 -> x0, blocking collectives: 279 us -> none  [the longest x3 82.3 us: normalize(): within = lax.psum(local_sums, 'img')]
    ppermute x6 -> x79, waiting for transfers between devices: 4.55 us -> 236 us  [the longest x76 233 us: swap(): return lax.ppermute(value, axis, pairs)]
    reshape x14 -> x9, local copies, waits for them, and re-layouts: 174 us -> 30.7 us  [the longest x2 13.7 us: pack_blocks(): kernel.reshape(taps, blocks, PACK, gw, gw).transpose(0, 1, 3, 2, 4)]
    pallas_call x0 -> x9, Pallas kernels: none -> 123 us  [the longest x1 33.5 us: conv_wgrad(): pl.pallas_call(functools.partial(wgrad_kernel, width, sides), grid_spec=p...]
    ppermute x6 -> x79, starting transfers between devices: 7.01 us -> 111 us  [the longest x76 103 us: swap(): return lax.ppermute(value, axis, pairs)]
    psum x1, waiting for transfers between devices: 123 us -> 34.6 us  [shards(): mine = lax.psum(mine, 'crop')]
  transfers between devices with their start and end apart: 8 -> 83, of which waited for: 5 -> 55; matrix products, arithmetic and copies ran while one was open for 4% -> 31% of each run, Pallas kernels for 0% -> 10%
where the time goes in v1:
time: 933 us; the launch traced here: 927 us
  waiting for transfers between devices  270 us (29%)
  local copies, waits for them, and re-layouts  186 us (20%)
  Pallas kernels  123 us (13%)
  matrix products  114 us (12%)
  starting transfers between devices  111 us (12%)
  other arithmetic  104 us (11%)
  between operations  18.4 us (2%)
    ppermute x76, waiting for transfers between devices, swap(): return lax.ppermute(value, axis, pairs)  233 us
    ppermute x76, starting transfers between devices, swap(): return lax.ppermute(value, axis, pairs)  103 us
    unnamed x125, local copies, waits for them, and re-layouts  59.2 us
    dot_general x11, matrix products, exact_dot(): jnp.dot(left, right, precision=exact_mode, preferred_element_type=jnp.flo...  51 us
    psum x1, waiting for transfers between devices, shards(): mine = lax.psum(mine, 'crop')  34.6 us
    pallas_call x1, Pallas kernels, conv_wgrad(): pl.pallas_call(functools.partial(wgrad_kernel, width, sides), grid_spec=p...  33.5 us
    pallas_call x1, Pallas kernels, conv_dgrad(): pl.pallas_call(functools.partial(dgrad_kernel, width, sides), grid_spec=p...  30.2 us
    ppermute x4, local copies, waits for them, and re-layouts, swap(): return lax.ppermute(value, axis, pairs)  26 us
  transfers between devices with their start and end apart: 83, of which 55 were waited for; matrix products, arithmetic and copies ran while one was open for 31% of the time, Pallas kernels for 10%

profile of v1, /device:TPU:0, one launch (start us, length us, event | category | flops | bytes accessed | tf_op | source)
XLA Modules:
  0.0 926.5 jit_solution(16456539086473472776)
XLA Ops:
  7.2 12.0 %fusion.95 = (f32[2016]{0:T(1024)S(1)}, f32[2016]{0:T(1024)S(1)}, f32[784,2016]{1,0:T(8,128)}) fusion(bf16[2016,2016]{1,0:T(8,128)(2,1)} %param.21, bf16[1,1,784,2016]{3,2,1,0:T(8,128)(2,1)} %param.18), kind=kOutput, calls=%fused_computation.326 | convolution fusion | flops 6377490944 | bytes 17627904 | tf_op jit(solution)/shard_map/dot_general | solution.py:482
  64.5 25.7 %conv_fwd.1 = (f32[784,2016]{1,0:T(8,128)}, f32[8,2016]{1,0:T(8,128)}) custom-call(s32[1]{0:T(128)} %bitcast.glob_ref, f32[784,2016]{1,0:T(8,128)} %get-tuple-element.123.h_ref, f32[8,2016]{1,0:T(8,128)} %stack.375.p_ref, f32[4,784,256]{2,1,0:T(8,128)} %broadcast_in_dim.105.mask_ref, bf16[9,768,768]{2,1,0:T(8,128)(2,1)} %pack.1.k_ref), custom_call_target="tpu_custom_call" | custom-call | tf_op jit(solution)/shard_map/conv_fwd/pallas_call | solution.py:207
  115.0 8.7 multiply_convert_fusion.3
  123.7 8.7 fusion.94
  147.1 16.2 %convert_bitcast_fusion = (bf16[1,1,784,2016]{3,2,1,0:T(8,128)(2,1)}, f32[784,2016]{1,0:T(8,128)S(1)}) fusion(f32[2016]{0:T(1024)S(1)} %copy-done.37, f32[2016]{0:T(1024)S(1)} %copy-done.34, f32[2016]{0:T(1024)S(1)} %bitcast.448, f32[784,2016]{1,0:T(8,128)} %get-tuple-element.126, f32[2016]{0:T(1024)S(1)} %bitcast.463, bf16[1,1,784,2016]{3,2,1,0:T(8,128)(2,1)} %param.18), kind=kLoop, calls=%fused_computation.23 | loop fusion | flops 17385984 | bytes 18998784 | tf_op jit(solution)/shard_map/reshape | solution.py:703
  183.3 9.5 %collective-permute-done.14 = f32[16,3000]{1,0:T(8,128)S(1)} collective-permute-done((f32[16,3000]{1,0:T(8,128)S(1)}, f32[16,3000]{1,0:T(8,128)S(1)}, u32[]{:S(2)}, u32[]{:S(2)}) %collective-permute-start.14) | collective-permute-done | bytes 192032 | tf_op jit(solution)/shard_map/ppermute | solution.py:280
  242.5 12.9 %fusion.109 = f32[784,2016]{1,0:T(8,128)} fusion(bf16[784,2016]{1,0:T(8,128)(2,1)S(1)} %multiply_convert_fusion.2.right_ref, bf16[2016,2016]{1,0:T(8,128)(2,1)} %param.27), kind=kOutput, calls=%fused_computation.337 | convolution fusion | flops 6372753408 | bytes 17611776 | tf_op jit(solution)/shard_map/rv,wv->rw/dot_general | solution.py:563
  265.6 12.1 %fusion.92 = (f32[2016]{0:T(1024)S(1)}, f32[2016]{0:T(1024)S(1)}, f32[784,2016]{1,0:T(8,128)}) fusion(f32[2016]{0:T(1024)S(1)} %bitcast.471, f32[784,2016]{1,0:T(8,128)} %get-tuple-element.22, f32[2016]{0:T(1024)S(1)} %bitcast.506, f32[2016]{0:T(1024)S(1)} %copy-done.44, f32[2016]{0:T(1024)S(1)} %copy-done.38, f32[16,2016]{1,0:T(8,128)S(1)} %convolution_divide_fusion, ...), kind=kOutput, calls=%fused_computation.323 | convolution fusion | flops 330342208 | bytes 25469248 | tf_op jit(solution)/shard_map/dot_general | solution.py:293
  311.9 8.7 copy.64
  328.7 30.2 %conv_dgrad.1 = (f32[784,2016]{1,0:T(8,128)}, f32[8,2016]{1,0:T(8,128)}) custom-call(s32[1]{0:T(128)} %bitcast.glob_ref, bf16[784,2016]{1,0:T(8,128)(2,1)} %multiply_convert_fusion.1.g_ref, f32[784,2016]{1,0:T(8,128)} %get-tuple-element.123.h_ref, f32[8,2016]{1,0:T(8,128)} %stack.375.p_ref, f32[4,784,256]{2,1,0:T(8,128)} %broadcast_in_dim.105.mask_ref, ...), custom_call_target="tpu_custom_call" | custom-call | tf_op jit(solution)/shard_map/conv_dgrad/pallas_call | solution.py:228
  358.9 33.5 %conv_wgrad.1 = f32[9,9,56,256]{3,2,1,0:T(8,128)} custom-call(s32[1]{0:T(128)} %bitcast.glob_ref, bf16[784,2016]{1,0:T(8,128)(2,1)} %multiply_convert_fusion.1.g_ref, f32[784,2016]{1,0:T(8,128)} %get-tuple-element.123.h_ref, f32[8,2016]{1,0:T(8,128)} %stack.375.p_ref, f32[4,784,256]{2,1,0:T(8,128)} %broadcast_in_dim.105.mask_ref), custom_call_target="tpu_custom_call" | custom-call | tf_op jit(solution)/shard_map/conv_wgrad/pallas_call | solution.py:250
  420.1 13.2 %add_bitcast_fusion = f32[1,1,784,2016]{3,2,1,0:T(8,128)} fusion(f32[784,2016]{1,0:T(8,128)} %get-tuple-element.133, bf16[784,2016]{1,0:T(8,128)(2,1)S(1)} %multiply_convert_fusion.right_ref, bf16[2016,2016]{1,0:T(8,128)(2,1)} %param.21), kind=kOutput, calls=%fused_computation | convolution fusion | flops 6374333952 | bytes 23933952 | tf_op jit(solution)/shard_map/rv,wv->rw/dot_general | solution.py:602
  452.0 9.1 copy.58
  477.9 14.9 %collective-permute-done.48 = f32[1,2,32,504]{3,2,1,0:T(8,128)S(1)} collective-permute-done((f32[1,2,32,504]{3,2,1,0:T(8,128)S(1)}, f32[1,2,32,504]{3,2,1,0:T(8,128)S(1)}, u32[]{:S(2)}, u32[]{:S(2)}) %collective-permute-start.48) | collective-permute-done | bytes 129056 | tf_op jit(solution)/shard_map/ppermute | solution.py:280
  574.4 10.2 %collective-permute-done.76 = f32[1,32,3000]{2,1,0:T(8,128)S(1)} collective-permute-done((f32[1,32,3000]{2,1,0:T(8,128)S(1)}, f32[1,32,3000]{2,1,0:T(8,128)S(1)}, u32[]{:S(2)}, u32[]{:S(2)}) %collective-permute-start.76) | collective-permute-done | bytes 384032 | tf_op jit(solution)/shard_map/ppermute | solution.py:280
  595.6 9.0 collective-permute-done.78
  605.7 8.7 copy.59
  614.4 12.0 %add.566 = f32[4,256,2016]{2,1,0:T(8,128)} add(f32[4,256,2016]{2,1,0:T(8,128)} %copy-done.3, f32[4,256,2016]{2,1,0:T(8,128)} %copy.59) | non-fusion elementwise | flops 2064384 | bytes 24772608 | tf_op jit(solution)/shard_map/add | solution.py:666
  637.7 8.8 copy.65
  646.5 11.9 %add.598 = f32[4,256,2016]{2,1,0:T(8,128)} add(f32[4,256,2016]{2,1,0:T(8,128)} %copy-done.2, f32[4,256,2016]{2,1,0:T(8,128)} %copy.65) | non-fusion elementwise | flops 2064384 | bytes 24772608 | tf_op jit(solution)/shard_map/add | solution.py:655
  698.0 34.6 %all-reduce.7.cloned.1.call-done = f32[12,56,256]{2,1,0:T(8,128)} async-done(((f32[12,56,256]{2,1,0:T(8,128)}), f32[12,56,256]{2,1,0:T(8,128)}) %all-reduce.7.cloned.1.call-update) | async-done | bytes 688144 | tf_op jit(solution)/shard_map/psum | solution.py:678
  736.5 25.0 %collective-permute-done.40 = f32[2,32,2016]{2,1,0:T(8,128)S(1)} collective-permute-done((f32[2,32,2016]{2,1,0:T(8,128)}, f32[2,32,2016]{2,1,0:T(8,128)S(1)}, u32[]{:S(2)}, u32[]{:S(2)}) %collective-permute-start.40) | collective-permute-done | bytes 516128 | tf_op jit(solution)/shard_map/ppermute | solution.py:280
  772.9 27.1 %collective-permute-start.42 = (f32[1,32,2016]{2,1,0:T(8,128)S(1)}, f32[1,32,2016]{2,1,0:T(8,128)S(1)}, u32[]{:S(2)}, u32[]{:S(2)}) collective-permute-start(f32[1,32,2016]{2,1,0:T(8,128)S(1)} %dynamic-slice_add_fusion.1), channel_id=1, source_target_pairs={{0,8},{8,0},{16,24},{24,16},{1,9},{9,1},{17,25},{25,17},{2,10},{10... | collective-permute-start | bytes 774152 | tf_op jit(solution)/shard_map/ppermute | solution.py:280
  832.6 36.1 %collective-permute-done.62 = f32[1,256,2016]{1,2,0:T(8,128)} collective-permute-done((f32[1,256,2016]{1,2,0:T(8,128)}, f32[1,256,2016]{1,2,0:T(8,128)}, u32[]{:S(2)}, u32[]{:S(2)}) %collective-permute-start.62) | collective-permute-done | bytes 2064416 | tf_op jit(solution)/shard_map/ppermute | solution.py:280
  (521 shorter events, 509.4 us)
Async XLA Ops:
  7.2 455.9 %all-gather.5.cloned.1.call-start = ((), (), s32[]{:S(2)}) async-start(), calls=%async_computation.4 | async-start | bytes 2949120 | tf_op jit(solution)/shard_map/all_gather | solution.py:633
  33.2 27.8 %collective-permute-start.3 = (f32[2,2016]{1,0:T(2,128)S(1)}, f32[2,2016]{1,0:T(2,128)S(1)}, u32[]{:S(2)}, u32[]{:S(2)}) collective-permute-start(f32[2,2016]{1,0:T(2,128)S(1)} %add.509), channel_id=1, source_target_pairs={{0,4},{1,5},{2,6},{3,7},{4,0},{5,1},{6,2},{7,3},{8,12},{9,13},{10,... | collective-permute-start | bytes 48392 | tf_op jit(solution)/shard_map/ppermute | solution.py:280
  232.6 240.6 %all-gather.3.cloned.1.call-start = ((), (), s32[]{:S(2)}) async-start(), calls=%async_computation.3 | async-start | bytes 2949120 | tf_op jit(solution)/shard_map/all_gather | solution.py:637
  284.7 400.2 %reduce-scatter.2.cloned.1.call-start = ((), (), s32[]{:S(2)}) async-start(), calls=%async_computation.1 | async-start | bytes 6193152 | tf_op jit(solution)/shard_map/reduce_scatter | solution.py:677
  289.0 31.7 %collective-permute-start.25 = (f32[4,2016]{1,0:T(4,128)S(1)}, f32[4,2016]{1,0:T(4,128)S(1)}, u32[]{:S(2)}, u32[]{:S(2)}) collective-permute-start(f32[4,2016]{1,0:T(4,128)S(1)} %add.557), channel_id=1, source_target_pairs={{0,4},{1,5},{2,6},{3,7},{4,0},{5,1},{6,2},{7,3},{8,12},{9,13},{10,... | collective-permute-start | bytes 96776 | tf_op jit(solution)/shard_map/ppermute | solution.py:280
  320.6 317.0 %collective-permute-start.60 = (f32[4,256,2016]{1,2,0:T(8,128)}, f32[4,256,2016]{1,2,0:T(8,128)}, u32[]{:S(2)}, u32[]{:S(2)}) collective-permute-start(f32[4,256,2016]{1,2,0:T(8,128)} %copy.64), channel_id=1, source_target_pairs={{0,1},{1,0},{2,3},{3,2},{4,5},{5,4},{6,7},{7,6},{8,9},{9,8},{10,11... | collective-permute-start | bytes 24772616 | tf_op jit(solution)/shard_map/ppermute | solution.py:280
  412.1 320.5 %all-reduce.7.cloned.1.call-start = ((), (), s32[]{:S(2)}) async-start(), calls=%async_computation.2 | async-start | bytes 1376256 | tf_op jit(solution)/shard_map/psum | solution.py:678
  413.0 48.2 %collective-permute-start.30 = (f32[8,2016]{1,0:T(8,128)S(1)}, f32[8,2016]{1,0:T(8,128)S(1)}, u32[]{:S(2)}, u32[]{:S(2)}) collective-permute-start(f32[8,2016]{1,0:T(8,128)S(1)} %pad_maximum_fusion.18), channel_id=1, source_target_pairs={{0,16},{8,24},{16,0},{24,8},{1,17},{9,25},{17,1},{25,9},{2,18},{10... | collective-permute-start | bytes 193544 | tf_op jit(solution)/shard_map/ppermute | solution.py:280
  461.1 144.5 %collective-permute-start.31 = (f32[4,256,2016]{1,2,0:T(8,128)}, f32[4,256,2016]{1,2,0:T(8,128)}, u32[]{:S(2)}, u32[]{:S(2)}) collective-permute-start(f32[4,256,2016]{1,2,0:T(8,128)} %copy.58), channel_id=1, source_target_pairs={{0,1},{1,0},{2,3},{3,2},{4,5},{5,4},{6,7},{7,6},{8,9},{9,8},{10,11... | collective-permute-start | bytes 24772616 | tf_op jit(solution)/shard_map/ppermute | solution.py:280
  469.6 101.4 %collective-permute-start.75 = (f32[1,2,32,3000]{3,2,1,0:T(8,128)}, f32[1,2,32,3000]{3,2,1,0:T(8,128)}, u32[]{:S(2)}, u32[]{:S(2)}) collective-permute-start(f32[1,2,32,3000]{3,2,1,0:T(8,128)} %dynamic-slice_bitcast_fusion.4), channel_id=1, source_target_pairs={{0,16},{8,24},{16,0},{24,8},{1,17},{9,25},{17,1},{25,9},{2,18},{10... | collective-permute-start | bytes 2304008 | tf_op jit(solution)/shard_map/ppermute | solution.py:280
  472.6 100.0 %collective-permute-start.71 = (f32[1,2,32,3000]{3,2,1,0:T(8,128)}, f32[1,2,32,3000]{3,2,1,0:T(8,128)S(1)}, u32[]{:S(2)}, u32[]{:S(2)}) collective-permute-start(f32[1,2,32,3000]{3,2,1,0:T(8,128)} %dynamic-slice_bitcast_fusion.5), channel_id=1, source_target_pairs={{0,8},{8,0},{16,24},{24,16},{1,9},{9,1},{17,25},{25,17},{2,10},{10... | collective-permute-start | bytes 2304008 | tf_op jit(solution)/shard_map/ppermute | solution.py:280
  476.5 16.3 %collective-permute-start.48 = (f32[1,2,32,504]{3,2,1,0:T(8,128)S(1)}, f32[1,2,32,504]{3,2,1,0:T(8,128)S(1)}, u32[]{:S(2)}, u32[]{:S(2)}) collective-permute-start(f32[1,2,32,504]{3,2,1,0:T(8,128)S(1)} %dynamic-slice_bitcast_fusion.16), channel_id=1, source_target_pairs={{0,16},{8,24},{16,0},{24,8},{1,17},{9,25},{17,1},{25,9},{2,18},{10... | collective-permute-start | bytes 387080 | tf_op jit(solution)/shard_map/ppermute | solution.py:280
  594.4 40.6 %collective-permute-start.74 = (f32[1,2,32,3000]{3,2,1,0:T(8,128)}, f32[1,2,32,3000]{3,2,1,0:T(8,128)}, u32[]{:S(2)}, u32[]{:S(2)}) collective-permute-start(f32[1,2,32,3000]{3,2,1,0:T(8,128)} %pad_maximum_fusion.3), channel_id=1, source_target_pairs={{0,8},{8,0},{16,24},{24,16},{1,9},{9,1},{17,25},{25,17},{2,10},{10... | collective-permute-start | bytes 2304008 | tf_op jit(solution)/shard_map/ppermute | solution.py:280
  631.9 38.6 %collective-permute-start.38 = (f32[4,2,32,2016]{3,2,1,0:T(8,128)}, f32[4,2,32,2016]{3,2,1,0:T(8,128)}, u32[]{:S(2)}, u32[]{:S(2)}) collective-permute-start(f32[4,2,32,2016]{3,2,1,0:T(8,128)} %dynamic-slice_bitcast_fusion), channel_id=1, source_target_pairs={{0,16},{8,24},{16,0},{24,8},{1,17},{9,25},{17,1},{25,9},{2,18},{10... | collective-permute-start | bytes 6193160 | tf_op jit(solution)/shard_map/ppermute | solution.py:280
  634.1 41.1 %collective-permute-start.32 = (f32[4,2,32,2016]{3,2,1,0:T(8,128)}, f32[4,2,32,2016]{3,2,1,0:T(8,128)}, u32[]{:S(2)}, u32[]{:S(2)}) collective-permute-start(f32[4,2,32,2016]{3,2,1,0:T(8,128)} %dynamic-slice_bitcast_fusion.1), channel_id=1, source_target_pairs={{0,8},{8,0},{16,24},{24,16},{1,9},{9,1},{17,25},{25,17},{2,10},{10... | collective-permute-start | bytes 6193160 | tf_op jit(solution)/shard_map/ppermute | solution.py:280
  668.4 136.1 %collective-permute-start.61 = (f32[2,256,2016]{1,2,0:T(8,128)}, f32[2,256,2016]{1,2,0:T(8,128)}, u32[]{:S(2)}, u32[]{:S(2)}) collective-permute-start(f32[2,256,2016]{1,2,0:T(8,128)} %bitcast.441), channel_id=1, source_target_pairs={{0,2},{1,3},{2,0},{3,1},{4,6},{5,7},{6,4},{7,5},{8,10},{9,11},{10,... | collective-permute-start | bytes 12386312 | tf_op jit(solution)/shard_map/ppermute | solution.py:280
  673.1 15.0 %collective-permute-start.39 = (f32[4,32,2016]{2,1,0:T(8,128)S(1)}, f32[4,32,2016]{2,1,0:T(8,128)}, u32[]{:S(2)}, u32[]{:S(2)}) collective-permute-start(f32[4,32,2016]{2,1,0:T(8,128)S(1)} %dynamic-slice_bitcast_fusion.2), channel_id=1, source_target_pairs={{0,8},{8,0},{16,24},{24,16},{1,9},{9,1},{17,25},{25,17},{2,10},{10... | collective-permute-start | bytes 3096584 | tf_op jit(solution)/shard_map/ppermute | solution.py:280
  678.2 16.3 %collective-permute-start.33 = (f32[4,32,2016]{2,1,0:T(8,128)}, f32[4,32,2016]{2,1,0:T(8,128)}, u32[]{:S(2)}, u32[]{:S(2)}) collective-permute-start(f32[4,32,2016]{2,1,0:T(8,128)} %dynamic-slice_bitcast_fusion.3), channel_id=1, source_target_pairs={{0,16},{8,24},{16,0},{24,8},{1,17},{9,25},{17,1},{25,9},{2,18},{10... | collective-permute-start | bytes 3096584 | tf_op jit(solution)/shard_map/ppermute | solution.py:280
  690.6 71.0 %collective-permute-start.40 = (f32[2,32,2016]{2,1,0:T(8,128)}, f32[2,32,2016]{2,1,0:T(8,128)S(1)}, u32[]{:S(2)}, u32[]{:S(2)}) collective-permute-start(f32[2,32,2016]{2,1,0:T(8,128)} %dynamic-slice_bitcast_fusion.8), channel_id=1, source_target_pairs={{0,2},{1,3},{2,0},{3,1},{4,6},{5,7},{6,4},{7,5},{8,10},{9,11},{10,... | collective-permute-start | bytes 1548296 | tf_op jit(solution)/shard_map/ppermute | solution.py:280
  698.0 69.3 %collective-permute-start.34 = (f32[2,32,2016]{2,1,0:T(8,128)}, f32[2,32,2016]{2,1,0:T(8,128)}, u32[]{:S(2)}, u32[]{:S(2)}) collective-permute-start(f32[2,32,2016]{2,1,0:T(8,128)} %dynamic-slice_bitcast_fusion.9), channel_id=1, source_target_pairs={{0,2},{1,3},{2,0},{3,1},{4,6},{5,7},{6,4},{7,5},{8,10},{9,11},{10,... | collective-permute-start | bytes 1548296 | tf_op jit(solution)/shard_map/ppermute | solution.py:280
  768.6 35.1 %collective-permute-start.35 = (f32[1,32,2016]{2,1,0:T(8,128)S(1)}, f32[1,32,2016]{2,1,0:T(8,128)S(1)}, u32[]{:S(2)}, u32[]{:S(2)}) collective-permute-start(f32[1,32,2016]{2,1,0:T(8,128)S(1)} %constant_dynamic-slice_fusion.6), channel_id=1, source_target_pairs={{0,4},{1,5},{2,6},{3,7},{4,0},{5,1},{6,2},{7,3},{8,12},{9,13},{10,... | collective-permute-start | bytes 774152 | tf_op jit(solution)/shard_map/ppermute | solution.py:280
  772.9 47.6 %collective-permute-start.42 = (f32[1,32,2016]{2,1,0:T(8,128)S(1)}, f32[1,32,2016]{2,1,0:T(8,128)S(1)}, u32[]{:S(2)}, u32[]{:S(2)}) collective-permute-start(f32[1,32,2016]{2,1,0:T(8,128)S(1)} %dynamic-slice_add_fusion.1), channel_id=1, source_target_pairs={{0,8},{8,0},{16,24},{24,16},{1,9},{9,1},{17,25},{25,17},{2,10},{10... | collective-permute-start | bytes 774152 | tf_op jit(solution)/shard_map/ppermute | solution.py:280
  803.8 18.3 %collective-permute-start.36 = (f32[1,32,2016]{2,1,0:T(8,128)S(1)}, f32[1,32,2016]{2,1,0:T(8,128)S(1)}, u32[]{:S(2)}, u32[]{:S(2)}) collective-permute-start(f32[1,32,2016]{2,1,0:T(8,128)S(1)} %dynamic-slice_add_fusion.2), channel_id=1, source_target_pairs={{0,16},{8,24},{16,0},{24,8},{1,17},{9,25},{17,1},{25,9},{2,18},{10... | collective-permute-start | bytes 774152 | tf_op jit(solution)/shard_map/ppermute | solution.py:280
  820.5 48.2 %collective-permute-start.62 = (f32[1,256,2016]{1,2,0:T(8,128)}, f32[1,256,2016]{1,2,0:T(8,128)}, u32[]{:S(2)}, u32[]{:S(2)}) collective-permute-start(f32[1,256,2016]{1,2,0:T(8,128)} %copy.68), channel_id=1, source_target_pairs={{0,4},{1,5},{2,6},{3,7},{4,0},{5,1},{6,2},{7,3},{8,12},{9,13},{10,... | collective-permute-start | bytes 6193160 | tf_op jit(solution)/shard_map/ppermute | solution.py:280
  (111 other events, 1017.6 us)
Sparse Core Ops, SparseCore 0:
  232.7 33.3 all-gather.4
  284.8 31.7 all-gather.2
  412.2 59.3 reduce-scatter.1
  685.0 47.5 all-reduce.6

commit v2 on v1

v2 whole, which is shorter than its diff:
```python
import functools
import jax
import jax.numpy as jnp
from jax import lax
from jax.experimental import pallas as pl
from jax.experimental.pallas import tpu as pltpu

VMEM_LIMIT = 56 * 1024 * 1024
PACK = 4
EDGE = 16
CHUNK = 112


def cost(micros):
    return pl.CostEstimate(flops=micros * 1000000, bytes_accessed=micros * 1000, transcendentals=0)


def params():
    return pltpu.CompilerParams(vmem_limit_bytes=VMEM_LIMIT)


def lane_of(rows):
    return lax.broadcasted_iota(jnp.int32, (rows, 128), 1)


def take(refs, start, rows, skip, width):
    a, b, c = [ref[start : start + rows, :].astype(jnp.float32) for ref in refs]
    back = lax.rem(128 - skip, 128)
    a, b, c = [pltpu.roll(v, back, 1) for v in (a, b, c)]
    lane = lane_of(rows)
    near = lane < 128 - skip
    return jnp.where(near, a, b), jnp.where(lane < width - 128, jnp.where(near, b, c), 0.0)


def put(ref, start, rows, base, skip, first, second):
    first, second = pltpu.roll(first, skip, 1), pltpu.roll(second, skip, 1)
    lane = lane_of(rows)
    inside = lane >= skip
    last = jnp.minimum(base + 2, ref.shape[1] // 128 - 1)

    def at(tile):
        return (slice(start, start + rows), pl.ds(pl.multiple_of(tile * 128, 128), 128))

    ref[at(last)] = second
    ref[at(base + 1)] = jnp.where(inside, second, first)
    ref[at(base)] = jnp.where(inside, first, ref[at(base)])


def place_of(block, width):
    start = block * width
    base = start // 128
    return base, start - base * 128


def clear_edges(ref):
    @pl.when(pl.program_id(0) == 0)
    def _():
        ref[0:EDGE, :] = jnp.zeros((EDGE, ref.shape[1]), ref.dtype)
        ref[ref.shape[0] - EDGE :, :] = jnp.zeros((EDGE, ref.shape[1]), ref.dtype)


def chunks(rows):
    return range(0, rows, CHUNK)


def fill_act(h_refs, p_refs, skip, width, starts, act):
    scale = take(p_refs, 0, 8, skip, width)
    for r in starts:
        for tile, h in enumerate(take(h_refs, r, CHUNK, skip, width)):
            pre = h * scale[tile][0:1] + scale[tile][1:2]
            value = pre * jax.nn.sigmoid(pre)
            act[EDGE + r : EDGE + r + CHUNK, 128 * tile : 128 * tile + 128] = value.astype(
                jnp.bfloat16
            ).astype(jnp.float32)


def fill_grad(g_refs, skip, width, starts, grad):
    for r in starts:
        for tile, g in enumerate(take(g_refs, r, CHUNK, skip, width)):
            grad[EDGE + r : EDGE + r + CHUNK, 128 * tile : 128 * tile + 128] = g


def stack(source, mask_ref, low, high, step, starts, dest):
    for r in starts:
        for tile in range(2):
            cols = slice(128 * tile, 128 * tile + 128)
            here = slice(r, r + CHUNK)
            before = source[EDGE + r - step : EDGE + r - step + CHUNK, cols] * mask_ref[low, here, :]
            after = source[EDGE + r + step : EDGE + r + step + CHUNK, cols] * mask_ref[high, here, :]
            middle = source[EDGE + r : EDGE + r + CHUNK, cols]
            dest[here, 128 * tile : 128 * tile + 128] = before.astype(jnp.bfloat16)
            dest[here, 256 + 128 * tile : 384 + 128 * tile] = middle.astype(jnp.bfloat16)
            dest[here, 512 + 128 * tile : 640 + 128 * tile] = after.astype(jnp.bfloat16)


def fwd_step(width, side, glob_ref, refs):
    h_refs, p_refs, (mask_ref, k_ref, out_ref, st_ref, act, cols, wide) = refs[:3], refs[3:6], refs[6:]
    rows = h_refs[0].shape[0]
    base, skip = place_of(pl.program_id(0), width)
    starts = list(chunks(rows))
    fill_act(h_refs, p_refs, skip, width, starts[:1], act)
    for i, r in enumerate(starts):
        fill_act(h_refs, p_refs, skip, width, starts[i + 1 : i + 2], act)
        stack(act, mask_ref, 0, 1, 1, [r], cols)
        wide[EDGE + r : EDGE + r + CHUNK, :] = jnp.dot(
            cols[r : r + CHUNK, :], k_ref[0], preferred_element_type=jnp.float32
        )
    sums = [jnp.zeros((8, 128), jnp.float32)] * 4
    for r in starts:
        here = slice(r, r + CHUNK)
        tiles = []
        for tile in range(2):
            lo = 128 * tile
            total = (
                wide[EDGE + r : EDGE + r + CHUNK, 256 + lo : 384 + lo]
                + wide[EDGE + r - side : EDGE + r - side + CHUNK, lo : 128 + lo] * mask_ref[2, here, :]
                + wide[EDGE + r + side : EDGE + r + side + CHUNK, 512 + lo : 640 + lo] * mask_ref[3, here, :]
            )
            tiles.append(total)
            sums[tile] += jnp.sum(total.reshape(-1, 8, 128), axis=0)
            sums[2 + tile] += jnp.sum((total * total).reshape(-1, 8, 128), axis=0)
        put(out_ref, r, CHUNK, base, skip, *tiles)
    put_sums(st_ref, base, skip, sums)


def put_sums(st_ref, base, skip, sums):
    line = lax.broadcasted_iota(jnp.int32, (8, 128), 0)
    tiles = [
        jnp.where(
            line == 0,
            jnp.sum(sums[tile], axis=0, keepdims=True),
            jnp.sum(sums[2 + tile], axis=0, keepdims=True),
        )
        for tile in range(2)
    ]
    put(st_ref, 0, 8, base, skip, *tiles)


def dgrad_step(width, side, glob_ref, refs):
    g_refs, h_refs, p_refs = refs[:3], refs[3:6], refs[6:9]
    mask_ref, k_ref, out_ref, st_ref, grad, lines, wide = refs[9:]
    rows = h_refs[0].shape[0]
    base, skip = place_of(pl.program_id(0), width)
    starts = list(chunks(rows))
    fill_grad(g_refs, skip, width, starts[:1], grad)
    for i, r in enumerate(starts):
        fill_grad(g_refs, skip, width, starts[i + 1 : i + 2], grad)
        stack_lines(grad, mask_ref, side, [r], lines)
    wide[EDGE : EDGE + rows, :] = lax.dot_general(
        lines[...], k_ref[0], (((1,), (1,)), ((), ())), preferred_element_type=jnp.float32
    )
    par = take(p_refs, 0, 8, skip, width)
    sums = [jnp.zeros((8, 128), jnp.float32)] * 4
    for r in starts:
        here = slice(r, r + CHUNK)
        h_tiles = take(h_refs, r, CHUNK, skip, width)
        tiles = []
        for tile in range(2):
            lo = 128 * tile
            total = (
                wide[EDGE + r : EDGE + r + CHUNK, 256 + lo : 384 + lo]
                + wide[EDGE + r + 1 : EDGE + r + 1 + CHUNK, lo : 128 + lo] * mask_ref[1, here, :]
                + wide[EDGE + r - 1 : EDGE + r - 1 + CHUNK, 512 + lo : 640 + lo] * mask_ref[0, here, :]
            )
            p = par[tile]
            pre = h_tiles[tile] * p[0:1] + p[1:2]
            sig = jax.nn.sigmoid(pre)
            ga = total * (sig * (1.0 + pre * (1.0 - sig)))
            xhat = h_tiles[tile] * p[2:3] + p[3:4]
            tiles.append(ga)
            sums[tile] += jnp.sum(ga.reshape(-1, 8, 128), axis=0)
            sums[2 + tile] += jnp.sum((ga * xhat).reshape(-1, 8, 128), axis=0)
        put(out_ref, r, CHUNK, base, skip, *tiles)
    put_sums(st_ref, base, skip, sums)


def stack_lines(grad, mask_ref, side, starts, dest):
    for r in starts:
        for tile in range(2):
            cols = slice(128 * tile, 128 * tile + 128)
            here = slice(r, r + CHUNK)
            below = grad[EDGE + r + side : EDGE + r + side + CHUNK, cols] * mask_ref[3, here, :]
            above = grad[EDGE + r - side : EDGE + r - side + CHUNK, cols] * mask_ref[2, here, :]
            middle = grad[EDGE + r : EDGE + r + CHUNK, cols]
            dest[here, 128 * tile : 128 * tile + 128] = below.astype(jnp.bfloat16)
            dest[here, 256 + 128 * tile : 384 + 128 * tile] = middle.astype(jnp.bfloat16)
            dest[here, 512 + 128 * tile : 640 + 128 * tile] = above.astype(jnp.bfloat16)


def wgrad_step(width, side, glob_ref, refs):
    g_refs, h_refs, p_refs = refs[:3], refs[3:6], refs[6:9]
    mask_ref, out_ref, source, grad, cols, lines = refs[9], *refs[-5:]
    rows = h_refs[0].shape[0]
    block = pl.program_id(0) + glob_ref[1]
    _, skip = place_of(block, width)
    starts = list(chunks(rows))
    fill_act(h_refs, p_refs, skip, width, starts, source)
    fill_grad(g_refs, skip, width, starts, grad)
    stack(source, mask_ref, 0, 1, 1, starts, cols)
    stack_lines(grad, mask_ref, side, starts, lines)
    gw = width // PACK
    lanes = lax.broadcasted_iota(jnp.int32, (gw, 256), 1)
    for dx in range(3):
        acc = lax.dot_general(
            cols[:, 256 * dx : 256 * dx + 256],
            lines[...],
            (((0,), (0,)), ((), ())),
            preferred_element_type=jnp.float32,
        )
        for dy in range(3):
            small = jnp.zeros((gw, 256), jnp.float32)
            for g in range(PACK):
                piece = acc[gw * g : gw * g + gw, 256 * dy : 256 * dy + 256]
                small = jnp.where((lanes >= gw * g) & (lanes < gw * g + gw), piece, small)
            out_ref[3 * dy + dx, 0] = small


def conv_kernel(step, tall, width, sides, glob_ref, *refs):
    for ref in refs:
        if ref.shape[0] == tall:
            clear_edges(ref)
    for flag, side in ((1, sides[0]), (0, sides[1])):

        @pl.when(glob_ref[0] == flag)
        def _(side=side):
            step(width, side, glob_ref, refs)


def pack_kernel(gw, k_ref, out_ref):
    width = PACK * gw
    lane = lax.broadcasted_iota(jnp.int32, (gw, 256), 1)
    row = lax.broadcasted_iota(jnp.int32, (gw, 256), 0)
    spread = jnp.zeros((gw, 256), jnp.float32)
    for g in range(PACK):
        spread = jnp.where(lane == row + gw * g, 1.0, spread)
    spread = spread.astype(jnp.bfloat16)
    lane = lax.broadcasted_iota(jnp.int32, (width, 256), 1)
    row = lax.broadcasted_iota(jnp.int32, (width, 256), 0)
    inside = lane < 0
    for g in range(PACK):
        low, high = gw * g, gw * g + gw
        inside = inside | ((lane >= low) & (lane < high) & (row >= low) & (row < high))
    rest = jnp.zeros((256 - width, 256), jnp.float32)
    for dy in range(3):
        for dx in range(3):
            tap = k_ref[3 * dy + dx].astype(jnp.float32).reshape(width, gw).astype(jnp.bfloat16)
            wide = jnp.dot(tap, spread, preferred_element_type=jnp.float32)
            out_ref[0, 256 * dx : 256 * dx + 256, 256 * dy : 256 * dy + 256] = jnp.concatenate(
                [jnp.where(inside, wide, 0.0), rest], axis=0
            ).astype(jnp.bfloat16)


def pack_blocks(first, count, kernel, done=None):
    taps, groups, gw, _ = kernel.shape
    given = () if done is None else (done,)

    def body(k_ref, *refs):
        pack_kernel(gw, k_ref, refs[-1])

    return pl.pallas_call(
        body,
        grid=(count,),
        in_specs=[pl.BlockSpec((taps, PACK, gw, gw), lambda b: (0, b + first, 0, 0))]
        + [pl.BlockSpec(memory_space=pl.ANY)] * len(given),
        out_specs=pl.BlockSpec((1, 768, 768), lambda b: (b + first, 0, 0)),
        out_shape=jax.ShapeDtypeStruct((groups // PACK, 768, 768), jnp.bfloat16),
        input_output_aliases={1: 0} if given else {},
        compiler_params=params(),
        cost_estimate=cost(3),
        name="pack",
    )(kernel, *given)


def tile_specs(rows, width, chans, first=0):
    def spec(j):
        last = -(-chans // 128) - 1
        return pl.BlockSpec(
            (rows, 128), lambda b, s: (0, jnp.minimum((b + first) * width // 128 + j, last))
        )

    return [spec(j) for j in range(3)]


def conv_specs(rows):
    whole = lambda r: pl.BlockSpec((r, 2048), lambda b, s: (0, 0))
    mask = pl.BlockSpec((4, rows, 128), lambda b, s: (0, 0, 0))
    kern = pl.BlockSpec((1, 768, 768), lambda b, s: (b, 0, 0))
    return whole, mask, kern


def conv_scratch(rows, count):
    tall = rows + 2 * EDGE
    return [pltpu.VMEM((tall, 256), jnp.float32)] + [pltpu.VMEM((rows, 768), jnp.bfloat16)] * count


def conv_fwd(glob, h, par, masks, packed, width, sides):
    rows, chans = h.shape
    whole, mask, kern = conv_specs(rows)
    tiles = functools.partial(tile_specs, width=width, chans=chans)
    return pl.pallas_call(
        functools.partial(conv_kernel, fwd_step, rows + 2 * EDGE, width, sides),
        grid_spec=pltpu.PrefetchScalarGridSpec(
            num_scalar_prefetch=1,
            grid=(packed.shape[0],),
            in_specs=tiles(rows) + tiles(8) + [mask, kern],
            out_specs=[whole(rows), whole(8)],
            scratch_shapes=conv_scratch(rows, 1) + [pltpu.VMEM((rows + 2 * EDGE, 768), jnp.float32)],
        ),
        out_shape=[
            jax.ShapeDtypeStruct((rows, chans), jnp.float32),
            jax.ShapeDtypeStruct((8, chans), jnp.float32),
        ],
        compiler_params=params(),
        cost_estimate=cost(20),
        name="conv_fwd",
    )(glob, h, h, h, par, par, par, masks, packed)


def conv_dgrad(glob, grad, h, par, masks, packed, width, sides):
    rows, chans = h.shape
    whole, mask, kern = conv_specs(rows)
    tiles = functools.partial(tile_specs, width=width, chans=chans)
    return pl.pallas_call(
        functools.partial(conv_kernel, dgrad_step, rows + 2 * EDGE, width, sides),
        grid_spec=pltpu.PrefetchScalarGridSpec(
            num_scalar_prefetch=1,
            grid=(packed.shape[0],),
            in_specs=tiles(rows) + tiles(rows) + tiles(8) + [mask, kern],
            out_specs=[whole(rows), whole(8)],
            scratch_shapes=conv_scratch(rows, 1) + [pltpu.VMEM((rows + 2 * EDGE, 768), jnp.float32)],
        ),
        out_shape=[
            jax.ShapeDtypeStruct((rows, chans), jnp.float32),
            jax.ShapeDtypeStruct((8, chans), jnp.float32),
        ],
        compiler_params=params(),
        cost_estimate=cost(20),
        name="conv_dgrad",
    )(glob, grad, grad, grad, h, h, h, par, par, par, masks, packed)


def conv_wgrad(glob, grad, h, par, masks, first, count, blocks, width, sides, done=None):
    rows, chans = h.shape
    whole, mask, kern = conv_specs(rows)
    tiles = functools.partial(tile_specs, width=width, chans=chans, first=first)
    gw = width // PACK
    given = () if done is None else (done,)
    return pl.pallas_call(
        functools.partial(conv_kernel, wgrad_step, rows + 2 * EDGE, width, sides),
        grid_spec=pltpu.PrefetchScalarGridSpec(
            num_scalar_prefetch=1,
            grid=(count,),
            in_specs=tiles(rows) + tiles(rows) + tiles(8) + [mask]
            + [pl.BlockSpec(memory_space=pl.ANY)] * len(given),
            out_specs=pl.BlockSpec((9, 1, gw, 256), lambda b, s: (0, b + first, 0, 0)),
            scratch_shapes=conv_scratch(rows, 0) + conv_scratch(rows, 2),
        ),
        out_shape=jax.ShapeDtypeStruct((9, blocks, gw, 256), jnp.float32),
        input_output_aliases={11: 0} if given else {},
        compiler_params=params(),
        cost_estimate=cost(2 * count),
        name="conv_wgrad",
    )(
        jnp.concatenate([glob, jnp.full((1,), first, jnp.int32)]),
        grad,
        grad,
        grad,
        h,
        h,
        h,
        par,
        par,
        par,
        masks,
        *given,
    )


from jax.experimental.layout import Layout, with_layout_constraint
from jax.sharding import PartitionSpec as P

IMG_DEV = 4
SIDE = 14
SMALL_SIDE = 7
LOW_COLUMNS = 0
TAIL = (0, 2, 0, 2, 1, 0, 2, 0, 2, 1, 2, 0, 2)
WIDE = 2048
WIDE_PROTOS = 3072

norm_epsilon = 1e-05
length_epsilon = 1e-06
sharpening_divisor = 0.1
sharpness = 0.05
exact_mode = lax.Precision.HIGHEST


def plain(value):
    return with_layout_constraint(value, Layout(major_to_minor=tuple(range(value.ndim))))


def swap(value, axis, mask):
    pairs = [(source, source ^ mask) for source in range(lax.axis_size(axis))]
    if value.ndim < 3:
        return lax.ppermute(value, axis, pairs)
    return plain(lax.ppermute(plain(value), axis, pairs))


def tie(*values):
    return lax.optimization_barrier(values)


def smooth_gate(values):
    return values * jax.nn.sigmoid(values)


def smooth_slope(values):
    sigma_values = jax.nn.sigmoid(values)
    return sigma_values * (1.0 + values * (1.0 - sigma_values))


def exact_dot(left, right):
    return jnp.dot(left, right, precision=exact_mode, preferred_element_type=jnp.float32)


def bits_of(size):
    return [1 << bit for bit in range(size.bit_length() - 1)]


def stream_sum(value, work=(), inputs=()):
    made = []
    if work:
        value, inputs = tie(value, inputs)
    for k, mask in enumerate([0] + bits_of(lax.axis_size("img"))):
        other = swap(value, "img", mask) if mask else swap(value, "crop", 1)
        if k < len(work):
            made.append(work[k](*inputs, *made[-1:]))
            value, other, inputs, made[-1] = tie(value, other, inputs, made[-1])
        value = value + other
    return value, made


def quarters(blocks):
    cuts = [blocks * i // 4 for i in range(5)]
    return [(low, high - low) for low, high in zip(cuts, cuts[1:])]


def pick(value, index, axis):
    return lax.dynamic_index_in_dim(value, index, axis, keepdims=False)


def slab_rows(width, devices):
    return -(-(width // devices) // 8) * 8


def slab_offset(index, width, devices):
    share = width // devices
    return 2 * share * (index // 2) + (index % 2) * (2 * share - slab_rows(width, devices))


def slab_part(devices, width, height, place_ref, left_ref, right_ref):
    step = pl.program_id(0)
    half = devices // 4
    apart = jnp.where(step < half, 2 * step, 2 * (step - half) + 1)
    index = 2 * (apart ^ place_ref[1]) + place_ref[0]
    offset = slab_offset(index, width, devices)
    base = jnp.minimum(offset // 128, left_ref.shape[1] // 128 - 3) * 128
    wide = left_ref[:, pl.ds(pl.multiple_of(base, 128), 384)].astype(jnp.float32)
    shift = offset - base
    moved = pltpu.roll(wide, jnp.where(shift == 0, 0, 384 - shift), 1)[:, :height]
    return lax.dot_general(
        moved.astype(jnp.bfloat16),
        right_ref[...],
        (((0,), (0,)), ((), ())),
        preferred_element_type=jnp.float32,
    )


def far_kernel(devices, width, height, low, place_ref, left_ref, right_ref, *refs):
    acc = slab_part(devices, width, height, place_ref, left_ref, right_ref)
    if low:
        refs[0][0] = acc[:, :low]
    refs[-1][0] = acc[:, low:]


def near_kernel(devices, width, height, low, place_ref, left_ref, right_ref, *refs):
    held = refs[-1]
    keep_x, send_x, keep_y, send_y = refs[-5:-1]
    acc = slab_part(devices, width, height, place_ref, left_ref, right_ref)
    step = pl.program_id(0)
    if low:
        low_in, high_in, keep_low, send_low = refs[:4]
        total = acc[:, :low] + low_in[0]

        @pl.when(step < devices // 4)
        def _():
            keep_low[0] = total

        @pl.when(step >= devices // 4)
        def _():
            send_low[0] = total

    else:
        high_in = refs[0]
    held[...] = acc[:, low:] + high_in[0]
    rows = height // 8
    bits = (place_ref[2], place_ref[3])
    for half, keep, send in ((0, keep_x, send_x), (1, keep_y, send_y)):
        first, second = bits[half], bits[1 - half]
        for other, ref in ((0, keep), (1, send)):
            for last in range(2):
                block = 4 * half + 2 * (first ^ other) + (second ^ last)
                ref[last, 0] = held[pl.ds(pl.multiple_of(block * rows, rows), rows), :]


def slab_specs(devices, rows, height, low):
    sides = [pl.BlockSpec((rows, WIDE), lambda t, c: (0, 0))] * 2
    widths = [low, WIDE - low] if low else [WIDE]
    parts = [pl.BlockSpec((1, height, n), lambda t, c: (t, 0, 0)) for n in widths]
    shapes = [jax.ShapeDtypeStruct((devices // 2, height, n), jnp.float32) for n in widths]
    return sides, parts, shapes


def far_product(place, left, right, devices, low):
    rows, width = left.shape
    height = slab_rows(width, devices)
    sides, parts, shapes = slab_specs(devices, rows, height, low)
    return pl.pallas_call(
        functools.partial(far_kernel, devices, width, height, low),
        grid_spec=pltpu.PrefetchScalarGridSpec(
            num_scalar_prefetch=1, grid=(devices // 2,), in_specs=sides, out_specs=parts
        ),
        out_shape=shapes,
        compiler_params=pltpu.CompilerParams(vmem_limit_bytes=40 * 1024 * 1024),
        cost_estimate=cost(9),
        name="far_product",
    )(place, left, right)


def near_product(place, left, right, devices, low, arrived):
    rows, width = left.shape
    height = slab_rows(width, devices)
    sides, parts, _ = slab_specs(devices, rows, height, low)
    chips, half = devices // 2, devices // 4
    high = WIDE - low
    piece = pl.BlockSpec((2, 1, height // 8, high), lambda t, c: (0, t, 0, 0))
    out_specs = [piece] * 4
    out_shape = [jax.ShapeDtypeStruct((2, chips, height // 8, high), jnp.float32)] * 4
    if low:
        out_specs = [
            pl.BlockSpec((1, height, low), lambda t, c: (jnp.minimum(t, half - 1), 0, 0)),
            pl.BlockSpec((1, height, low), lambda t, c: (jnp.maximum(t - half, 0), 0, 0)),
        ] + out_specs
        out_shape = [jax.ShapeDtypeStruct((half, height, low), jnp.float32)] * 2 + out_shape
    return pl.pallas_call(
        functools.partial(near_kernel, devices, width, height, low),
        grid_spec=pltpu.PrefetchScalarGridSpec(
            num_scalar_prefetch=1,
            grid=(chips,),
            in_specs=sides + parts,
            out_specs=out_specs,
            scratch_shapes=[pltpu.VMEM((height, high), jnp.float32)],
        ),
        out_shape=out_shape,
        compiler_params=pltpu.CompilerParams(vmem_limit_bytes=48 * 1024 * 1024),
        cost_estimate=cost(13),
        name="near_product",
    )(place, left, right, *arrived)


UNIT_ROWS = 704


def unit_start(index, share, unit, gw, rows):
    return jnp.minimum((share * index // unit) * gw, rows - UNIT_ROWS)


def unit_part(devices, size, gw, place_ref, units_ref):
    step = pl.program_id(0)
    half = devices // 4
    apart = jnp.where(step < half, 2 * step, 2 * (step - half) + 1)
    index = 2 * (apart ^ place_ref[1]) + place_ref[0]
    start = unit_start(index, size // devices, gw * gw * PACK, gw, units_ref.shape[0])
    return pl.multiple_of(start, 8)


def far_units_kernel(devices, size, gw, place_ref, units_ref, out_ref):
    start = unit_part(devices, size, gw, place_ref, units_ref)
    out_ref[0] = units_ref[pl.ds(start, UNIT_ROWS), :]


def near_units_kernel(devices, size, gw, place_ref, units_ref, in_ref, *refs):
    keep_x, send_x, keep_y, send_y = refs
    start = unit_part(devices, size, gw, place_ref, units_ref)
    rows = UNIT_ROWS // 8
    bits = (place_ref[2], place_ref[3])
    for half, keep, send in ((0, keep_x, send_x), (1, keep_y, send_y)):
        first, second = bits[half], bits[1 - half]
        for other, ref in ((0, keep), (1, send)):
            for last in range(2):
                block = 4 * half + 2 * (first ^ other) + (second ^ last)
                skip = pl.multiple_of(block * rows, 8)
                ref[last, 0] = (
                    units_ref[pl.ds(pl.multiple_of(start + skip, 8), rows), :]
                    + in_ref[0, pl.ds(skip, rows), :]
                )


def unit_call(place, units, devices, size, gw, arrived=None):
    rows = units.shape[0]
    chips = devices // 2
    part = pl.BlockSpec((1, UNIT_ROWS, 256), lambda t, c: (t, 0, 0))
    if arrived is None:
        body, extra = far_units_kernel, ()
        out_specs, out_shape = part, jax.ShapeDtypeStruct((chips, UNIT_ROWS, 256), jnp.float32)
    else:
        body, extra = near_units_kernel, (arrived,)
        piece = (2, chips, UNIT_ROWS // 8, 256)
        out_specs = [pl.BlockSpec((2, 1) + piece[2:], lambda t, c: (0, t, 0, 0))] * 4
        out_shape = [jax.ShapeDtypeStruct(piece, jnp.float32)] * 4
    return pl.pallas_call(
        functools.partial(body, devices, size, gw),
        grid_spec=pltpu.PrefetchScalarGridSpec(
            num_scalar_prefetch=1,
            grid=(chips,),
            in_specs=[pl.BlockSpec((rows, 256), lambda t, c: (0, 0))] + [part] * len(extra),
            out_specs=out_specs,
        ),
        out_shape=out_shape,
        compiler_params=pltpu.CompilerParams(vmem_limit_bytes=32 * 1024 * 1024),
        cost_estimate=cost(3),
        name="units",
    )(place, units, *extra)


def share_kernel(left_ref, right_ref, out_ref):
    out_ref[...] = lax.dot_general(
        left_ref[...].astype(jnp.bfloat16),
        right_ref[...].astype(jnp.bfloat16),
        (((0,), (0,)), ((), ())),
        preferred_element_type=jnp.float32,
    )


def share_product(left, right):
    return pl.pallas_call(
        share_kernel,
        out_shape=jax.ShapeDtypeStruct((left.shape[1], right.shape[1]), jnp.float32),
        compiler_params=pltpu.CompilerParams(vmem_limit_bytes=32 * 1024 * 1024),
        cost_estimate=cost(3),
        name="share_product",
    )(left, right)


def crop_bits():
    crop = lax.axis_index("crop")
    return (crop & 1, crop >> 1)


def crop_halves(value):
    lead, rows, cols = value.shape
    whole = value.reshape(lead, 2, 2, 2, rows // 8, cols)
    return [whole[:, 0], whole[:, 1]]


CROP_ORDER = ((0, 1), (1, 0))


def crop_send(parts, step):
    bits = crop_bits()
    return [
        swap(pick(part, 1 - bits[order[step]], 1), "crop", 1 << order[step])
        for part, order in zip(parts, CROP_ORDER)
    ]


def crop_add(parts, arrived, step):
    bits = crop_bits()
    return [
        pick(part, bits[order[step]], 1) + other
        for part, other, order in zip(parts, arrived, CROP_ORDER)
    ]


def crop_fetch(parts, step):
    return [swap(part, "crop", 1 << order[1 - step]) for part, order in zip(parts, CROP_ORDER)]


def crop_join(parts, arrived, step):
    bits = crop_bits()
    joined = []
    for part, other, order in zip(parts, arrived, CROP_ORDER):
        upper = bits[order[1 - step]] == 1
        joined.append(
            jnp.stack([jnp.where(upper, other, part), jnp.where(upper, part, other)], axis=1)
        )
    return joined


def crop_whole(parts):
    both = jnp.stack(parts, axis=1)
    return both.reshape(both.shape[0], -1, both.shape[-1])


def chip_swap(value, step):
    return swap(value, "img", 2 << step)


class LowChain:
    def __init__(self, keep, send):
        self.keep, self.away = keep, [send]
        self.chips = keep.shape[0].bit_length()
        self.steps, self.step = self.chips + 4, 0

    def send(self):
        if self.step < self.chips:
            return [chip_swap(v, self.step) for v in self.away]
        if self.step < self.chips + 2:
            return crop_send(self.keep, self.step - self.chips)
        return crop_fetch(self.keep, self.step - self.chips - 2)

    def take(self, arrived):
        step, chips = self.step, self.chips
        if step < chips:
            total = self.keep + arrived[0]
            half = total.shape[0] // 2
            self.keep, self.away = total[:half], [total[half:]]
            if step == chips - 1:
                self.keep, self.away = crop_halves(total), []
        elif step < chips + 2:
            self.keep = crop_add(self.keep, arrived, step - chips)
        else:
            self.keep = crop_join(self.keep, arrived, step - chips - 2)
        self.step += 1

    def result(self):
        return crop_whole(self.keep)[0]


class HighChain:
    def __init__(self, keep_x, send_x, keep_y, send_y):
        self.keep, self.away = [keep_x, keep_y], [send_x, send_y]
        self.chips = keep_x.shape[1].bit_length() - 1
        self.steps, self.step = self.chips + 4, 0

    def send(self):
        step = self.step
        if step < 2:
            return [swap(v, "crop", 1 << order[step]) for v, order in zip(self.away, CROP_ORDER)]
        if step < self.chips + 2:
            return [chip_swap(v, step - 2) for v in self.away]
        return crop_fetch(self.keep, step - self.chips - 2)

    def take(self, arrived):
        step, chips = self.step, self.chips
        if step < chips + 2:
            total = [keep + other for keep, other in zip(self.keep, arrived)]
            if step == 0:
                self.keep, self.away = [v[0] for v in total], [v[1] for v in total]
            else:
                if step == 1:
                    total = [jnp.concatenate(total, axis=1)]
                half = total[0].shape[0] // 2
                self.keep, self.away = [total[0][:half]], [total[0][half:]]
            if step == chips + 1:
                rows = total[0].shape[1] // 2
                self.keep, self.away = [total[0][:, :rows], total[0][:, rows:]], []
        else:
            self.keep = crop_join(self.keep, arrived, step - chips - 2)
        self.step += 1

    def result(self):
        return crop_whole(self.keep)[0]


class CropSum:
    steps = 4

    def __init__(self, value):
        self.away = []
        self.keep = crop_halves(value[None])
        self.step = 0

    def send(self):
        if self.step < 2:
            return crop_send(self.keep, self.step)
        return crop_fetch(self.keep, self.step - 2)

    def take(self, arrived):
        if self.step < 2:
            self.keep = crop_add(self.keep, arrived, self.step)
        else:
            self.keep = crop_join(self.keep, arrived, self.step - 2)
        self.step += 1

    def result(self):
        return crop_whole(self.keep)[0]


class Flow:
    def __init__(self):
        self.sent = {}

    def begin(self, chain):
        self.sent[id(chain)] = chain.send()

    def advance(self, chain, beside):
        arrived, beside = tie(self.sent[id(chain)], beside)
        chain.take(arrived)
        (chain.keep, chain.away), beside = tie((chain.keep, chain.away), beside)
        if chain.step < chain.steps:
            self.begin(chain)
        return beside


def shards(
    pixels,
    counts,
    slot_order,
    w_in,
    kernel,
    w_red,
    b_red,
    w_exp,
    b_exp,
    w_out,
    gain_one,
    shift_one,
    gain_two,
    shift_two,
    gain_three,
    shift_three,
    protos,
):
    row_count = pixels.shape[2]
    width = pixels.shape[3]
    proto_count = protos.shape[1]
    squeeze = w_red.shape[1]
    seg_count = row_count // (SMALL_SIDE * SMALL_SIDE)
    slot_total = slot_order.shape[1]
    devices = lax.axis_size("img")
    img_index = lax.axis_index("img")
    crop_index = lax.axis_index("crop")
    core = img_index % 2
    fast = width % devices == 0 and (2 * width // devices) % 8 == 0
    is_global = crop_index < 2
    glob = is_global.astype(jnp.int32).reshape(1)
    stream_rows = 2.0 * devices * row_count
    couple_number = 2.0 * devices * (IMG_DEV + slot_total)
    inputs = pixels.reshape(row_count, width)
    row_ids = jnp.arange(row_count, dtype=jnp.int32)
    side = jnp.where(is_global, SIDE, SMALL_SIDE)
    seg_of_row = row_ids // (side * side)
    across = row_ids % side
    down = (row_ids // side) % side
    masks = jnp.stack([across > 0, across < side - 1, down > 0, down < side - 1])
    masks = jnp.broadcast_to(masks.astype(jnp.float32)[:, :, None], (4, row_count, 128))
    member = (seg_of_row[None, :] == jnp.arange(seg_count, dtype=jnp.int32)[:, None]).astype(
        jnp.float32
    )
    member_rows = member.T
    crop_pixels = jnp.where(is_global, float(SIDE * SIDE), float(SMALL_SIDE * SMALL_SIDE))
    block_width = PACK * kernel.shape[2]
    block_count = kernel.shape[1] // PACK
    sides = (SIDE, SMALL_SIDE)

    def norm_rows(local_sums, work=(), inputs=()):
        sums, made = stream_sum(local_sums, work, inputs)
        average = sums[0] / stream_rows
        inv = lax.rsqrt(sums[1] / stream_rows - average * average + norm_epsilon)
        return average, inv, made

    def back_rows(local_sums, gain, inv, work=(), inputs=()):
        sums, made = stream_sum(local_sums, work, inputs)
        return sums, gain * inv, sums[0] / stream_rows, sums[1] / stream_rows, made

    hidden_one = jnp.dot(inputs, w_in, preferred_element_type=jnp.float32)
    sums = jnp.stack([jnp.sum(hidden_one, axis=0), jnp.sum(hidden_one * hidden_one, axis=0)])
    mean_one, inv_one, packed = norm_rows(
        sums,
        [functools.partial(pack_blocks, low, count) for low, count in quarters(block_count)],
        (kernel,),
    )
    packed = packed[-1]
    zero_row = jnp.zeros((width,), jnp.float32)
    scale_one = gain_one * inv_one
    par = jnp.stack(
        [scale_one, shift_one - mean_one * scale_one, inv_one, -mean_one * inv_one] + [zero_row] * 4
    )
    hidden_two, sums = conv_fwd(glob, hidden_one, par, masks, packed, block_width, sides)
    mean_two, inv_two, _ = norm_rows(sums[:2])
    centred_two = (hidden_two - mean_two) * inv_two
    pre_two = centred_two * gain_two + shift_two
    act_two = smooth_gate(pre_two)
    red_float = w_red.astype(jnp.float32)
    exp_float = w_exp.astype(jnp.float32)
    pooled = exact_dot(member, act_two) / crop_pixels
    reduce_pre = exact_dot(pooled, red_float) + b_red
    reduced = smooth_gate(reduce_pre)
    gate_values = jax.nn.sigmoid(exact_dot(reduced, exp_float) + b_exp)
    gate_rows = exact_dot(member_rows, gate_values)
    excited = (act_two * gate_rows).astype(jnp.bfloat16)
    hidden_three = jnp.dot(excited, w_out, preferred_element_type=jnp.float32)
    sums = jnp.stack([jnp.sum(hidden_three, axis=0), jnp.sum(hidden_three * hidden_three, axis=0)])
    mean_three, inv_three, _ = norm_rows(sums)
    centred_three = (hidden_three - mean_three) * inv_three
    summed_in = inputs.astype(jnp.float32) + centred_three * gain_three + shift_three
    output = smooth_gate(summed_in)
    pooled_out = exact_dot(member, output) / crop_pixels
    length_inv = lax.rsqrt(jnp.sum(pooled_out * pooled_out, axis=1, keepdims=True) + length_epsilon)
    unit_wide = pooled_out * length_inv
    unit_rows = unit_wide.astype(jnp.bfloat16)
    match_matrix = jnp.dot(unit_rows, protos, preferred_element_type=jnp.float32)

    every = match_matrix[:IMG_DEV]
    for mask in bits_of(devices):
        every = jnp.concatenate([every, swap(every, "img", mask)], axis=0)
    plan_rows = jnp.exp(every / sharpness)
    for sweep_index in range(3):
        plan_rows = plan_rows / jnp.sum(plan_rows, axis=0, keepdims=True)
        plan_rows = plan_rows / jnp.sum(plan_rows, axis=1, keepdims=True)
    codes = plan_rows[:IMG_DEV]
    partner = lax.ppermute(codes, "crop", [(0, 1), (1, 0)])
    both_codes = lax.ppermute(codes, "crop", [(0, 2), (1, 3)]) + lax.ppermute(
        codes, "crop", [(0, 3), (1, 2)]
    )
    wide_target = jnp.concatenate(
        [partner, jnp.zeros((seg_count - IMG_DEV, proto_count), jnp.float32)], axis=0
    )
    ends = [jnp.sum(counts[0, : i + 1]) for i in range(IMG_DEV)]
    first_slot = jnp.maximum(crop_index - 2, 0) * seg_count
    order_here = lax.dynamic_slice_in_dim(slot_order[0], first_slot, seg_count)
    owner = sum((order_here >= end).astype(jnp.int32) for end in ends)
    narrow_target = jnp.zeros((seg_count, proto_count), jnp.float32)
    for i in range(IMG_DEV):
        narrow_target = jnp.where(owner[:, None] == i, both_codes[i : i + 1], narrow_target)
    target = jnp.where(is_global, wide_target, narrow_target)
    sharpened = match_matrix / sharpening_divisor
    shifted = sharpened - jnp.max(sharpened, axis=1, keepdims=True)
    log_probs = shifted - jnp.log(jnp.sum(jnp.exp(shifted), axis=1, keepdims=True))
    loss_here = -jnp.sum(target * log_probs) / couple_number
    scores_wide = (jnp.exp(log_probs) * jnp.sum(target, axis=1, keepdims=True) - target) / (
        sharpening_divisor * couple_number
    )
    grad_scores = scores_wide.astype(jnp.bfloat16)

    grad_unit = jnp.einsum("sk,wk->sw", grad_scores, protos, preferred_element_type=jnp.float32)
    inner_term = jnp.sum(pooled_out * grad_unit, axis=1, keepdims=True)
    grad_pooled_out = (
        length_inv * grad_unit - pooled_out * length_inv * length_inv * length_inv * inner_term
    )
    grad_output = exact_dot(member_rows, grad_pooled_out / crop_pixels)
    grad_summed = grad_output * smooth_slope(summed_in)
    sums_three, scale_three, first, second, _ = back_rows(
        jnp.stack([jnp.sum(grad_summed, axis=0), jnp.sum(grad_summed * centred_three, axis=0)]),
        gain_three,
        inv_three,
    )
    grad_three_low = (scale_three * (grad_summed - first - centred_three * second)).astype(
        jnp.bfloat16
    )
    if fast:
        share = width // devices
        height = slab_rows(width, devices)
        chip = img_index // 2
        near = jnp.stack([core, chip, crop_index & 1, crop_index >> 1]).astype(jnp.int32)
        far = jnp.stack([1 - core, chip, crop_index & 1, crop_index >> 1]).astype(jnp.int32)

        def kept(value):
            skip = core * (value.shape[0] - share)
            return lax.dynamic_slice_in_dim(value, skip, share, axis=0)

        seen_scores = lax.all_gather(
            jnp.concatenate(
                [
                    unit_wide,
                    jnp.zeros((seg_count, WIDE - width), jnp.float32),
                    scores_wide,
                    jnp.zeros((seg_count, WIDE_PROTOS - proto_count), jnp.float32),
                ],
                axis=1,
            ),
            "img",
            tiled=True,
        )

    grad_excited = jnp.einsum(
        "rv,wv->rw", grad_three_low, w_out, preferred_element_type=jnp.float32
    )
    flow = Flow()
    if fast:
        grad_excited, seen_scores = tie(grad_excited, seen_scores)
        protos_sum = CropSum(
            share_product(
                lax.dynamic_slice_in_dim(seen_scores, img_index * share, height, axis=1),
                seen_scores[:, WIDE:],
            )
        )
        (protos_sum.keep, grad_excited) = tie(protos_sum.keep, grad_excited)
        flow.begin(protos_sum)
    grad_gate = exact_dot(member, grad_excited * act_two)
    grad_gate_pre = grad_gate * gate_values * (1.0 - gate_values)
    grad_reduce_pre = exact_dot(grad_gate_pre, exp_float.T) * smooth_slope(reduce_pre)
    grad_pooled = exact_dot(grad_reduce_pre, red_float.T)
    grad_act_two = grad_excited * gate_rows + exact_dot(member_rows, grad_pooled / crop_pixels)
    grad_pre_two = grad_act_two * smooth_slope(pre_two)
    bias_row = jnp.concatenate(
        [
            jnp.sum(grad_reduce_pre, axis=0),
            loss_here.reshape(1),
            jnp.zeros((width - squeeze - 1,), jnp.float32),
        ]
    )
    local_two = jnp.stack(
        [
            jnp.sum(grad_pre_two, axis=0),
            jnp.sum(grad_pre_two * centred_two, axis=0),
            jnp.sum(grad_gate_pre, axis=0),
            bias_row,
        ]
    )
    work = []
    if fast:
        seen_gates = lax.all_gather(
            jnp.concatenate([pooled, reduced, grad_reduce_pre, grad_gate_pre], axis=1),
            "img",
            tiled=True,
        )

        def out_far(left, right):
            return far_product(far, left, right, devices, 0)

        def proto_step(left, right, arrived):
            return flow.advance(protos_sum, arrived)

        work = [out_far, proto_step]
    sums_two, scale_two, first, second, made = back_rows(
        local_two, gain_two, inv_two, work, (excited, grad_three_low)
    )
    if fast:
        arrived = [swap(v, "img", 1) for v in made[-1]]
    grad_two_low = (scale_two * (grad_pre_two - first - centred_two * second)).astype(jnp.bfloat16)
    if fast:
        grad_two_low, arrived = tie(grad_two_low, arrived)
        arrived = flow.advance(protos_sum, arrived)
        outs = HighChain(*near_product(near, excited, grad_three_low, devices, 0, arrived))
        outs.keep, outs.away, grad_two_low = tie(outs.keep, outs.away, grad_two_low)
        flow.begin(outs)
    grad_pre_one, sums = conv_dgrad(
        glob, grad_two_low, hidden_one, par, masks, packed, block_width, sides
    )

    def some_wgrad(low, count, grad, done=None):
        return conv_wgrad(
            glob, grad, hidden_one, par, masks, low, count, block_count, block_width, sides, done
        )

    cut = block_count // 2
    steps = [
        functools.partial(some_wgrad, 0, cut),
        functools.partial(some_wgrad, cut, block_count - cut),
    ]
    early = []
    if fast:
        grad_two_low, grad_pre_one, sums = tie(grad_two_low, grad_pre_one, sums)
        units = steps[0](grad_two_low)
        units = flow.advance(outs, units)
        units, sums = tie(units, sums)

        def my_columns(value):
            count = value.shape[1] // devices
            return lax.dynamic_slice_in_dim(value, img_index * count, count, axis=1)

        def shares_of(seen):
            seen = flow.advance(protos_sum, seen)
            return (
                exact_dot(
                    my_columns(seen[:, :width]).T, seen[:, width + squeeze : width + 2 * squeeze]
                ),
                exact_dot(my_columns(seen[:, width : width + squeeze]).T, seen[:, width + 2 * squeeze :]),
            )

        early = [shares_of]
    sums_one, scale_one, first, second, made = back_rows(
        sums[:2], gain_one, inv_one, early, (seen_gates,) if fast else ()
    )
    centred_one = (hidden_one - mean_one) * inv_one
    grad_one_low = (scale_one * (grad_pre_one - first - centred_one * second)).astype(jnp.bfloat16)
    if fast:
        share_red, share_exp = made[-1]
        share_red, share_exp = lax.psum((share_red, share_exp), "crop")
        grad_one_low = flow.advance(outs, grad_one_low)
        arrived = far_product(far, inputs, grad_one_low, devices, LOW_COLUMNS)
        arrived = [swap(v, "img", 1) for v in arrived]
        arrived = flow.advance(protos_sum, arrived)
        arrived = flow.advance(outs, arrived)
        parts = near_product(near, inputs, grad_one_low, devices, LOW_COLUMNS, arrived)
        ins = HighChain(*parts)
        units, grad_two_low, grad_one_low, ins.keep, ins.away = tie(
            units, grad_two_low, grad_one_low, ins.keep, ins.away
        )
        flow.begin(ins)
        units = steps[1](grad_two_low, units)
        units = flow.advance(outs, units)
        gw = kernel.shape[2]
        unit_size = gw * gw * PACK
        units = units.reshape(-1, 256)
        swapped = unit_call(far, units, devices, kernel.size, gw)
        swapped, units, grad_one_low = tie(swapped, units, grad_one_low)
        swapped, units, grad_one_low = flow.advance(ins, (swapped, units, grad_one_low))
        swapped = swap(swapped, "img", 1)
        grad_inputs = (
            jnp.einsum("rv,wv->rw", grad_one_low, w_in, preferred_element_type=jnp.float32)
            + grad_summed
        )
        swapped, grad_inputs = tie(swapped, grad_inputs)
        gks = HighChain(*unit_call(near, units, devices, kernel.size, gw, swapped))
        flow.begin(gks)
        chains = [ins, outs, gks]
        last = None
        for chain in (chains[index] for index in TAIL):
            arrived = flow.sent[id(chain)]
            if last is not None:
                arrived, _ = tie(arrived, (last.keep, last.away))
            chain.take(arrived)
            if chain.step < chain.steps:
                flow.begin(chain)
            last = chain
    else:
        made = None
        for step in steps:
            made = step(grad_two_low, made)
        small_kernel = made
        grad_inputs = (
            jnp.einsum("rv,wv->rw", grad_one_low, w_in, preferred_element_type=jnp.float32)
            + grad_summed
        )

    last = jnp.concatenate([sums_one, sums_two, sums_three], axis=0)
    last = last + swap(last, "crop", 2)
    tail = (
        last[5, :squeeze],
        last[4],
        last[1],
        last[0],
        last[3],
        last[2],
        last[7],
        last[6],
    )
    loss_total = last[5, squeeze]

    if fast:
        flat_in = kept(ins.result()[:, :width]).reshape(-1)
        flat_out = kept(outs.result()[:, :width]).reshape(-1)
        flat_protos = protos_sum.result()[:share, :proto_count].reshape(-1)
        flat_red = share_red.reshape(-1)
        flat_exp = share_exp.reshape(-1)
        total = kernel.size // devices
        first_unit = total * img_index // unit_size
        start = unit_start(img_index, total, unit_size, gw, units.size // 256)
        span = -(-total // unit_size) + 1
        mine = jnp.pad(gks.result(), ((0, gw), (0, 0)))
        mine = lax.dynamic_slice_in_dim(mine, first_unit * gw - start, span * gw, axis=0)
        mine = mine[:, : PACK * gw].reshape(span, gw, PACK, gw).transpose(0, 2, 1, 3).reshape(-1)
        flat_kernel = lax.dynamic_slice_in_dim(mine, total * img_index - unit_size * first_unit, total)
        shares = (flat_in, flat_kernel, flat_red, flat_exp, flat_out, flat_protos)
    else:
        gw = kernel.shape[2]
        grads = (
            jnp.einsum("rw,rv->wv", inputs, grad_one_low, preferred_element_type=jnp.float32),
            small_kernel[..., : PACK * gw]
            .reshape(9, block_count, gw, PACK, gw)
            .transpose(0, 1, 3, 2, 4),
            exact_dot(pooled.T, grad_reduce_pre),
            exact_dot(reduced.T, grad_gate_pre),
            jnp.einsum("rw,rv->wv", excited, grad_three_low, preferred_element_type=jnp.float32),
            jnp.einsum("sw,sk->wk", unit_rows, grad_scores, preferred_element_type=jnp.float32),
        )
        shares = tuple(
            lax.psum(
                lax.psum_scatter(grad.reshape(-1), "img", scatter_dimension=0, tiled=True), "crop"
            )
            for grad in grads
        )
    return (
        loss_total,
        output.astype(jnp.bfloat16).reshape(pixels.shape),
        grad_inputs.reshape(pixels.shape),
        *shares,
        *tail,
    )


def solution(mesh):
    return jax.shard_map(
        shards,
        mesh=mesh,
        in_specs=(P("crop", "img", None, None), P("img", None), P("img", None)) + (P(),) * 14,
        out_specs=(P(), P("crop", "img", None, None), P("crop", "img", None, None))
        + (P("img"),) * 6
        + (P(),) * 8,
        check_vma=False,
    )
```

time: 933 us -> 666 us (0.71)
  local copies, waits for them, and re-layouts: 186 us -> 57.3 us
  waiting for transfers between devices: 270 us -> 193 us
  starting transfers between devices: 111 us -> 69.9 us
  other arithmetic: 104 us -> 67 us
  Pallas kernels: 123 us -> 145 us
    ppermute x76 -> x28, waiting for transfers between devices: 233 us -> 60.4 us  [swap(): return lax.ppermute(value, axis, pairs)]
    ppermute x0 -> x41, waiting for transfers between devices: none -> 130 us  [swap(): return plain(lax.ppermute(plain(value), axis, pairs))]
    ppermute x76 -> x28, starting transfers between devices: 103 us -> 20.1 us  [swap(): return lax.ppermute(value, axis, pairs)]
    unnamed x125 -> x130, local copies, waits for them, and re-layouts: 59.2 us -> 16.3 us
    ppermute x0 -> x41, starting transfers between devices: none -> 41.2 us  [swap(): return plain(lax.ppermute(plain(value), axis, pairs))]
    psum x1, waiting for transfers between devices: 34.6 us -> 0.01 us  [shards(): share_red, share_exp = lax.psum((share_red, share_exp), 'crop')]
    add x52 -> x46, other arithmetic: 45 us -> 13.4 us  [the longest x18 9.91 us: take(): total = [keep + other for keep, other in zip(self.keep, arrived)]]
    ppermute x4 -> x0, local copies, waits for them, and re-layouts: 26 us -> none  [swap(): return lax.ppermute(value, axis, pairs)]
  transfers between devices with their start and end apart: 83 -> 75, of which waited for: 55 -> 42; matrix products, arithmetic and copies ran while one was open for 31% -> 20% of each run, Pallas kernels for 10% -> 15%
where the time goes in v2:
time: 666 us; the launch traced here: 657 us
  waiting for transfers between devices  193 us (29%)
  Pallas kernels  145 us (22%)
  matrix products  108 us (16%)
  starting transfers between devices  69.9 us (10%)
  other arithmetic  67 us (10%)
  local copies, waits for them, and re-layouts  57.3 us (9%)
  between operations  16.6 us (2%)
    ppermute x41, waiting for transfers between devices, swap(): return plain(lax.ppermute(plain(value), axis, pairs))  130 us
    ppermute x28, waiting for transfers between devices, swap(): return lax.ppermute(value, axis, pairs)  60.4 us
    dot_general x12, matrix products, exact_dot(): jnp.dot(left, right, precision=exact_mode, preferred_element_type=jnp.flo...  50.5 us
    ppermute x41, starting transfers between devices, swap(): return plain(lax.ppermute(plain(value), axis, pairs))  41.2 us
    pallas_call x2, Pallas kernels, conv_wgrad(): pl.pallas_call(functools.partial(conv_kernel, wgrad_step, rows + 2 * EDGE...  35 us
    pallas_call x2, Pallas kernels, near_product(): pl.pallas_call(functools.partial(near_kernel, devices, width, height, low...  25.7 us
    pallas_call x1, Pallas kernels, conv_fwd(): pl.pallas_call(functools.partial(conv_kernel, fwd_step, rows + 2 * EDGE,...  23.6 us
    pallas_call x1, Pallas kernels, conv_dgrad(): pl.pallas_call(functools.partial(conv_kernel, dgrad_step, rows + 2 * EDGE...  23 us
  transfers between devices with their start and end apart: 75, of which 42 were waited for; matrix products, arithmetic and copies ran while one was open for 20% of the time, Pallas kernels for 15%

profile of v2, /device:TPU:0, one launch (start us, length us, event | category | flops | bytes accessed | tf_op | source)
XLA Modules:
  0.0 656.8 jit_solution(15463691328646994499)
XLA Ops:
  7.2 12.0 %fusion.78 = (f32[2016]{0:T(1024)S(1)}, f32[2016]{0:T(1024)S(1)}, f32[784,2016]{1,0:T(8,128)}) fusion(bf16[2016,2016]{1,0:T(8,128)(2,1)} %param.20, bf16[1,1,784,2016]{3,2,1,0:T(8,128)(2,1)} %param.17), kind=kOutput, calls=%fused_computation.255 | convolution fusion | flops 6377490944 | bytes 17627904 | tf_op jit(solution)/shard_map/dot_general | solution.py:876
  43.9 23.6 %conv_fwd.1 = (f32[784,2016]{1,0:T(8,128)}, f32[8,2016]{1,0:T(8,128)}) custom-call(s32[1]{0:T(128)} %bitcast.4.glob_ref, f32[784,2016]{1,0:T(8,128)} %get-tuple-element.441.refs_0_.refs_1_.refs_2_.refs_3_.refs_4_.refs_5_, f32[784,2016]{1,0:T(8,128)} %get-tuple-element.441.refs_0_.refs_1_.refs_2_.refs_3_.refs_4_.refs_5_, ...), custom_call_target="tpu_custom_call" | custom-call | flops 20000000 | bytes 20000 | tf_op jit(solution)/shard_map/conv_fwd/pallas_call | solution.py:300
  91.5 6.6 %multiply_convert_fusion.3 = (bf16[784,2016]{1,0:T(8,128)(2,1)S(1)}, f32[784,2016]{1,0:T(8,128)}) fusion(f32[2016]{0:T(1024)S(1)} %copy-done.53, f32[2016]{0:T(1024)S(1)} %copy-done.47, f32[2016]{0:T(1024)S(1)} %bitcast.260, f32[784,2016]{1,0:T(8,128)S(1)} %copy-done.15, f32[2016]{0:T(1024)S(1)} %bitcast.280, f32[16,2016]{1,0:T(8,128)S(1)} %fusion.7, ...), kind=kOutput, calls=%fused_computation.14 | convolution fusion | flops 319282432 | bytes 15969856 | tf_op jit(solution)/shard_map/dot_general | solution.py:422
  98.2 10.5 %fusion.77 = (f32[2016]{0:T(1024)S(1)}, f32[2016]{0:T(1024)S(1)}, f32[784,2016]{1,0:T(8,128)S(1)}) fusion(bf16[784,2016]{1,0:T(8,128)(2,1)S(1)} %get-tuple-element.199.left_ref, bf16[2016,2016]{1,0:T(8,128)(2,1)} %param.26), kind=kOutput, calls=%fused_computation.254 | convolution fusion | flops 6377490944 | bytes 17627904 | tf_op jit(solution)/shard_map/dot_general | solution.py:902
  143.6 11.2 %collective-permute-done.14 = f32[16,3000]{1,0:T(8,128)S(1)} collective-permute-done((f32[16,3000]{1,0:T(8,128)S(1)}, f32[16,3000]{1,0:T(8,128)S(1)}, u32[]{:S(2)}, u32[]{:S(2)}) %collective-permute-start.14) | collective-permute-done | bytes 192032 | tf_op jit(solution)/shard_map/ppermute | solution.py:404
  175.9 10.9 %fusion.76 = (f32[2016]{0:T(1024)S(1)}, f32[2016]{0:T(1024)S(1)}, f32[784,2016]{1,0:T(8,128)}) fusion(f32[2016]{0:T(1024)S(1)} %bitcast.243, f32[784,2016]{1,0:T(8,128)} %copy-done.12, f32[2016]{0:T(1024)S(1)} %bitcast.255, f32[2016]{0:T(1024)S(1)} %copy-done.46, f32[2016]{0:T(1024)S(1)} %copy-done.44, bf16[1,1,784,2016]{3,2,1,0:T(8,128)(2,1)} %param.17, ...), kind=kOutput, calls=%fused_computation.253 | convolution fusion | flops 330535744 | bytes 16115140 | tf_op jit(solution)/shard_map/dot_general | solution.py:422
  208.8 11.3 %fusion.91 = f32[784,2016]{1,0:T(8,128)} fusion(bf16[784,2016]{1,0:T(8,128)(2,1)S(1)} %multiply_convert_fusion.2.right_ref, bf16[2016,2016]{1,0:T(8,128)(2,1)} %param.26), kind=kOutput, calls=%fused_computation.265 | convolution fusion | flops 6372753408 | bytes 17611776 | tf_op jit(solution)/shard_map/rv,wv->rw/dot_general | solution.py:986
  238.8 8.3 %fusion.75 = (f32[2016]{0:T(1024)S(1)}, f32[2016]{0:T(1024)S(1)}, f32[784,2016]{1,0:T(8,128)}) fusion(f32[2016]{0:T(1024)S(1)} %bitcast.262, f32[784,2016]{1,0:T(8,128)S(1)} %bitcast.237, f32[2016]{0:T(1024)S(1)} %bitcast.282, f32[2016]{0:T(1024)S(1)} %copy-done.53, f32[2016]{0:T(1024)S(1)} %copy-done.47, f32[16,2016]{1,0:T(8,128)S(1)} %convolution_divide_fusion, ...), kind=kOutput, calls=%fused_computation.252 | convolution fusion | flops 330342208 | bytes 25469248 | tf_op jit(solution)/shard_map/dot_general | solution.py:422
  252.4 9.0 %far_product.2 = f32[4,256,2048]{2,1,0:T(8,128)} custom-call(s32[4]{0:T(128)S(1)} %add_add_fusion.2.place_ref, bf16[784,2016]{1,0:T(8,128)(2,1)S(1)} %copy-done.9, bf16[784,2016]{1,0:T(8,128)(2,1)S(1)} %copy-done.7), custom_call_target="tpu_custom_call" | custom-call | flops 9000000 | bytes 9000 | tf_op jit(solution)/shard_map/far_product/pallas_call | solution.py:527
  274.3 8.2 %multiply_convert_fusion.1.refs_0_.refs_1_.refs_2_ = bf16[784,2016]{1,0:T(8,128)(2,1)} fusion(f32[784,2016]{1,0:T(8,128)} %get-tuple-element.456, f32[784,2016]{1,0:T(8,128)} %get-tuple-element.191, f32[2016]{0:T(1024)S(1)} %bitcast.285, f32[2016]{0:T(1024)S(1)} %bitcast.284, f32[2016]{0:T(1024)S(1)} %mul.340, f32[2016]{0:T(1024)S(1)} %bitcast.264, ...), kind=kLoop, calls=%fused_computation.1 | loop fusion | flops 11063808 | bytes 15845760 | tf_op jit(solution)/shard_map/convert_element_type | solution.py:1041
  282.7 13.0 %near_product.2 = (f32[2,4,32,2048]{3,2,1,0:T(8,128)S(1)}, f32[2,4,32,2048]{3,2,1,0:T(8,128)}, f32[2,4,32,2048]{3,2,1,0:T(8,128)}, f32[2,4,32,2048]{3,2,1,0:T(8,128)}) custom-call(s32[4]{0:T(128)S(1)} %add_add_fusion.1.place_ref, bf16[784,2016]{1,0:T(8,128)(2,1)} %copy-done.8, bf16[784,2016]{1,0:T(8,128)(2,1)} %copy-done.6, ...), custom_call_target="tpu_custom_call" | custom-call | flops 13000000 | bytes 13000 | tf_op jit(solution)/shard_map/near_product/pallas_call | solution.py:554
  300.3 23.0 %conv_dgrad.1 = (f32[784,2016]{1,0:T(8,128)}, f32[8,2016]{1,0:T(8,128)}) custom-call(s32[1]{0:T(128)} %bitcast.4.glob_ref, bf16[784,2016]{1,0:T(8,128)(2,1)} %multiply_convert_fusion.1.refs_0_.refs_1_.refs_2_, bf16[784,2016]{1,0:T(8,128)(2,1)} %multiply_convert_fusion.1.refs_0_.refs_1_.refs_2_, ...), custom_call_target="tpu_custom_call" | custom-call | flops 20000000 | bytes 20000 | tf_op jit(solution)/shard_map/conv_dgrad/pallas_call | solution.py:323
  326.6 16.0 %conv_wgrad.2.refs_10_ = f32[9,9,56,256]{3,2,1,0:T(8,128)} custom-call(s32[2]{0:T(128)} %pad_add_fusion.glob_ref, bf16[784,2016]{1,0:T(8,128)(2,1)} %multiply_convert_fusion.1.refs_0_.refs_1_.refs_2_, bf16[784,2016]{1,0:T(8,128)(2,1)} %multiply_convert_fusion.1.refs_0_.refs_1_.refs_2_, bf16[784,2016]{1,0:T(8,128)(2,1)} %multiply_convert_fusion.1.refs_0_.refs_1_.refs_2_, ...), custom_call_target="tpu_custom_call" | custom-call | flops 8000000 | bytes 8000 | tf_op jit(solution)/shard_map/conv_wgrad/pallas_call | solution.py:348
  377.4 13.3 %collective-permute-done.40 = f32[4,32,2048]{2,1,0:T(8,128)S(1)} collective-permute-done((f32[4,32,2048]{2,1,0:T(8,128)S(1)}, f32[4,32,2048]{2,1,0:T(8,128)S(1)}, u32[]{:S(2)}, u32[]{:S(2)}) %collective-permute-start.40) | collective-permute-done | bytes 1048608 | tf_op jit(solution)/shard_map/ppermute | solution.py:405
  392.6 8.6 %far_product.3 = f32[4,256,2048]{2,1,0:T(8,128)} custom-call(s32[4]{0:T(128)S(1)} %add_add_fusion.2.place_ref, bf16[784,2016]{1,0:T(8,128)(2,1)S(1)} %bitcast.229, bf16[784,2016]{1,0:T(8,128)(2,1)S(1)} %multiply_convert_fusion.right_ref), custom_call_target="tpu_custom_call" | custom-call | flops 9000000 | bytes 9000 | tf_op jit(solution)/shard_map/far_product/pallas_call | solution.py:527
  403.2 18.0 %collective-permute-done.43 = f32[1,2,32,3072]{3,2,1,0:T(8,128)S(1)} collective-permute-done((f32[1,2,32,3072]{3,2,1,0:T(8,128)S(1)}, f32[1,2,32,3072]{3,2,1,0:T(8,128)S(1)}, u32[]{:S(2)}, u32[]{:S(2)}) %collective-permute-start.43) | collective-permute-done | bytes 786464 | tf_op jit(solution)/shard_map/ppermute | solution.py:405
  427.6 12.7 %near_product.3 = (f32[2,4,32,2048]{3,2,1,0:T(8,128)S(1)}, f32[2,4,32,2048]{3,2,1,0:T(8,128)S(1)}, f32[2,4,32,2048]{3,2,1,0:T(8,128)}, f32[2,4,32,2048]{3,2,1,0:T(8,128)}) custom-call(s32[4]{0:T(128)S(1)} %add_add_fusion.1.place_ref, bf16[784,2016]{1,0:T(8,128)(2,1)} %bitcast.228, bf16[784,2016]{1,0:T(8,128)(2,1)} %copy-done.5, ...), custom_call_target="tpu_custom_call" | custom-call | flops 13000000 | bytes 13000 | tf_op jit(solution)/shard_map/near_product/pallas_call | solution.py:554
  446.3 19.0 %conv_wgrad.3 = f32[9,9,56,256]{3,2,1,0:T(8,128)} custom-call(s32[2]{0:T(128)} %pad_add_fusion.1.glob_ref, bf16[784,2016]{1,0:T(8,128)(2,1)} %multiply_convert_fusion.1.refs_0_.refs_1_.refs_2_, bf16[784,2016]{1,0:T(8,128)(2,1)} %multiply_convert_fusion.1.refs_0_.refs_1_.refs_2_, ...), custom_call_target="tpu_custom_call", output_to_operand_aliasing={{}: (11, {})} | custom-call | flops 10000000 | bytes 10000 | tf_op jit(solution)/shard_map/conv_wgrad/pallas_call | solution.py:348
  473.5 13.4 %collective-permute-done.46 = f32[2,4,32,2048]{3,2,1,0:T(8,128)} collective-permute-done((f32[2,4,32,2048]{3,2,1,0:T(8,128)S(1)}, f32[2,4,32,2048]{3,2,1,0:T(8,128)}, u32[]{:S(2)}, u32[]{:S(2)}) %collective-permute-start.46) | collective-permute-done | bytes 2097184 | tf_op jit(solution)/shard_map/ppermute | solution.py:405
  500.0 13.9 %convolution_add_fusion = f32[784,2016]{1,0:T(8,128)} fusion(f32[784,2016]{1,0:T(8,128)} %get-tuple-element.451, bf16[784,2016]{1,0:T(8,128)(2,1)} %copy-done.5, bf16[2016,2016]{1,0:T(8,128)(2,1)} %param.20), kind=kOutput, calls=%fused_computation.20 | convolution fusion | flops 6374333952 | bytes 23933952 | tf_op jit(solution)/shard_map/rv,wv->rw/dot_general | solution.py:1112
  513.9 19.0 %collective-permute-done.51 = f32[4,32,2048]{2,1,0:T(8,128)S(1)} collective-permute-done((f32[4,32,2048]{2,1,0:T(8,128)}, f32[4,32,2048]{2,1,0:T(8,128)S(1)}, u32[]{:S(2)}, u32[]{:S(2)}) %collective-permute-start.51) | collective-permute-done | bytes 1048608 | tf_op jit(solution)/shard_map/ppermute | solution.py:405
  541.1 19.5 %collective-permute-done.53 = f32[2,4,88,256]{3,2,1,0:T(8,128)S(1)} collective-permute-done((f32[2,4,88,256]{3,2,1,0:T(8,128)S(1)}, f32[2,4,88,256]{3,2,1,0:T(8,128)S(1)}, u32[]{:S(2)}, u32[]{:S(2)}) %collective-permute-start.53) | collective-permute-done | bytes 720928 | tf_op jit(solution)/shard_map/ppermute | solution.py:405
  580.0 10.6 %collective-permute-done.55 = f32[1,64,2048]{2,1,0:T(8,128)S(1)} collective-permute-done((f32[1,64,2048]{2,1,0:T(8,128)S(1)}, f32[1,64,2048]{2,1,0:T(8,128)S(1)}, u32[]{:S(2)}, u32[]{:S(2)}) %collective-permute-start.55) | collective-permute-done | bytes 524320 | tf_op jit(solution)/shard_map/ppermute | solution.py:405
  616.7 10.6 %collective-permute-done.66 = f32[1,88,256]{2,1,0:T(8,128)S(1)} collective-permute-done((f32[1,88,256]{2,1,0:T(8,128)S(1)}, f32[1,88,256]{2,1,0:T(8,128)S(1)}, u32[]{:S(2)}, u32[]{:S(2)}) %collective-permute-start.66) | collective-permute-done | bytes 90144 | tf_op jit(solution)/shard_map/ppermute | solution.py:405
  (478 shorter events, 318.2 us)
Async XLA Ops:
  7.2 214.6 %all-gather.3.cloned.1.call-start = ((), (), s32[]{:S(2)}) async-start(), calls=%async_computation | async-start | bytes 2949120 | tf_op jit(solution)/shard_map/all_gather | solution.py:972
  175.8 177.7 %all-gather.5.cloned.1.call-start = ((), (), s32[]{:S(2)}) async-start(), calls=%async_computation.1 | async-start | bytes 2949120 | tf_op jit(solution)/shard_map/all_gather | solution.py:1023
  237.1 24.4 %collective-permute-start.22 = (f32[1,2,32,3072]{3,2,1,0:T(8,128)}, f32[1,2,32,3072]{3,2,1,0:T(8,128)S(1)}, u32[]{:S(2)}, u32[]{:S(2)}) collective-permute-start(f32[1,2,32,3072]{3,2,1,0:T(8,128)} %dynamic-slice_bitcast_fusion.1), channel_id=1, source_target_pairs={{0,8},{8,0},{16,24},{24,16},{1,9},{9,1},{17,25},{25,17},{2,10},{10... | collective-permute-start | bytes 2359304 | tf_op jit(solution)/shard_map/ppermute | solution.py:405
  265.2 380.9 %all-reduce.5.cloned.1.call-start = ((), (), s32[]{:S(2)}) async-start(), calls=%async_computation.2 | async-start | bytes 2048000 | tf_op jit(solution)/shard_map/psum | solution.py:1090
  297.0 48.9 %collective-permute-start.31 = (f32[2,4,32,2048]{3,2,1,0:T(8,128)}, f32[2,4,32,2048]{3,2,1,0:T(8,128)}, u32[]{:S(2)}, u32[]{:S(2)}) collective-permute-start(f32[2,4,32,2048]{3,2,1,0:T(8,128)} %get-tuple-element.224), channel_id=1, source_target_pairs={{0,8},{8,0},{16,24},{24,16},{1,9},{9,1},{17,25},{25,17},{2,10},{10... | collective-permute-start | bytes 6291464 | tf_op jit(solution)/shard_map/ppermute | solution.py:405
  297.6 49.0 %collective-permute-start.32 = (f32[2,4,32,2048]{3,2,1,0:T(8,128)}, f32[2,4,32,2048]{3,2,1,0:T(8,128)}, u32[]{:S(2)}, u32[]{:S(2)}) collective-permute-start(f32[2,4,32,2048]{3,2,1,0:T(8,128)} %get-tuple-element.225), channel_id=1, source_target_pairs={{0,16},{8,24},{16,0},{24,8},{1,17},{9,25},{17,1},{25,9},{2,18},{10... | collective-permute-start | bytes 6291464 | tf_op jit(solution)/shard_map/ppermute | solution.py:405
  323.3 30.2 %collective-permute-start.34 = (f32[1,32,3072]{2,1,0:T(8,128)S(1)}, f32[1,32,3072]{2,1,0:T(8,128)}, u32[]{:S(2)}, u32[]{:S(2)}) collective-permute-start(f32[1,32,3072]{2,1,0:T(8,128)S(1)} %bitcast_add_fusion.3), channel_id=1, source_target_pairs={{0,16},{8,24},{16,0},{24,8},{1,17},{9,25},{17,1},{25,9},{2,18},{10... | collective-permute-start | bytes 1179656 | tf_op jit(solution)/shard_map/ppermute | solution.py:405
  325.3 28.3 %collective-permute-start.35 = (f32[1,32,3072]{2,1,0:T(8,128)S(1)}, f32[1,32,3072]{2,1,0:T(8,128)S(1)}, u32[]{:S(2)}, u32[]{:S(2)}) collective-permute-start(f32[1,32,3072]{2,1,0:T(8,128)S(1)} %bitcast_add_fusion.2), channel_id=1, source_target_pairs={{0,8},{8,0},{16,24},{24,16},{1,9},{9,1},{17,25},{25,17},{2,10},{10... | collective-permute-start | bytes 1179656 | tf_op jit(solution)/shard_map/ppermute | solution.py:405
  366.6 24.1 %collective-permute-start.40 = (f32[4,32,2048]{2,1,0:T(8,128)S(1)}, f32[4,32,2048]{2,1,0:T(8,128)S(1)}, u32[]{:S(2)}, u32[]{:S(2)}) collective-permute-start(f32[4,32,2048]{2,1,0:T(8,128)S(1)} %copy-done.33), channel_id=1, source_target_pairs={{0,16},{8,24},{16,0},{24,8},{1,17},{9,25},{17,1},{25,9},{2,18},{10... | collective-permute-start | bytes 3145736 | tf_op jit(solution)/shard_map/ppermute | solution.py:405
  368.3 23.8 %collective-permute-start.41 = (f32[4,32,2048]{2,1,0:T(8,128)S(1)}, f32[4,32,2048]{2,1,0:T(8,128)S(1)}, u32[]{:S(2)}, u32[]{:S(2)}) collective-permute-start(f32[4,32,2048]{2,1,0:T(8,128)S(1)} %copy-done.34), channel_id=1, source_target_pairs={{0,8},{8,0},{16,24},{24,16},{1,9},{9,1},{17,25},{25,17},{2,10},{10... | collective-permute-start | bytes 3145736 | tf_op jit(solution)/shard_map/ppermute | solution.py:405
  402.3 25.0 %collective-permute-start.42 = (f32[2,64,2048]{2,1,0:T(8,128)S(1)}, f32[2,64,2048]{2,1,0:T(8,128)S(1)}, u32[]{:S(2)}, u32[]{:S(2)}) collective-permute-start(f32[2,64,2048]{2,1,0:T(8,128)S(1)} %get-tuple-element.258), channel_id=1, source_target_pairs={{0,2},{1,3},{2,0},{3,1},{4,6},{5,7},{6,4},{7,5},{8,10},{9,11},{10,... | collective-permute-start | bytes 3145736 | tf_op jit(solution)/shard_map/ppermute | solution.py:405
  440.2 46.7 %collective-permute-start.46 = (f32[2,4,32,2048]{3,2,1,0:T(8,128)S(1)}, f32[2,4,32,2048]{3,2,1,0:T(8,128)}, u32[]{:S(2)}, u32[]{:S(2)}) collective-permute-start(f32[2,4,32,2048]{3,2,1,0:T(8,128)S(1)} %get-tuple-element.273), channel_id=1, source_target_pairs={{0,8},{8,0},{16,24},{24,16},{1,9},{9,1},{17,25},{25,17},{2,10},{10... | collective-permute-start | bytes 6291464 | tf_op jit(solution)/shard_map/ppermute | solution.py:405
  441.5 46.7 %collective-permute-start.47 = (f32[2,4,32,2048]{3,2,1,0:T(8,128)}, f32[2,4,32,2048]{3,2,1,0:T(8,128)}, u32[]{:S(2)}, u32[]{:S(2)}) collective-permute-start(f32[2,4,32,2048]{3,2,1,0:T(8,128)} %get-tuple-element.274), channel_id=1, source_target_pairs={{0,16},{8,24},{16,0},{24,8},{1,17},{9,25},{17,1},{25,9},{2,18},{10... | collective-permute-start | bytes 6291464 | tf_op jit(solution)/shard_map/ppermute | solution.py:405
  443.2 24.5 %collective-permute-start.48 = (f32[1,64,2048]{2,1,0:T(8,128)S(1)}, f32[1,64,2048]{2,1,0:T(8,128)S(1)}, u32[]{:S(2)}, u32[]{:S(2)}) collective-permute-start(f32[1,64,2048]{2,1,0:T(8,128)S(1)} %get-tuple-element.276), channel_id=1, source_target_pairs={{0,4},{1,5},{2,6},{3,7},{4,0},{5,1},{6,2},{7,3},{8,12},{9,13},{10,... | collective-permute-start | bytes 1572872 | tf_op jit(solution)/shard_map/ppermute | solution.py:405
  494.6 38.9 %collective-permute-start.49 = (f32[4,704,256]{2,1,0:T(8,128)}, f32[4,704,256]{2,1,0:T(8,128)}, u32[]{:S(2)}, u32[]{:S(2)}) collective-permute-start(f32[4,704,256]{2,1,0:T(8,128)} %units.2), channel_id=1, source_target_pairs={{0,1},{1,0},{2,3},{3,2},{4,5},{5,4},{6,7},{7,6},{8,9},{9,8},{10,11... | collective-permute-start | bytes 8650760 | tf_op jit(solution)/shard_map/ppermute | solution.py:405
  497.1 42.8 %collective-permute-start.39 = (f32[8,2016]{1,0:T(8,128)S(1)}, f32[8,2016]{1,0:T(8,128)S(1)}, u32[]{:S(2)}, u32[]{:S(2)}) collective-permute-start(f32[8,2016]{1,0:T(8,128)S(1)} %pad_maximum_fusion.23), channel_id=1, source_target_pairs={{0,16},{8,24},{16,0},{24,8},{1,17},{9,25},{17,1},{25,9},{2,18},{10... | collective-permute-start | bytes 193544 | tf_op jit(solution)/shard_map/ppermute | solution.py:404
  498.9 34.0 %collective-permute-start.51 = (f32[4,32,2048]{2,1,0:T(8,128)}, f32[4,32,2048]{2,1,0:T(8,128)S(1)}, u32[]{:S(2)}, u32[]{:S(2)}) collective-permute-start(f32[4,32,2048]{2,1,0:T(8,128)} %get-tuple-element.298), channel_id=1, source_target_pairs={{0,8},{8,0},{16,24},{24,16},{1,9},{9,1},{17,25},{25,17},{2,10},{10... | collective-permute-start | bytes 3145736 | tf_op jit(solution)/shard_map/ppermute | solution.py:405
  499.6 33.7 %collective-permute-start.50 = (f32[4,32,2048]{2,1,0:T(8,128)}, f32[4,32,2048]{2,1,0:T(8,128)S(1)}, u32[]{:S(2)}, u32[]{:S(2)}) collective-permute-start(f32[4,32,2048]{2,1,0:T(8,128)} %get-tuple-element.296), channel_id=1, source_target_pairs={{0,16},{8,24},{16,0},{24,8},{1,17},{9,25},{17,1},{25,9},{2,18},{10... | collective-permute-start | bytes 3145736 | tf_op jit(solution)/shard_map/ppermute | solution.py:405
  537.1 23.5 %collective-permute-start.53 = (f32[2,4,88,256]{3,2,1,0:T(8,128)S(1)}, f32[2,4,88,256]{3,2,1,0:T(8,128)S(1)}, u32[]{:S(2)}, u32[]{:S(2)}) collective-permute-start(f32[2,4,88,256]{3,2,1,0:T(8,128)S(1)} %get-tuple-element.302), channel_id=1, source_target_pairs={{0,8},{8,0},{16,24},{24,16},{1,9},{9,1},{17,25},{25,17},{2,10},{10... | collective-permute-start | bytes 2162696 | tf_op jit(solution)/shard_map/ppermute | solution.py:405
  538.5 23.5 %collective-permute-start.54 = (f32[2,4,88,256]{3,2,1,0:T(8,128)S(1)}, f32[2,4,88,256]{3,2,1,0:T(8,128)S(1)}, u32[]{:S(2)}, u32[]{:S(2)}) collective-permute-start(f32[2,4,88,256]{3,2,1,0:T(8,128)S(1)} %get-tuple-element.303), channel_id=1, source_target_pairs={{0,16},{8,24},{16,0},{24,8},{1,17},{9,25},{17,1},{25,9},{2,18},{10... | collective-permute-start | bytes 2162696 | tf_op jit(solution)/shard_map/ppermute | solution.py:405
  538.8 28.3 %collective-permute-start.52 = (f32[2,64,2048]{2,1,0:T(8,128)S(1)}, f32[2,64,2048]{2,1,0:T(8,128)S(1)}, u32[]{:S(2)}, u32[]{:S(2)}) collective-permute-start(f32[2,64,2048]{2,1,0:T(8,128)S(1)} %get-tuple-element.355), channel_id=1, source_target_pairs={{0,2},{1,3},{2,0},{3,1},{4,6},{5,7},{6,4},{7,5},{8,10},{9,11},{10,... | collective-permute-start | bytes 3145736 | tf_op jit(solution)/shard_map/ppermute | solution.py:405
  575.1 27.2 %collective-permute-start.62 = (f32[2,176,256]{2,1,0:T(8,128)}, f32[2,176,256]{2,1,0:T(8,128)}, u32[]{:S(2)}, u32[]{:S(2)}) collective-permute-start(f32[2,176,256]{2,1,0:T(8,128)} %get-tuple-element.389), channel_id=1, source_target_pairs={{0,2},{1,3},{2,0},{3,1},{4,6},{5,7},{6,4},{7,5},{8,10},{9,11},{10,... | collective-permute-start | bytes 1081352 | tf_op jit(solution)/shard_map/ppermute | solution.py:405
  605.6 32.4 %collective-permute-start.63 = (f32[1,2,32,2048]{3,2,1,0:T(8,128)}, f32[1,2,32,2048]{3,2,1,0:T(8,128)}, u32[]{:S(2)}, u32[]{:S(2)}) collective-permute-start(f32[1,2,32,2048]{3,2,1,0:T(8,128)} %pad_maximum_fusion.16), channel_id=1, source_target_pairs={{0,8},{8,0},{16,24},{24,16},{1,9},{9,1},{17,25},{25,17},{2,10},{10... | collective-permute-start | bytes 1572872 | tf_op jit(solution)/shard_map/ppermute | solution.py:405
  607.3 30.7 %collective-permute-start.64 = (f32[1,2,32,2048]{3,2,1,0:T(8,128)}, f32[1,2,32,2048]{3,2,1,0:T(8,128)}, u32[]{:S(2)}, u32[]{:S(2)}) collective-permute-start(f32[1,2,32,2048]{3,2,1,0:T(8,128)} %pad_maximum_fusion.17), channel_id=1, source_target_pairs={{0,16},{8,24},{16,0},{24,8},{1,17},{9,25},{17,1},{25,9},{2,18},{10... | collective-permute-start | bytes 1572872 | tf_op jit(solution)/shard_map/ppermute | solution.py:405
  (116 other events, 1517.7 us)
Sparse Core Ops, SparseCore 0:
  176.0 31.5 all-gather.2
  265.3 32.0 all-gather.4
  497.2 66.9 all-reduce.4

commit v3 on v2

--- a/solution.py
+++ b/solution.py
@@ -383,7 +383,7 @@
 SIDE = 14
 SMALL_SIDE = 7
 LOW_COLUMNS = 0
-TAIL = (0, 2, 0, 2, 1, 0, 2, 0, 2, 1, 2, 0, 2)
+TAIL = (0, 1, 2, 0, 2, 1, 0, 2, 0, 2, 1, 2, 0, 2)
 WIDE = 2048
 WIDE_PROTOS = 3072
 
@@ -420,6 +420,23 @@
 
 def exact_dot(left, right):
     return jnp.dot(left, right, precision=exact_mode, preferred_element_type=jnp.float32)
+
+
+def spread_dot(member_rows, values):
+    terms, rest = [], values
+    for _ in range(3):
+        term = lax.reduce_precision(rest, 8, 7)
+        terms.append(term.astype(jnp.bfloat16))
+        rest = rest - term
+    return jnp.dot(
+        jnp.concatenate([member_rows] * 3, axis=1),
+        jnp.concatenate(terms, axis=0),
+        preferred_element_type=jnp.float32,
+    )
+
+
+def pool_dot(member, values):
+    return jnp.dot(member, values.astype(jnp.bfloat16), preferred_element_type=jnp.float32)
 
 
 def bits_of(size):
@@ -855,7 +872,7 @@
     masks = jnp.stack([across > 0, across < side - 1, down > 0, down < side - 1])
     masks = jnp.broadcast_to(masks.astype(jnp.float32)[:, :, None], (4, row_count, 128))
     member = (seg_of_row[None, :] == jnp.arange(seg_count, dtype=jnp.int32)[:, None]).astype(
-        jnp.float32
+        jnp.bfloat16
     )
     member_rows = member.T
     crop_pixels = jnp.where(is_global, float(SIDE * SIDE), float(SMALL_SIDE * SMALL_SIDE))
@@ -893,11 +910,11 @@
     act_two = smooth_gate(pre_two)
     red_float = w_red.astype(jnp.float32)
     exp_float = w_exp.astype(jnp.float32)
-    pooled = exact_dot(member, act_two) / crop_pixels
+    pooled = pool_dot(member, act_two) / crop_pixels
     reduce_pre = exact_dot(pooled, red_float) + b_red
     reduced = smooth_gate(reduce_pre)
     gate_values = jax.nn.sigmoid(exact_dot(reduced, exp_float) + b_exp)
-    gate_rows = exact_dot(member_rows, gate_values)
+    gate_rows = spread_dot(member_rows, gate_values)
     excited = (act_two * gate_rows).astype(jnp.bfloat16)
     hidden_three = jnp.dot(excited, w_out, preferred_element_type=jnp.float32)
     sums = jnp.stack([jnp.sum(hidden_three, axis=0), jnp.sum(hidden_three * hidden_three, axis=0)])
@@ -905,7 +922,15 @@
     centred_three = (hidden_three - mean_three) * inv_three
     summed_in = inputs.astype(jnp.float32) + centred_three * gain_three + shift_three
     output = smooth_gate(summed_in)
-    pooled_out = exact_dot(member, output) / crop_pixels
+    pooled_out = (
+        jnp.dot(
+            member.astype(jnp.float32),
+            output,
+            precision=lax.Precision.HIGH,
+            preferred_element_type=jnp.float32,
+        )
+        / crop_pixels
+    )
     length_inv = lax.rsqrt(jnp.sum(pooled_out * pooled_out, axis=1, keepdims=True) + length_epsilon)
     unit_wide = pooled_out * length_inv
     unit_rows = unit_wide.astype(jnp.bfloat16)
@@ -948,7 +973,7 @@
     grad_pooled_out = (
         length_inv * grad_unit - pooled_out * length_inv * length_inv * length_inv * inner_term
     )
-    grad_output = exact_dot(member_rows, grad_pooled_out / crop_pixels)
+    grad_output = spread_dot(member_rows, grad_pooled_out / crop_pixels)
     grad_summed = grad_output * smooth_slope(summed_in)
     sums_three, scale_three, first, second, _ = back_rows(
         jnp.stack([jnp.sum(grad_summed, axis=0), jnp.sum(grad_summed * centred_three, axis=0)]),
@@ -997,11 +1022,11 @@
         )
         (protos_sum.keep, grad_excited) = tie(protos_sum.keep, grad_excited)
         flow.begin(protos_sum)
-    grad_gate = exact_dot(member, grad_excited * act_two)
+    grad_gate = pool_dot(member, grad_excited * act_two)
     grad_gate_pre = grad_gate * gate_values * (1.0 - gate_values)
     grad_reduce_pre = exact_dot(grad_gate_pre, exp_float.T) * smooth_slope(reduce_pre)
     grad_pooled = exact_dot(grad_reduce_pre, red_float.T)
-    grad_act_two = grad_excited * gate_rows + exact_dot(member_rows, grad_pooled / crop_pixels)
+    grad_act_two = grad_excited * gate_rows + spread_dot(member_rows, grad_pooled / crop_pixels)
     grad_pre_two = grad_act_two * smooth_slope(pre_two)
     bias_row = jnp.concatenate(
         [
@@ -1088,11 +1113,11 @@
     if fast:
         share_red, share_exp = made[-1]
         share_red, share_exp = lax.psum((share_red, share_exp), "crop")
-        grad_one_low = flow.advance(outs, grad_one_low)
-        arrived = far_product(far, inputs, grad_one_low, devices, LOW_COLUMNS)
-        arrived = [swap(v, "img", 1) for v in arrived]
-        arrived = flow.advance(protos_sum, arrived)
-        arrived = flow.advance(outs, arrived)
+        sent_far = far_product(far, inputs, grad_one_low, devices, LOW_COLUMNS)
+        flow.sent[id(outs)], sent_far = tie(flow.sent[id(outs)], sent_far)
+        outs.take(flow.sent[id(outs)])
+        flow.begin(outs)
+        arrived = [swap(v, "img", 1) for v in sent_far]
         parts = near_product(near, inputs, grad_one_low, devices, LOW_COLUMNS, arrived)
         ins = HighChain(*parts)
         units, grad_two_low, grad_one_low, ins.keep, ins.away = tie(
@@ -1101,6 +1126,7 @@
         flow.begin(ins)
         units = steps[1](grad_two_low, units)
         units = flow.advance(outs, units)
+        units = flow.advance(protos_sum, units)
         gw = kernel.shape[2]
         unit_size = gw * gw * PACK
         units = units.reshape(-1, 256)

time: 666 us -> 640 us (0.961)
  waiting for transfers between devices: 193 us -> 170 us
  matrix products: 108 us -> 95.6 us
    dot_general x12 -> x6, matrix products: 50.5 us -> 8.67 us  [exact_dot(): jnp.dot(left, right, precision=exact_mode, preferred_element_type=jnp.flo...]
    dot_general x0 -> x6, matrix products: none -> 29.7 us  [the longest x3 18.5 us: spread_dot(): jnp.dot(jnp.concatenate([member_rows] * 3, axis=1), jnp.concatenate(terms...]
    ppermute x41, waiting for transfers between devices: 130 us -> 110 us  [swap(): return plain(lax.ppermute(plain(value), axis, pairs))]
    another operation x24 -> x23, other arithmetic: 13.9 us -> 16.4 us  [crop_join(): jnp.stack([jnp.where(upper, other, part), jnp.where(upper, part, other)],...]
    unnamed x130 -> x134, local copies, waits for them, and re-layouts: 16.3 us -> 17.5 us
  transfers between devices with their start and end apart: 75 -> 75, of which waited for: 42 -> 38; matrix products, arithmetic and copies ran while one was open for 20% -> 21% of each run, Pallas kernels for 15% -> 19%
where the time goes in v3:
time: 640 us; the launch traced here: 631 us
  waiting for transfers between devices  170 us (27%)
  Pallas kernels  145 us (23%)
  matrix products  95.6 us (15%)
  other arithmetic  71.4 us (11%)
  starting transfers between devices  71.1 us (11%)
  local copies, waits for them, and re-layouts  60.6 us (9%)
  between operations  16.6 us (3%)
    ppermute x41, waiting for transfers between devices, swap(): return plain(lax.ppermute(plain(value), axis, pairs))  110 us
    ppermute x28, waiting for transfers between devices, swap(): return lax.ppermute(value, axis, pairs)  58.1 us
    ppermute x41, starting transfers between devices, swap(): return plain(lax.ppermute(plain(value), axis, pairs))  44.8 us
    pallas_call x2, Pallas kernels, conv_wgrad(): pl.pallas_call(functools.partial(conv_kernel, wgrad_step, rows + 2 * EDGE...  35 us
    pallas_call x2, Pallas kernels, near_product(): pl.pallas_call(functools.partial(near_kernel, devices, width, height, low...  26.1 us
    pallas_call x1, Pallas kernels, conv_fwd(): pl.pallas_call(functools.partial(conv_kernel, fwd_step, rows + 2 * EDGE,...  23.6 us
    pallas_call x1, Pallas kernels, conv_dgrad(): pl.pallas_call(functools.partial(conv_kernel, dgrad_step, rows + 2 * EDGE...  23 us
    dot_general x3, matrix products, spread_dot(): jnp.dot(jnp.concatenate([member_rows] * 3, axis=1), jnp.concatenate(terms...  18.5 us
  transfers between devices with their start and end apart: 75, of which 38 were waited for; matrix products, arithmetic and copies ran while one was open for 21% of the time, Pallas kernels for 19%

profile of v3, /device:TPU:0, one launch (start us, length us, event | category | flops | bytes accessed | tf_op | source)
XLA Modules:
  0.0 630.6 jit_solution(12569052937149637409)
XLA Ops:
  7.2 12.0 %fusion.91 = (f32[2016]{0:T(1024)S(1)}, f32[2016]{0:T(1024)S(1)}, f32[784,2016]{1,0:T(8,128)}) fusion(bf16[2016,2016]{1,0:T(8,128)(2,1)} %param.20, bf16[1,1,784,2016]{3,2,1,0:T(8,128)(2,1)} %param.17), kind=kOutput, calls=%fused_computation.285 | convolution fusion | flops 6377490944 | bytes 17627904 | tf_op jit(solution)/shard_map/dot_general | solution.py:893
  43.9 23.6 %conv_fwd.1 = (f32[784,2016]{1,0:T(8,128)}, f32[8,2016]{1,0:T(8,128)}) custom-call(s32[1]{0:T(128)} %bitcast.4.glob_ref, f32[784,2016]{1,0:T(8,128)} %get-tuple-element.437.refs_0_.refs_1_.refs_2_.refs_3_.refs_4_.refs_5_, f32[784,2016]{1,0:T(8,128)} %get-tuple-element.437.refs_0_.refs_1_.refs_2_.refs_3_.refs_4_.refs_5_, ...), custom_call_target="tpu_custom_call" | custom-call | flops 20000000 | bytes 20000 | tf_op jit(solution)/shard_map/conv_fwd/pallas_call | solution.py:300
  94.0 10.5 %fusion.90 = (f32[2016]{0:T(1024)S(1)}, f32[2016]{0:T(1024)S(1)}, f32[784,2016]{1,0:T(8,128)S(1)}) fusion(bf16[784,2016]{1,0:T(8,128)(2,1)S(1)} %get-tuple-element.192.left_ref, bf16[2016,2016]{1,0:T(8,128)(2,1)} %param.26), kind=kOutput, calls=%fused_computation.284 | convolution fusion | flops 6377490944 | bytes 17627904 | tf_op jit(solution)/shard_map/dot_general | solution.py:919
  137.9 11.2 %collective-permute-done.14 = f32[16,3000]{1,0:T(8,128)S(1)} collective-permute-done((f32[16,3000]{1,0:T(8,128)S(1)}, f32[16,3000]{1,0:T(8,128)S(1)}, u32[]{:S(2)}, u32[]{:S(2)}) %collective-permute-start.14) | collective-permute-done | bytes 192032 | tf_op jit(solution)/shard_map/ppermute | solution.py:404
  162.8 6.5 %multiply_reduce_fusion.6 = (f32[16]{0:T(128)S(1)}, f32[16,2016]{1,0:T(8,128)S(1)}) fusion(f32[16,2016]{1,0:T(8,128)S(1)} %get-tuple-element.443, bf16[2016,3000]{0,1:T(8,128)(2,1)} %param.33, f32[16,3000]{1,0:T(8,128)S(1)} %subtract_multiply_fusion.2), kind=kOutput, calls=%fused_computation.182 | convolution fusion | flops 193648496 | bytes 12546112 | tf_op jit(solution)/shard_map/sk,wk->sw/dot_general | solution.py:971
  170.4 8.3 %fusion.89 = (f32[2016]{0:T(1024)S(1)}, f32[2016]{0:T(1024)S(1)}, f32[784,2016]{1,0:T(8,128)}) fusion(f32[2016]{0:T(1024)S(1)} %bitcast.243, f32[784,2016]{1,0:T(8,128)} %copy-done.11, f32[2016]{0:T(1024)S(1)} %bitcast.255, f32[2016]{0:T(1024)S(1)} %copy-done.46, f32[2016]{0:T(1024)S(1)} %copy-done.44, bf16[1,1,784,2016]{3,2,1,0:T(8,128)(2,1)} %param.17, ...), kind=kOutput, calls=%fused_computation.283 | convolution fusion | flops 179253312 | bytes 16059904 | tf_op jit(solution)/shard_map/dot_general | solution.py:431
  193.9 6.5 %multiply_convert_fusion.3.right_ref = bf16[784,2016]{1,0:T(8,128)(2,1)S(1)} fusion(f32[784,2016]{1,0:T(8,128)} %get-tuple-element.448, f32[784,2016]{1,0:T(8,128)} %copy-done.11, f32[2016]{0:T(1024)S(1)} %bitcast.287, f32[2016]{0:T(1024)S(1)} %bitcast.286, f32[2016]{0:T(1024)S(1)} %bitcast.245, f32[2016]{0:T(1024)S(1)} %bitcast.256, f32[2016]{0:T(1024)S(1)} %mul.299), kind=kLoop, calls=%fused_computation.5 | loop fusion | flops 11063808 | bytes 15845760 | tf_op jit(solution)/shard_map/convert_element_type | solution.py:983
  200.4 11.3 %fusion.104 = f32[784,2016]{1,0:T(8,128)} fusion(bf16[784,2016]{1,0:T(8,128)(2,1)S(1)} %multiply_convert_fusion.3.right_ref, bf16[2016,2016]{1,0:T(8,128)(2,1)} %param.26), kind=kOutput, calls=%fused_computation.295 | convolution fusion | flops 6372753408 | bytes 17611776 | tf_op jit(solution)/shard_map/rv,wv->rw/dot_general | solution.py:1011
  239.8 8.6 %far_product.2 = f32[4,256,2048]{2,1,0:T(8,128)} custom-call(s32[4]{0:T(128)S(1)} %add_add_fusion.2.place_ref, bf16[784,2016]{1,0:T(8,128)(2,1)S(1)} %copy-done.8, bf16[784,2016]{1,0:T(8,128)(2,1)S(1)} %copy-done.6), custom_call_target="tpu_custom_call" | custom-call | flops 9000000 | bytes 9000 | tf_op jit(solution)/shard_map/far_product/pallas_call | solution.py:544
  261.2 8.1 %multiply_convert_fusion.1.refs_0_.refs_1_.refs_2_ = bf16[784,2016]{1,0:T(8,128)(2,1)} fusion(f32[784,2016]{1,0:T(8,128)} %get-tuple-element.453, f32[784,2016]{1,0:T(8,128)} %get-tuple-element.184, f32[2016]{0:T(1024)S(1)} %bitcast.285, f32[2016]{0:T(1024)S(1)} %bitcast.284, f32[2016]{0:T(1024)S(1)} %mul.340, f32[2016]{0:T(1024)S(1)} %bitcast.264, ...), kind=kLoop, calls=%fused_computation.1 | loop fusion | flops 11063808 | bytes 15845760 | tf_op jit(solution)/shard_map/convert_element_type | solution.py:1066
  269.5 13.4 %near_product.2 = (f32[2,4,32,2048]{3,2,1,0:T(8,128)S(1)}, f32[2,4,32,2048]{3,2,1,0:T(8,128)}, f32[2,4,32,2048]{3,2,1,0:T(8,128)}, f32[2,4,32,2048]{3,2,1,0:T(8,128)}) custom-call(s32[4]{0:T(128)S(1)} %add_add_fusion.1.place_ref, bf16[784,2016]{1,0:T(8,128)(2,1)} %copy-done.7, bf16[784,2016]{1,0:T(8,128)(2,1)} %copy-done.5, ...), custom_call_target="tpu_custom_call" | custom-call | flops 13000000 | bytes 13000 | tf_op jit(solution)/shard_map/near_product/pallas_call | solution.py:571
  288.3 23.0 %conv_dgrad.1 = (f32[784,2016]{1,0:T(8,128)}, f32[8,2016]{1,0:T(8,128)}) custom-call(s32[1]{0:T(128)} %bitcast.4.glob_ref, bf16[784,2016]{1,0:T(8,128)(2,1)} %multiply_convert_fusion.1.refs_0_.refs_1_.refs_2_, bf16[784,2016]{1,0:T(8,128)(2,1)} %multiply_convert_fusion.1.refs_0_.refs_1_.refs_2_, ...), custom_call_target="tpu_custom_call" | custom-call | flops 20000000 | bytes 20000 | tf_op jit(solution)/shard_map/conv_dgrad/pallas_call | solution.py:323
  313.9 16.0 %conv_wgrad.2.refs_10_ = f32[9,9,56,256]{3,2,1,0:T(8,128)} custom-call(s32[2]{0:T(128)} %pad_add_fusion.1.glob_ref, bf16[784,2016]{1,0:T(8,128)(2,1)} %multiply_convert_fusion.1.refs_0_.refs_1_.refs_2_, bf16[784,2016]{1,0:T(8,128)(2,1)} %multiply_convert_fusion.1.refs_0_.refs_1_.refs_2_, bf16[784,2016]{1,0:T(8,128)(2,1)} %multiply_convert_fusion.1.refs_0_.refs_1_.refs_2_, ...), custom_call_target="tpu_custom_call" | custom-call | flops 8000000 | bytes 8000 | tf_op jit(solution)/shard_map/conv_wgrad/pallas_call | solution.py:348
  359.3 6.6 %multiply_convert_fusion.right_ref = bf16[784,2016]{1,0:T(8,128)(2,1)S(1)} fusion(f32[784,2016]{1,0:T(8,128)} %get-tuple-element.437.refs_0_.refs_1_.refs_2_.refs_3_.refs_4_.refs_5_, f32[784,2016]{1,0:T(8,128)} %get-tuple-element.241, f32[2016]{0:T(1024)S(1)} %bitcast.289, f32[2016]{0:T(1024)S(1)} %bitcast.257, f32[2016]{0:T(1024)S(1)} %bitcast.266, ...), kind=kLoop, calls=%fused_computation | loop fusion | flops 11063808 | bytes 15845760 | tf_op jit(solution)/shard_map/convert_element_type | solution.py:1112
  365.9 8.6 %far_product.3 = f32[4,256,2048]{2,1,0:T(8,128)} custom-call(s32[4]{0:T(128)S(1)} %add_add_fusion.2.place_ref, bf16[784,2016]{1,0:T(8,128)(2,1)S(1)} %bitcast.229, bf16[784,2016]{1,0:T(8,128)(2,1)S(1)} %multiply_convert_fusion.right_ref), custom_call_target="tpu_custom_call" | custom-call | flops 9000000 | bytes 9000 | tf_op jit(solution)/shard_map/far_product/pallas_call | solution.py:544
  385.6 8.3 %collective-permute-done.42.refs_0_ = f32[4,256,2048]{2,1,0:T(8,128)S(1)} collective-permute-done((f32[4,256,2048]{2,1,0:T(8,128)}, f32[4,256,2048]{2,1,0:T(8,128)S(1)}, u32[]{:S(2)}, u32[]{:S(2)}) %collective-permute-start.42) | collective-permute-done | bytes 8388640 | tf_op jit(solution)/shard_map/ppermute | solution.py:405
  397.2 12.6 %near_product.3 = (f32[2,4,32,2048]{3,2,1,0:T(8,128)S(1)}, f32[2,4,32,2048]{3,2,1,0:T(8,128)S(1)}, f32[2,4,32,2048]{3,2,1,0:T(8,128)}, f32[2,4,32,2048]{3,2,1,0:T(8,128)}) custom-call(s32[4]{0:T(128)S(1)} %add_add_fusion.1.place_ref, bf16[784,2016]{1,0:T(8,128)(2,1)} %bitcast.228, bf16[784,2016]{1,0:T(8,128)(2,1)} %copy-done.4, f32[4,256,2048]{2,1,0:T(8,128)} %copy-done.12), custom_call_target="tpu_custom_call" | custom-call | flops 13000000 | bytes 13000 | tf_op jit(solution)/shard_map/near_product/pallas_call | solution.py:571
  411.7 19.0 %conv_wgrad.3 = f32[9,9,56,256]{3,2,1,0:T(8,128)} custom-call(s32[2]{0:T(128)} %pad_add_fusion.2.glob_ref, bf16[784,2016]{1,0:T(8,128)(2,1)} %multiply_convert_fusion.1.refs_0_.refs_1_.refs_2_, bf16[784,2016]{1,0:T(8,128)(2,1)} %multiply_convert_fusion.1.refs_0_.refs_1_.refs_2_, ...), custom_call_target="tpu_custom_call", output_to_operand_aliasing={{}: (11, {})} | custom-call | flops 10000000 | bytes 10000 | tf_op jit(solution)/shard_map/conv_wgrad/pallas_call | solution.py:348
  441.1 16.6 %collective-permute-done.43 = f32[2,4,32,2048]{3,2,1,0:T(8,128)} collective-permute-done((f32[2,4,32,2048]{3,2,1,0:T(8,128)S(1)}, f32[2,4,32,2048]{3,2,1,0:T(8,128)}, u32[]{:S(2)}, u32[]{:S(2)}) %collective-permute-start.43) | collective-permute-done | bytes 2097184 | tf_op jit(solution)/shard_map/ppermute | solution.py:405
  476.3 13.5 %convolution_add_fusion = f32[784,2016]{1,0:T(8,128)} fusion(f32[784,2016]{1,0:T(8,128)} %get-tuple-element.448, bf16[784,2016]{1,0:T(8,128)(2,1)} %copy-done.4, bf16[2016,2016]{1,0:T(8,128)(2,1)} %param.20), kind=kOutput, calls=%fused_computation.19 | convolution fusion | flops 6374333952 | bytes 23933952 | tf_op jit(solution)/shard_map/rv,wv->rw/dot_general | solution.py:1138
  489.8 18.0 %collective-permute-done.50 = f32[4,32,2048]{2,1,0:T(8,128)S(1)} collective-permute-done((f32[4,32,2048]{2,1,0:T(8,128)}, f32[4,32,2048]{2,1,0:T(8,128)S(1)}, u32[]{:S(2)}, u32[]{:S(2)}) %collective-permute-start.50) | collective-permute-done | bytes 1048608 | tf_op jit(solution)/shard_map/ppermute | solution.py:405
  515.3 19.9 %collective-permute-done.52 = f32[2,4,88,256]{3,2,1,0:T(8,128)S(1)} collective-permute-done((f32[2,4,88,256]{3,2,1,0:T(8,128)S(1)}, f32[2,4,88,256]{3,2,1,0:T(8,128)S(1)}, u32[]{:S(2)}, u32[]{:S(2)}) %collective-permute-start.52) | collective-permute-done | bytes 720928 | tf_op jit(solution)/shard_map/ppermute | solution.py:405
  553.6 11.2 %collective-permute-done.55 = f32[1,64,2048]{2,1,0:T(8,128)S(1)} collective-permute-done((f32[1,64,2048]{2,1,0:T(8,128)S(1)}, f32[1,64,2048]{2,1,0:T(8,128)S(1)}, u32[]{:S(2)}, u32[]{:S(2)}) %collective-permute-start.55) | collective-permute-done | bytes 524320 | tf_op jit(solution)/shard_map/ppermute | solution.py:405
  591.3 10.0 %collective-permute-done.66 = f32[1,88,256]{2,1,0:T(8,128)S(1)} collective-permute-done((f32[1,88,256]{2,1,0:T(8,128)S(1)}, f32[1,88,256]{2,1,0:T(8,128)S(1)}, u32[]{:S(2)}, u32[]{:S(2)}) %collective-permute-start.66) | collective-permute-done | bytes 90144 | tf_op jit(solution)/shard_map/ppermute | solution.py:405
  (485 shorter events, 310.6 us)
Async XLA Ops:
  7.2 206.1 %all-gather.3.cloned.1.call-start = ((), (), s32[]{:S(2)}) async-start(), calls=%async_computation | async-start | bytes 2949120 | tf_op jit(solution)/shard_map/all_gather | solution.py:997
  170.3 171.5 %all-gather.5.cloned.1.call-start = ((), (), s32[]{:S(2)}) async-start(), calls=%async_computation.1 | async-start | bytes 2949120 | tf_op jit(solution)/shard_map/all_gather | solution.py:1048
  252.2 367.7 %all-reduce.5.cloned.1.call-start = ((), (), s32[]{:S(2)}) async-start(), calls=%async_computation.2 | async-start | bytes 2048000 | tf_op jit(solution)/shard_map/psum | solution.py:1115
  284.2 48.9 %collective-permute-start.31 = (f32[2,4,32,2048]{3,2,1,0:T(8,128)}, f32[2,4,32,2048]{3,2,1,0:T(8,128)}, u32[]{:S(2)}, u32[]{:S(2)}) collective-permute-start(f32[2,4,32,2048]{3,2,1,0:T(8,128)} %get-tuple-element.217), channel_id=1, source_target_pairs={{0,8},{8,0},{16,24},{24,16},{1,9},{9,1},{17,25},{25,17},{2,10},{10... | collective-permute-start | bytes 6291464 | tf_op jit(solution)/shard_map/ppermute | solution.py:405
  285.6 48.9 %collective-permute-start.32 = (f32[2,4,32,2048]{3,2,1,0:T(8,128)}, f32[2,4,32,2048]{3,2,1,0:T(8,128)}, u32[]{:S(2)}, u32[]{:S(2)}) collective-permute-start(f32[2,4,32,2048]{3,2,1,0:T(8,128)} %get-tuple-element.218), channel_id=1, source_target_pairs={{0,16},{8,24},{16,0},{24,8},{1,17},{9,25},{17,1},{25,9},{2,18},{10... | collective-permute-start | bytes 6291464 | tf_op jit(solution)/shard_map/ppermute | solution.py:405
  311.3 30.5 %collective-permute-start.34 = (f32[1,32,3072]{2,1,0:T(8,128)S(1)}, f32[1,32,3072]{2,1,0:T(8,128)}, u32[]{:S(2)}, u32[]{:S(2)}) collective-permute-start(f32[1,32,3072]{2,1,0:T(8,128)S(1)} %bitcast_add_fusion.3), channel_id=1, source_target_pairs={{0,16},{8,24},{16,0},{24,8},{1,17},{9,25},{17,1},{25,9},{2,18},{10... | collective-permute-start | bytes 1179656 | tf_op jit(solution)/shard_map/ppermute | solution.py:405
  313.3 28.6 %collective-permute-start.35 = (f32[1,32,3072]{2,1,0:T(8,128)S(1)}, f32[1,32,3072]{2,1,0:T(8,128)S(1)}, u32[]{:S(2)}, u32[]{:S(2)}) collective-permute-start(f32[1,32,3072]{2,1,0:T(8,128)S(1)} %bitcast_add_fusion.2), channel_id=1, source_target_pairs={{0,8},{8,0},{16,24},{24,16},{1,9},{9,1},{17,25},{25,17},{2,10},{10... | collective-permute-start | bytes 1179656 | tf_op jit(solution)/shard_map/ppermute | solution.py:405
  355.0 24.2 %collective-permute-start.40 = (f32[4,32,2048]{2,1,0:T(8,128)}, f32[4,32,2048]{2,1,0:T(8,128)S(1)}, u32[]{:S(2)}, u32[]{:S(2)}) collective-permute-start(f32[4,32,2048]{2,1,0:T(8,128)} %get-tuple-element.242), channel_id=1, source_target_pairs={{0,16},{8,24},{16,0},{24,8},{1,17},{9,25},{17,1},{25,9},{2,18},{10... | collective-permute-start | bytes 3145736 | tf_op jit(solution)/shard_map/ppermute | solution.py:405
  356.7 23.8 %collective-permute-start.41 = (f32[4,32,2048]{2,1,0:T(8,128)S(1)}, f32[4,32,2048]{2,1,0:T(8,128)S(1)}, u32[]{:S(2)}, u32[]{:S(2)}) collective-permute-start(f32[4,32,2048]{2,1,0:T(8,128)S(1)} %copy-done.34), channel_id=1, source_target_pairs={{0,8},{8,0},{16,24},{24,16},{1,9},{9,1},{17,25},{25,17},{2,10},{10... | collective-permute-start | bytes 3145736 | tf_op jit(solution)/shard_map/ppermute | solution.py:405
  381.8 49.0 %collective-permute-start.47 = (f32[2,64,2048]{2,1,0:T(8,128)}, f32[2,64,2048]{2,1,0:T(8,128)}, u32[]{:S(2)}, u32[]{:S(2)}) collective-permute-start(f32[2,64,2048]{2,1,0:T(8,128)} %pad_maximum_fusion.6), channel_id=1, source_target_pairs={{0,2},{1,3},{2,0},{3,1},{4,6},{5,7},{6,4},{7,5},{8,10},{9,11},{10,... | collective-permute-start | bytes 3145736 | tf_op jit(solution)/shard_map/ppermute | solution.py:405
  383.5 49.5 %collective-permute-start.45 = (f32[1,2,32,3072]{3,2,1,0:T(8,128)S(1)}, f32[1,2,32,3072]{3,2,1,0:T(8,128)}, u32[]{:S(2)}, u32[]{:S(2)}) collective-permute-start(f32[1,2,32,3072]{3,2,1,0:T(8,128)S(1)} %pad_maximum_fusion.11), channel_id=1, source_target_pairs={{0,8},{8,0},{16,24},{24,16},{1,9},{9,1},{17,25},{25,17},{2,10},{10... | collective-permute-start | bytes 2359304 | tf_op jit(solution)/shard_map/ppermute | solution.py:405
  385.1 48.0 %collective-permute-start.46 = (f32[1,2,32,3072]{3,2,1,0:T(8,128)}, f32[1,2,32,3072]{3,2,1,0:T(8,128)}, u32[]{:S(2)}, u32[]{:S(2)}) collective-permute-start(f32[1,2,32,3072]{3,2,1,0:T(8,128)} %pad_maximum_fusion.12), channel_id=1, source_target_pairs={{0,16},{8,24},{16,0},{24,8},{1,17},{9,25},{17,1},{25,9},{2,18},{10... | collective-permute-start | bytes 2359304 | tf_op jit(solution)/shard_map/ppermute | solution.py:405
  409.9 47.8 %collective-permute-start.43 = (f32[2,4,32,2048]{3,2,1,0:T(8,128)S(1)}, f32[2,4,32,2048]{3,2,1,0:T(8,128)}, u32[]{:S(2)}, u32[]{:S(2)}) collective-permute-start(f32[2,4,32,2048]{3,2,1,0:T(8,128)S(1)} %get-tuple-element.250), channel_id=1, source_target_pairs={{0,8},{8,0},{16,24},{24,16},{1,9},{9,1},{17,25},{25,17},{2,10},{10... | collective-permute-start | bytes 6291464 | tf_op jit(solution)/shard_map/ppermute | solution.py:405
  411.3 47.7 %collective-permute-start.44 = (f32[2,4,32,2048]{3,2,1,0:T(8,128)}, f32[2,4,32,2048]{3,2,1,0:T(8,128)}, u32[]{:S(2)}, u32[]{:S(2)}) collective-permute-start(f32[2,4,32,2048]{3,2,1,0:T(8,128)} %get-tuple-element.251), channel_id=1, source_target_pairs={{0,16},{8,24},{16,0},{24,8},{1,17},{9,25},{17,1},{25,9},{2,18},{10... | collective-permute-start | bytes 6291464 | tf_op jit(solution)/shard_map/ppermute | solution.py:405
  465.4 43.0 %collective-permute-start.48 = (f32[4,704,256]{2,1,0:T(8,128)}, f32[4,704,256]{2,1,0:T(8,128)}, u32[]{:S(2)}, u32[]{:S(2)}) collective-permute-start(f32[4,704,256]{2,1,0:T(8,128)} %units.2), channel_id=1, source_target_pairs={{0,1},{1,0},{2,3},{3,2},{4,5},{5,4},{6,7},{7,6},{8,9},{9,8},{10,11... | collective-permute-start | bytes 8650760 | tf_op jit(solution)/shard_map/ppermute | solution.py:405
  471.5 43.7 %collective-permute-start.54 = (f32[1,64,2048]{2,1,0:T(8,128)}, f32[1,64,2048]{2,1,0:T(8,128)S(1)}, u32[]{:S(2)}, u32[]{:S(2)}) collective-permute-start(f32[1,64,2048]{2,1,0:T(8,128)} %get-tuple-element.290), channel_id=1, source_target_pairs={{0,4},{1,5},{2,6},{3,7},{4,0},{5,1},{6,2},{7,3},{8,12},{9,13},{10,... | collective-permute-start | bytes 1572872 | tf_op jit(solution)/shard_map/ppermute | solution.py:405
  474.1 33.7 %collective-permute-start.50 = (f32[4,32,2048]{2,1,0:T(8,128)}, f32[4,32,2048]{2,1,0:T(8,128)S(1)}, u32[]{:S(2)}, u32[]{:S(2)}) collective-permute-start(f32[4,32,2048]{2,1,0:T(8,128)} %get-tuple-element.283), channel_id=1, source_target_pairs={{0,8},{8,0},{16,24},{24,16},{1,9},{9,1},{17,25},{25,17},{2,10},{10... | collective-permute-start | bytes 3145736 | tf_op jit(solution)/shard_map/ppermute | solution.py:405
  474.8 33.5 %collective-permute-start.49 = (f32[4,32,2048]{2,1,0:T(8,128)}, f32[4,32,2048]{2,1,0:T(8,128)S(1)}, u32[]{:S(2)}, u32[]{:S(2)}) collective-permute-start(f32[4,32,2048]{2,1,0:T(8,128)} %get-tuple-element.281), channel_id=1, source_target_pairs={{0,16},{8,24},{16,0},{24,8},{1,17},{9,25},{17,1},{25,9},{2,18},{10... | collective-permute-start | bytes 3145736 | tf_op jit(solution)/shard_map/ppermute | solution.py:405
  512.0 23.2 %collective-permute-start.52 = (f32[2,4,88,256]{3,2,1,0:T(8,128)S(1)}, f32[2,4,88,256]{3,2,1,0:T(8,128)S(1)}, u32[]{:S(2)}, u32[]{:S(2)}) collective-permute-start(f32[2,4,88,256]{3,2,1,0:T(8,128)S(1)} %get-tuple-element.287), channel_id=1, source_target_pairs={{0,8},{8,0},{16,24},{24,16},{1,9},{9,1},{17,25},{25,17},{2,10},{10... | collective-permute-start | bytes 2162696 | tf_op jit(solution)/shard_map/ppermute | solution.py:405
  514.0 27.1 %collective-permute-start.51 = (f32[2,64,2048]{2,1,0:T(8,128)S(1)}, f32[2,64,2048]{2,1,0:T(8,128)S(1)}, u32[]{:S(2)}, u32[]{:S(2)}) collective-permute-start(f32[2,64,2048]{2,1,0:T(8,128)S(1)} %get-tuple-element.343), channel_id=1, source_target_pairs={{0,2},{1,3},{2,0},{3,1},{4,6},{5,7},{6,4},{7,5},{8,10},{9,11},{10,... | collective-permute-start | bytes 3145736 | tf_op jit(solution)/shard_map/ppermute | solution.py:405
  541.4 23.4 %collective-permute-start.55 = (f32[1,64,2048]{2,1,0:T(8,128)S(1)}, f32[1,64,2048]{2,1,0:T(8,128)S(1)}, u32[]{:S(2)}, u32[]{:S(2)}) collective-permute-start(f32[1,64,2048]{2,1,0:T(8,128)S(1)} %slice.336), channel_id=1, source_target_pairs={{0,4},{1,5},{2,6},{3,7},{4,0},{5,1},{6,2},{7,3},{8,12},{9,13},{10,... | collective-permute-start | bytes 1572872 | tf_op jit(solution)/shard_map/ppermute | solution.py:405
  549.4 27.0 %collective-permute-start.62 = (f32[2,176,256]{2,1,0:T(8,128)}, f32[2,176,256]{2,1,0:T(8,128)}, u32[]{:S(2)}, u32[]{:S(2)}) collective-permute-start(f32[2,176,256]{2,1,0:T(8,128)} %get-tuple-element.379), channel_id=1, source_target_pairs={{0,2},{1,3},{2,0},{3,1},{4,6},{5,7},{6,4},{7,5},{8,10},{9,11},{10,... | collective-permute-start | bytes 1081352 | tf_op jit(solution)/shard_map/ppermute | solution.py:405
  579.8 32.0 %collective-permute-start.63 = (f32[1,2,32,2048]{3,2,1,0:T(8,128)}, f32[1,2,32,2048]{3,2,1,0:T(8,128)}, u32[]{:S(2)}, u32[]{:S(2)}) collective-permute-start(f32[1,2,32,2048]{3,2,1,0:T(8,128)} %pad_maximum_fusion.16), channel_id=1, source_target_pairs={{0,8},{8,0},{16,24},{24,16},{1,9},{9,1},{17,25},{25,17},{2,10},{10... | collective-permute-start | bytes 1572872 | tf_op jit(solution)/shard_map/ppermute | solution.py:405
  581.5 30.2 %collective-permute-start.64 = (f32[1,2,32,2048]{3,2,1,0:T(8,128)}, f32[1,2,32,2048]{3,2,1,0:T(8,128)}, u32[]{:S(2)}, u32[]{:S(2)}) collective-permute-start(f32[1,2,32,2048]{3,2,1,0:T(8,128)} %pad_maximum_fusion.17), channel_id=1, source_target_pairs={{0,16},{8,24},{16,0},{24,8},{1,17},{9,25},{17,1},{25,9},{2,18},{10... | collective-permute-start | bytes 1572872 | tf_op jit(solution)/shard_map/ppermute | solution.py:405
  (118 other events, 1374.5 us)
Sparse Core Ops, SparseCore 0:
  170.4 31.5 all-gather.2
  252.4 32.6 all-gather.4
  470.4 66.6 all-reduce.4

commit v4 on v3

--- a/solution.py
+++ b/solution.py
@@ -1108,16 +1108,21 @@
     sums_one, scale_one, first, second, made = back_rows(
         sums[:2], gain_one, inv_one, early, (seen_gates,) if fast else ()
     )
+    last = jnp.concatenate([sums_one, sums_two, sums_three], axis=0)
+    last = last + swap(last, "crop", 2)
     centred_one = (hidden_one - mean_one) * inv_one
     grad_one_low = (scale_one * (grad_pre_one - first - centred_one * second)).astype(jnp.bfloat16)
     if fast:
         share_red, share_exp = made[-1]
-        share_red, share_exp = lax.psum((share_red, share_exp), "crop")
+        share_red, share_exp = lax.optimization_barrier(
+            lax.psum((share_red, share_exp), "crop")
+        )
         sent_far = far_product(far, inputs, grad_one_low, devices, LOW_COLUMNS)
         flow.sent[id(outs)], sent_far = tie(flow.sent[id(outs)], sent_far)
         outs.take(flow.sent[id(outs)])
         flow.begin(outs)
         arrived = [swap(v, "img", 1) for v in sent_far]
+        last, arrived = tie(last, arrived)
         parts = near_product(near, inputs, grad_one_low, devices, LOW_COLUMNS, arrived)
         ins = HighChain(*parts)
         units, grad_two_low, grad_one_low, ins.keep, ins.away = tie(
@@ -1131,8 +1136,10 @@
         unit_size = gw * gw * PACK
         units = units.reshape(-1, 256)
         swapped = unit_call(far, units, devices, kernel.size, gw)
-        swapped, units, grad_one_low = tie(swapped, units, grad_one_low)
-        swapped, units, grad_one_low = flow.advance(ins, (swapped, units, grad_one_low))
+        flat_protos = protos_sum.result()[:share, :proto_count].reshape(-1)
+        swapped, units, grad_one_low, flat_protos = flow.advance(
+            ins, (swapped, units, grad_one_low, flat_protos)
+        )
         swapped = swap(swapped, "img", 1)
         grad_inputs = (
             jnp.einsum("rv,wv->rw", grad_one_low, w_in, preferred_element_type=jnp.float32)
@@ -1142,15 +1149,24 @@
         gks = HighChain(*unit_call(near, units, devices, kernel.size, gw, swapped))
         flow.begin(gks)
         chains = [ins, outs, gks]
-        last = None
+        last_chain = None
+        flat_out = None
         for chain in (chains[index] for index in TAIL):
-            arrived = flow.sent[id(chain)]
-            if last is not None:
-                arrived, _ = tie(arrived, (last.keep, last.away))
-            chain.take(arrived)
+            landed = flow.sent[id(chain)]
+            if last_chain is not None:
+                landed, _ = tie(landed, (last_chain.keep, last_chain.away))
+            if chain is ins and chain.step == 5:
+                flat_red = share_red.reshape(-1)
+                flat_exp = share_exp.reshape(-1)
+                landed, flat_out, flat_red, flat_exp = tie(landed, flat_out, flat_red, flat_exp)
+            chain.take(landed)
             if chain.step < chain.steps:
                 flow.begin(chain)
-            last = chain
+            if chain is ins and chain.step == 3:
+                share_red, share_exp, _ = tie(share_red, share_exp, (ins.keep, ins.away))
+            if chain is outs and chain.step == chain.steps:
+                flat_out = kept(outs.result()[:, :width]).reshape(-1)
+            last_chain = chain
     else:
         made = None
         for step in steps:
@@ -1161,26 +1177,8 @@
             + grad_summed
         )
 
-    last = jnp.concatenate([sums_one, sums_two, sums_three], axis=0)
-    last = last + swap(last, "crop", 2)
-    tail = (
-        last[5, :squeeze],
-        last[4],
-        last[1],
-        last[0],
-        last[3],
-        last[2],
-        last[7],
-        last[6],
-    )
-    loss_total = last[5, squeeze]
-
     if fast:
         flat_in = kept(ins.result()[:, :width]).reshape(-1)
-        flat_out = kept(outs.result()[:, :width]).reshape(-1)
-        flat_protos = protos_sum.result()[:share, :proto_count].reshape(-1)
-        flat_red = share_red.reshape(-1)
-        flat_exp = share_exp.reshape(-1)
         total = kernel.size // devices
         first_unit = total * img_index // unit_size
         start = unit_start(img_index, total, unit_size, gw, units.size // 256)
@@ -1208,6 +1206,18 @@
             )
             for grad in grads
         )
+    tail = (
+        last[5, :squeeze],
+        last[4],
+        last[1],
+        last[0],
+        last[3],
+        last[2],
+        last[7],
+        last[6],
+    )
+    loss_total = last[5, squeeze]
+
     return (
         loss_total,
         output.astype(jnp.bfloat16).reshape(pixels.shape),

time: 640 us -> 631 us (0.986)
    unnamed x134 -> x124, local copies, waits for them, and re-layouts: 17.5 us -> 15.5 us
  transfers between devices with their start and end apart: 75 -> 75, of which waited for: 38 -> 40; matrix products, arithmetic and copies ran while one was open for 21% -> 19% of each run, Pallas kernels for 19% -> 19%
where the time goes in v4:
time: 631 us; the launch traced here: 622 us
  waiting for transfers between devices  166 us (26%)
  Pallas kernels  145 us (23%)
  matrix products  95.9 us (15%)
  starting transfers between devices  70.1 us (11%)
  other arithmetic  67.6 us (11%)
  local copies, waits for them, and re-layouts  60.2 us (10%)
  between operations  16.4 us (3%)
    ppermute x41, waiting for transfers between devices, swap(): return plain(lax.ppermute(plain(value), axis, pairs))  105 us
    ppermute x28, waiting for transfers between devices, swap(): return lax.ppermute(value, axis, pairs)  58.5 us
    ppermute x41, starting transfers between devices, swap(): return plain(lax.ppermute(plain(value), axis, pairs))  43.8 us
    pallas_call x2, Pallas kernels, conv_wgrad(): pl.pallas_call(functools.partial(conv_kernel, wgrad_step, rows + 2 * EDGE...  35.3 us
    pallas_call x2, Pallas kernels, near_product(): pl.pallas_call(functools.partial(near_kernel, devices, width, height, low...  26.2 us
    pallas_call x1, Pallas kernels, conv_fwd(): pl.pallas_call(functools.partial(conv_kernel, fwd_step, rows + 2 * EDGE,...  23.6 us
    pallas_call x1, Pallas kernels, conv_dgrad(): pl.pallas_call(functools.partial(conv_kernel, dgrad_step, rows + 2 * EDGE...  23 us
    dot_general x3, matrix products, spread_dot(): jnp.dot(jnp.concatenate([member_rows] * 3, axis=1), jnp.concatenate(terms...  18.7 us
  transfers between devices with their start and end apart: 75, of which 40 were waited for; matrix products, arithmetic and copies ran while one was open for 19% of the time, Pallas kernels for 19%

profile of v4, /device:TPU:0, one launch (start us, length us, event | category | flops | bytes accessed | tf_op | source)
XLA Modules:
  0.0 621.5 jit_solution(3017736364647753342)
XLA Ops:
  7.2 12.0 %fusion.91 = (f32[2016]{0:T(1024)S(1)}, f32[2016]{0:T(1024)S(1)}, f32[784,2016]{1,0:T(8,128)}) fusion(bf16[2016,2016]{1,0:T(8,128)(2,1)} %param.20, bf16[1,1,784,2016]{3,2,1,0:T(8,128)(2,1)} %param.17), kind=kOutput, calls=%fused_computation.285 | convolution fusion | flops 6377490944 | bytes 17627904 | tf_op jit(solution)/shard_map/dot_general | solution.py:893
  43.9 23.6 %conv_fwd.1 = (f32[784,2016]{1,0:T(8,128)}, f32[8,2016]{1,0:T(8,128)}) custom-call(s32[1]{0:T(128)} %bitcast.4.glob_ref, f32[784,2016]{1,0:T(8,128)} %get-tuple-element.457.refs_0_.refs_1_.refs_2_.refs_3_.refs_4_.refs_5_, f32[784,2016]{1,0:T(8,128)} %get-tuple-element.457.refs_0_.refs_1_.refs_2_.refs_3_.refs_4_.refs_5_, ...), custom_call_target="tpu_custom_call" | custom-call | flops 20000000 | bytes 20000 | tf_op jit(solution)/shard_map/conv_fwd/pallas_call | solution.py:300
  93.7 10.5 %fusion.90 = (f32[2016]{0:T(1024)S(1)}, f32[2016]{0:T(1024)S(1)}, f32[784,2016]{1,0:T(8,128)S(1)}) fusion(bf16[784,2016]{1,0:T(8,128)(2,1)S(1)} %get-tuple-element.202.left_ref, bf16[2016,2016]{1,0:T(8,128)(2,1)} %param.26), kind=kOutput, calls=%fused_computation.284 | convolution fusion | flops 6377490944 | bytes 17627904 | tf_op jit(solution)/shard_map/dot_general | solution.py:919
  137.7 11.2 %collective-permute-done.14 = f32[16,3000]{1,0:T(8,128)S(1)} collective-permute-done((f32[16,3000]{1,0:T(8,128)S(1)}, f32[16,3000]{1,0:T(8,128)S(1)}, u32[]{:S(2)}, u32[]{:S(2)}) %collective-permute-start.14) | collective-permute-done | bytes 192032 | tf_op jit(solution)/shard_map/ppermute | solution.py:404
  162.6 6.5 %multiply_reduce_fusion.6 = (f32[16]{0:T(128)S(1)}, f32[16,2016]{1,0:T(8,128)S(1)}) fusion(f32[16,2016]{1,0:T(8,128)S(1)} %get-tuple-element.463, bf16[2016,3000]{0,1:T(8,128)(2,1)} %param.33, f32[16,3000]{1,0:T(8,128)S(1)} %subtract_multiply_fusion.2), kind=kOutput, calls=%fused_computation.182 | convolution fusion | flops 193648496 | bytes 12546112 | tf_op jit(solution)/shard_map/sk,wk->sw/dot_general | solution.py:971
  170.1 8.4 %fusion.89 = (f32[2016]{0:T(1024)S(1)}, f32[2016]{0:T(1024)S(1)}, f32[784,2016]{1,0:T(8,128)}) fusion(f32[2016]{0:T(1024)S(1)} %bitcast.241, f32[784,2016]{1,0:T(8,128)} %copy-done.13, f32[2016]{0:T(1024)S(1)} %bitcast.253, f32[2016]{0:T(1024)S(1)} %copy-done.44, f32[2016]{0:T(1024)S(1)} %copy-done.42, bf16[1,1,784,2016]{3,2,1,0:T(8,128)(2,1)} %param.17, ...), kind=kOutput, calls=%fused_computation.283 | convolution fusion | flops 179253312 | bytes 16059904 | tf_op jit(solution)/shard_map/dot_general | solution.py:431
  193.8 6.5 %multiply_convert_fusion.3.right_ref = bf16[784,2016]{1,0:T(8,128)(2,1)S(1)} fusion(f32[784,2016]{1,0:T(8,128)} %get-tuple-element.468, f32[784,2016]{1,0:T(8,128)} %copy-done.13, f32[2016]{0:T(1024)S(1)} %bitcast.285, f32[2016]{0:T(1024)S(1)} %bitcast.284, f32[2016]{0:T(1024)S(1)} %bitcast.243, f32[2016]{0:T(1024)S(1)} %bitcast.254, f32[2016]{0:T(1024)S(1)} %mul.299), kind=kLoop, calls=%fused_computation.5 | loop fusion | flops 11063808 | bytes 15845760 | tf_op jit(solution)/shard_map/convert_element_type | solution.py:983
  200.3 11.5 %fusion.104 = f32[784,2016]{1,0:T(8,128)} fusion(bf16[784,2016]{1,0:T(8,128)(2,1)S(1)} %multiply_convert_fusion.3.right_ref, bf16[2016,2016]{1,0:T(8,128)(2,1)} %param.26), kind=kOutput, calls=%fused_computation.295 | convolution fusion | flops 6372753408 | bytes 17611776 | tf_op jit(solution)/shard_map/rv,wv->rw/dot_general | solution.py:1011
  240.0 8.6 %far_product.2 = f32[4,256,2048]{2,1,0:T(8,128)} custom-call(s32[4]{0:T(128)S(1)} %add_add_fusion.2.place_ref, bf16[784,2016]{1,0:T(8,128)(2,1)S(1)} %copy-done.9, bf16[784,2016]{1,0:T(8,128)(2,1)S(1)} %copy-done.6), custom_call_target="tpu_custom_call" | custom-call | flops 9000000 | bytes 9000 | tf_op jit(solution)/shard_map/far_product/pallas_call | solution.py:544
  261.4 8.1 %multiply_convert_fusion.1.refs_0_.refs_1_.refs_2_ = bf16[784,2016]{1,0:T(8,128)(2,1)} fusion(f32[784,2016]{1,0:T(8,128)} %get-tuple-element.473, f32[784,2016]{1,0:T(8,128)} %get-tuple-element.194, f32[2016]{0:T(1024)S(1)} %bitcast.283, f32[2016]{0:T(1024)S(1)} %bitcast.282, f32[2016]{0:T(1024)S(1)} %mul.340, f32[2016]{0:T(1024)S(1)} %bitcast.262, ...), kind=kLoop, calls=%fused_computation.1 | loop fusion | flops 11063808 | bytes 15845760 | tf_op jit(solution)/shard_map/convert_element_type | solution.py:1066
  269.7 13.2 %near_product.2 = (f32[2,4,32,2048]{3,2,1,0:T(8,128)S(1)}, f32[2,4,32,2048]{3,2,1,0:T(8,128)}, f32[2,4,32,2048]{3,2,1,0:T(8,128)}, f32[2,4,32,2048]{3,2,1,0:T(8,128)}) custom-call(s32[4]{0:T(128)S(1)} %add_add_fusion.1.place_ref, bf16[784,2016]{1,0:T(8,128)(2,1)} %copy-done.8, bf16[784,2016]{1,0:T(8,128)(2,1)} %copy-done.5, ...), custom_call_target="tpu_custom_call" | custom-call | flops 13000000 | bytes 13000 | tf_op jit(solution)/shard_map/near_product/pallas_call | solution.py:571
  288.1 23.0 %conv_dgrad.1 = (f32[784,2016]{1,0:T(8,128)}, f32[8,2016]{1,0:T(8,128)}) custom-call(s32[1]{0:T(128)} %bitcast.4.glob_ref, bf16[784,2016]{1,0:T(8,128)(2,1)} %multiply_convert_fusion.1.refs_0_.refs_1_.refs_2_, bf16[784,2016]{1,0:T(8,128)(2,1)} %multiply_convert_fusion.1.refs_0_.refs_1_.refs_2_, ...), custom_call_target="tpu_custom_call" | custom-call | flops 20000000 | bytes 20000 | tf_op jit(solution)/shard_map/conv_dgrad/pallas_call | solution.py:323
  313.9 16.0 %conv_wgrad.2.refs_10_ = f32[9,9,56,256]{3,2,1,0:T(8,128)} custom-call(s32[2]{0:T(128)} %pad_add_fusion.1.glob_ref, bf16[784,2016]{1,0:T(8,128)(2,1)} %multiply_convert_fusion.1.refs_0_.refs_1_.refs_2_, bf16[784,2016]{1,0:T(8,128)(2,1)} %multiply_convert_fusion.1.refs_0_.refs_1_.refs_2_, bf16[784,2016]{1,0:T(8,128)(2,1)} %multiply_convert_fusion.1.refs_0_.refs_1_.refs_2_, ...), custom_call_target="tpu_custom_call" | custom-call | flops 8000000 | bytes 8000 | tf_op jit(solution)/shard_map/conv_wgrad/pallas_call | solution.py:348
  359.1 6.6 %multiply_convert_fusion.right_ref = bf16[784,2016]{1,0:T(8,128)(2,1)S(1)} fusion(f32[784,2016]{1,0:T(8,128)} %get-tuple-element.457.refs_0_.refs_1_.refs_2_.refs_3_.refs_4_.refs_5_, f32[784,2016]{1,0:T(8,128)} %get-tuple-element.252, f32[2016]{0:T(1024)S(1)} %bitcast.287, f32[2016]{0:T(1024)S(1)} %bitcast.255, f32[2016]{0:T(1024)S(1)} %bitcast.264, ...), kind=kLoop, calls=%fused_computation | loop fusion | flops 11063808 | bytes 15845760 | tf_op jit(solution)/shard_map/convert_element_type | solution.py:1114
  365.7 8.6 %far_product.3 = f32[4,256,2048]{2,1,0:T(8,128)} custom-call(s32[4]{0:T(128)S(1)} %add_add_fusion.2.place_ref, bf16[784,2016]{1,0:T(8,128)(2,1)S(1)} %bitcast.227, bf16[784,2016]{1,0:T(8,128)(2,1)S(1)} %multiply_convert_fusion.right_ref), custom_call_target="tpu_custom_call" | custom-call | flops 9000000 | bytes 9000 | tf_op jit(solution)/shard_map/far_product/pallas_call | solution.py:544
  386.3 7.7 %collective-permute-done.42.refs_0_ = f32[4,256,2048]{2,1,0:T(8,128)} collective-permute-done((f32[4,256,2048]{2,1,0:T(8,128)}, f32[4,256,2048]{2,1,0:T(8,128)}, u32[]{:S(2)}, u32[]{:S(2)}) %collective-permute-start.42) | collective-permute-done | bytes 8388640 | tf_op jit(solution)/shard_map/ppermute | solution.py:405
  394.0 13.0 %near_product.3 = (f32[2,4,32,2048]{3,2,1,0:T(8,128)S(1)}, f32[2,4,32,2048]{3,2,1,0:T(8,128)}, f32[2,4,32,2048]{3,2,1,0:T(8,128)}, f32[2,4,32,2048]{3,2,1,0:T(8,128)}) custom-call(s32[4]{0:T(128)S(1)} %add_add_fusion.1.place_ref, bf16[784,2016]{1,0:T(8,128)(2,1)} %bitcast.226, bf16[784,2016]{1,0:T(8,128)(2,1)} %copy-done.7, ...), custom_call_target="tpu_custom_call" | custom-call | flops 13000000 | bytes 13000 | tf_op jit(solution)/shard_map/near_product/pallas_call | solution.py:571
  409.9 19.2 %conv_wgrad.3 = f32[9,9,56,256]{3,2,1,0:T(8,128)} custom-call(s32[2]{0:T(128)} %pad_add_fusion.2.glob_ref, bf16[784,2016]{1,0:T(8,128)(2,1)} %multiply_convert_fusion.1.refs_0_.refs_1_.refs_2_, bf16[784,2016]{1,0:T(8,128)(2,1)} %multiply_convert_fusion.1.refs_0_.refs_1_.refs_2_, ...), custom_call_target="tpu_custom_call", output_to_operand_aliasing={{}: (11, {})} | custom-call | flops 10000000 | bytes 10000 | tf_op jit(solution)/shard_map/conv_wgrad/pallas_call | solution.py:348
  442.5 13.9 %collective-permute-done.43 = f32[2,4,32,2048]{3,2,1,0:T(8,128)} collective-permute-done((f32[2,4,32,2048]{3,2,1,0:T(8,128)}, f32[2,4,32,2048]{3,2,1,0:T(8,128)}, u32[]{:S(2)}, u32[]{:S(2)}) %collective-permute-start.43) | collective-permute-done | bytes 2097184 | tf_op jit(solution)/shard_map/ppermute | solution.py:405
  468.0 13.8 %convolution_add_fusion = f32[784,2016]{1,0:T(8,128)} fusion(f32[784,2016]{1,0:T(8,128)} %get-tuple-element.468, bf16[784,2016]{1,0:T(8,128)(2,1)} %copy-done.7, bf16[2016,2016]{1,0:T(8,128)(2,1)} %param.20), kind=kOutput, calls=%fused_computation.19 | convolution fusion | flops 6374333952 | bytes 23933952 | tf_op jit(solution)/shard_map/rv,wv->rw/dot_general | solution.py:1145
  481.8 19.1 %collective-permute-done.50 = f32[4,32,2048]{2,1,0:T(8,128)S(1)} collective-permute-done((f32[4,32,2048]{2,1,0:T(8,128)}, f32[4,32,2048]{2,1,0:T(8,128)S(1)}, u32[]{:S(2)}, u32[]{:S(2)}) %collective-permute-start.50) | collective-permute-done | bytes 1048608 | tf_op jit(solution)/shard_map/ppermute | solution.py:405
  511.3 17.2 %collective-permute-done.52 = f32[2,4,88,256]{3,2,1,0:T(8,128)S(1)} collective-permute-done((f32[2,4,88,256]{3,2,1,0:T(8,128)S(1)}, f32[2,4,88,256]{3,2,1,0:T(8,128)S(1)}, u32[]{:S(2)}, u32[]{:S(2)}) %collective-permute-start.52) | collective-permute-done | bytes 720928 | tf_op jit(solution)/shard_map/ppermute | solution.py:405
  548.0 13.0 %collective-permute-done.55 = f32[1,64,2048]{2,1,0:T(8,128)S(1)} collective-permute-done((f32[1,64,2048]{2,1,0:T(8,128)S(1)}, f32[1,64,2048]{2,1,0:T(8,128)S(1)}, u32[]{:S(2)}, u32[]{:S(2)}) %collective-permute-start.55) | collective-permute-done | bytes 524320 | tf_op jit(solution)/shard_map/ppermute | solution.py:405
  585.3 10.1 %collective-permute-done.66 = f32[1,88,256]{2,1,0:T(8,128)S(1)} collective-permute-done((f32[1,88,256]{2,1,0:T(8,128)S(1)}, f32[1,88,256]{2,1,0:T(8,128)S(1)}, u32[]{:S(2)}, u32[]{:S(2)}) %collective-permute-start.66) | collective-permute-done | bytes 90144 | tf_op jit(solution)/shard_map/ppermute | solution.py:405
  (474 shorter events, 303.9 us)
Async XLA Ops:
  7.2 206.2 %all-gather.3.cloned.1.call-start = ((), (), s32[]{:S(2)}) async-start(), calls=%async_computation | async-start | bytes 2949120 | tf_op jit(solution)/shard_map/all_gather | solution.py:997
  170.1 171.5 %all-gather.5.cloned.1.call-start = ((), (), s32[]{:S(2)}) async-start(), calls=%async_computation.1 | async-start | bytes 2949120 | tf_op jit(solution)/shard_map/all_gather | solution.py:1048
  252.4 279.6 %all-reduce.5.cloned.1.call-start = ((), (), s32[]{:S(2)}) async-start(), calls=%async_computation.2 | async-start | bytes 2080768 | tf_op jit(solution)/shard_map/psum | solution.py:1118
  284.2 48.9 %collective-permute-start.31 = (f32[2,4,32,2048]{3,2,1,0:T(8,128)}, f32[2,4,32,2048]{3,2,1,0:T(8,128)}, u32[]{:S(2)}, u32[]{:S(2)}) collective-permute-start(f32[2,4,32,2048]{3,2,1,0:T(8,128)} %get-tuple-element.227), channel_id=1, source_target_pairs={{0,8},{8,0},{16,24},{24,16},{1,9},{9,1},{17,25},{25,17},{2,10},{10... | collective-permute-start | bytes 6291464 | tf_op jit(solution)/shard_map/ppermute | solution.py:405
  285.5 48.9 %collective-permute-start.32 = (f32[2,4,32,2048]{3,2,1,0:T(8,128)}, f32[2,4,32,2048]{3,2,1,0:T(8,128)}, u32[]{:S(2)}, u32[]{:S(2)}) collective-permute-start(f32[2,4,32,2048]{3,2,1,0:T(8,128)} %get-tuple-element.228), channel_id=1, source_target_pairs={{0,16},{8,24},{16,0},{24,8},{1,17},{9,25},{17,1},{25,9},{2,18},{10... | collective-permute-start | bytes 6291464 | tf_op jit(solution)/shard_map/ppermute | solution.py:405
  311.1 30.5 %collective-permute-start.34 = (f32[1,32,3072]{2,1,0:T(8,128)S(1)}, f32[1,32,3072]{2,1,0:T(8,128)}, u32[]{:S(2)}, u32[]{:S(2)}) collective-permute-start(f32[1,32,3072]{2,1,0:T(8,128)S(1)} %bitcast_add_fusion.3), channel_id=1, source_target_pairs={{0,16},{8,24},{16,0},{24,8},{1,17},{9,25},{17,1},{25,9},{2,18},{10... | collective-permute-start | bytes 1179656 | tf_op jit(solution)/shard_map/ppermute | solution.py:405
  313.0 28.6 %collective-permute-start.35 = (f32[1,32,3072]{2,1,0:T(8,128)S(1)}, f32[1,32,3072]{2,1,0:T(8,128)S(1)}, u32[]{:S(2)}, u32[]{:S(2)}) collective-permute-start(f32[1,32,3072]{2,1,0:T(8,128)S(1)} %bitcast_add_fusion.2), channel_id=1, source_target_pairs={{0,8},{8,0},{16,24},{24,16},{1,9},{9,1},{17,25},{25,17},{2,10},{10... | collective-permute-start | bytes 1179656 | tf_op jit(solution)/shard_map/ppermute | solution.py:405
  354.7 24.3 %collective-permute-start.40 = (f32[4,32,2048]{2,1,0:T(8,128)}, f32[4,32,2048]{2,1,0:T(8,128)S(1)}, u32[]{:S(2)}, u32[]{:S(2)}) collective-permute-start(f32[4,32,2048]{2,1,0:T(8,128)} %get-tuple-element.250), channel_id=1, source_target_pairs={{0,16},{8,24},{16,0},{24,8},{1,17},{9,25},{17,1},{25,9},{2,18},{10... | collective-permute-start | bytes 3145736 | tf_op jit(solution)/shard_map/ppermute | solution.py:405
  356.5 24.0 %collective-permute-start.41 = (f32[4,32,2048]{2,1,0:T(8,128)}, f32[4,32,2048]{2,1,0:T(8,128)S(1)}, u32[]{:S(2)}, u32[]{:S(2)}) collective-permute-start(f32[4,32,2048]{2,1,0:T(8,128)} %get-tuple-element.251), channel_id=1, source_target_pairs={{0,8},{8,0},{16,24},{24,16},{1,9},{9,1},{17,25},{25,17},{2,10},{10... | collective-permute-start | bytes 3145736 | tf_op jit(solution)/shard_map/ppermute | solution.py:405
  380.9 48.3 %collective-permute-start.47 = (f32[2,64,2048]{2,1,0:T(8,128)S(1)}, f32[2,64,2048]{2,1,0:T(8,128)S(1)}, u32[]{:S(2)}, u32[]{:S(2)}) collective-permute-start(f32[2,64,2048]{2,1,0:T(8,128)S(1)} %pad_maximum_fusion.6), channel_id=1, source_target_pairs={{0,2},{1,3},{2,0},{3,1},{4,6},{5,7},{6,4},{7,5},{8,10},{9,11},{10,... | collective-permute-start | bytes 3145736 | tf_op jit(solution)/shard_map/ppermute | solution.py:405
  382.9 47.5 %collective-permute-start.45 = (f32[1,2,32,3072]{3,2,1,0:T(8,128)S(1)}, f32[1,2,32,3072]{3,2,1,0:T(8,128)S(1)}, u32[]{:S(2)}, u32[]{:S(2)}) collective-permute-start(f32[1,2,32,3072]{3,2,1,0:T(8,128)S(1)} %pad_maximum_fusion.11), channel_id=1, source_target_pairs={{0,8},{8,0},{16,24},{24,16},{1,9},{9,1},{17,25},{25,17},{2,10},{10... | collective-permute-start | bytes 2359304 | tf_op jit(solution)/shard_map/ppermute | solution.py:405
  384.4 46.0 %collective-permute-start.46 = (f32[1,2,32,3072]{3,2,1,0:T(8,128)S(1)}, f32[1,2,32,3072]{3,2,1,0:T(8,128)S(1)}, u32[]{:S(2)}, u32[]{:S(2)}) collective-permute-start(f32[1,2,32,3072]{3,2,1,0:T(8,128)S(1)} %copy-done.24), channel_id=1, source_target_pairs={{0,16},{8,24},{16,0},{24,8},{1,17},{9,25},{17,1},{25,9},{2,18},{10... | collective-permute-start | bytes 2359304 | tf_op jit(solution)/shard_map/ppermute | solution.py:405
  408.3 48.0 %collective-permute-start.43 = (f32[2,4,32,2048]{3,2,1,0:T(8,128)}, f32[2,4,32,2048]{3,2,1,0:T(8,128)}, u32[]{:S(2)}, u32[]{:S(2)}) collective-permute-start(f32[2,4,32,2048]{3,2,1,0:T(8,128)} %get-tuple-element.262), channel_id=1, source_target_pairs={{0,8},{8,0},{16,24},{24,16},{1,9},{9,1},{17,25},{25,17},{2,10},{10... | collective-permute-start | bytes 6291464 | tf_op jit(solution)/shard_map/ppermute | solution.py:405
  409.5 47.7 %collective-permute-start.44 = (f32[2,4,32,2048]{3,2,1,0:T(8,128)}, f32[2,4,32,2048]{3,2,1,0:T(8,128)}, u32[]{:S(2)}, u32[]{:S(2)}) collective-permute-start(f32[2,4,32,2048]{3,2,1,0:T(8,128)} %get-tuple-element.263), channel_id=1, source_target_pairs={{0,16},{8,24},{16,0},{24,8},{1,17},{9,25},{17,1},{25,9},{2,18},{10... | collective-permute-start | bytes 6291464 | tf_op jit(solution)/shard_map/ppermute | solution.py:405
  464.2 37.4 %collective-permute-start.48 = (f32[4,704,256]{2,1,0:T(8,128)}, f32[4,704,256]{2,1,0:T(8,128)}, u32[]{:S(2)}, u32[]{:S(2)}) collective-permute-start(f32[4,704,256]{2,1,0:T(8,128)} %units.2), channel_id=1, source_target_pairs={{0,1},{1,0},{2,3},{3,2},{4,5},{5,4},{6,7},{7,6},{8,9},{9,8},{10,11... | collective-permute-start | bytes 8650760 | tf_op jit(solution)/shard_map/ppermute | solution.py:405
  464.3 44.3 %collective-permute-start.54 = (f32[1,64,2048]{2,1,0:T(8,128)}, f32[1,64,2048]{2,1,0:T(8,128)S(1)}, u32[]{:S(2)}, u32[]{:S(2)}) collective-permute-start(f32[1,64,2048]{2,1,0:T(8,128)} %get-tuple-element.302), channel_id=1, source_target_pairs={{0,4},{1,5},{2,6},{3,7},{4,0},{5,1},{6,2},{7,3},{8,12},{9,13},{10,... | collective-permute-start | bytes 1572872 | tf_op jit(solution)/shard_map/ppermute | solution.py:405
  466.9 34.0 %collective-permute-start.50 = (f32[4,32,2048]{2,1,0:T(8,128)}, f32[4,32,2048]{2,1,0:T(8,128)S(1)}, u32[]{:S(2)}, u32[]{:S(2)}) collective-permute-start(f32[4,32,2048]{2,1,0:T(8,128)} %get-tuple-element.295), channel_id=1, source_target_pairs={{0,8},{8,0},{16,24},{24,16},{1,9},{9,1},{17,25},{25,17},{2,10},{10... | collective-permute-start | bytes 3145736 | tf_op jit(solution)/shard_map/ppermute | solution.py:405
  467.7 33.7 %collective-permute-start.49 = (f32[4,32,2048]{2,1,0:T(8,128)}, f32[4,32,2048]{2,1,0:T(8,128)S(1)}, u32[]{:S(2)}, u32[]{:S(2)}) collective-permute-start(f32[4,32,2048]{2,1,0:T(8,128)} %get-tuple-element.293), channel_id=1, source_target_pairs={{0,16},{8,24},{16,0},{24,8},{1,17},{9,25},{17,1},{25,9},{2,18},{10... | collective-permute-start | bytes 3145736 | tf_op jit(solution)/shard_map/ppermute | solution.py:405
  505.0 23.5 %collective-permute-start.52 = (f32[2,4,88,256]{3,2,1,0:T(8,128)S(1)}, f32[2,4,88,256]{3,2,1,0:T(8,128)S(1)}, u32[]{:S(2)}, u32[]{:S(2)}) collective-permute-start(f32[2,4,88,256]{3,2,1,0:T(8,128)S(1)} %get-tuple-element.299), channel_id=1, source_target_pairs={{0,8},{8,0},{16,24},{24,16},{1,9},{9,1},{17,25},{25,17},{2,10},{10... | collective-permute-start | bytes 2162696 | tf_op jit(solution)/shard_map/ppermute | solution.py:405
  507.6 28.2 %collective-permute-start.51 = (f32[2,64,2048]{2,1,0:T(8,128)}, f32[2,64,2048]{2,1,0:T(8,128)}, u32[]{:S(2)}, u32[]{:S(2)}) collective-permute-start(f32[2,64,2048]{2,1,0:T(8,128)} %get-tuple-element.363), channel_id=1, source_target_pairs={{0,2},{1,3},{2,0},{3,1},{4,6},{5,7},{6,4},{7,5},{8,10},{9,11},{10,... | collective-permute-start | bytes 3145736 | tf_op jit(solution)/shard_map/ppermute | solution.py:405
  537.2 23.8 %collective-permute-start.55 = (f32[1,64,2048]{2,1,0:T(8,128)S(1)}, f32[1,64,2048]{2,1,0:T(8,128)S(1)}, u32[]{:S(2)}, u32[]{:S(2)}) collective-permute-start(f32[1,64,2048]{2,1,0:T(8,128)S(1)} %slice.336), channel_id=1, source_target_pairs={{0,4},{1,5},{2,6},{3,7},{4,0},{5,1},{6,2},{7,3},{8,12},{9,13},{10,... | collective-permute-start | bytes 1572872 | tf_op jit(solution)/shard_map/ppermute | solution.py:405
  544.6 25.8 %collective-permute-start.62 = (f32[2,176,256]{2,1,0:T(8,128)}, f32[2,176,256]{2,1,0:T(8,128)S(1)}, u32[]{:S(2)}, u32[]{:S(2)}) collective-permute-start(f32[2,176,256]{2,1,0:T(8,128)} %get-tuple-element.399), channel_id=1, source_target_pairs={{0,2},{1,3},{2,0},{3,1},{4,6},{5,7},{6,4},{7,5},{8,10},{9,11},{10,... | collective-permute-start | bytes 1081352 | tf_op jit(solution)/shard_map/ppermute | solution.py:405
  572.7 33.9 %collective-permute-start.63 = (f32[1,2,32,2048]{3,2,1,0:T(8,128)}, f32[1,2,32,2048]{3,2,1,0:T(8,128)}, u32[]{:S(2)}, u32[]{:S(2)}) collective-permute-start(f32[1,2,32,2048]{3,2,1,0:T(8,128)} %pad_maximum_fusion.16), channel_id=1, source_target_pairs={{0,8},{8,0},{16,24},{24,16},{1,9},{9,1},{17,25},{25,17},{2,10},{10... | collective-permute-start | bytes 1572872 | tf_op jit(solution)/shard_map/ppermute | solution.py:405
  574.7 31.9 %collective-permute-start.64 = (f32[1,2,32,2048]{3,2,1,0:T(8,128)}, f32[1,2,32,2048]{3,2,1,0:T(8,128)}, u32[]{:S(2)}, u32[]{:S(2)}) collective-permute-start(f32[1,2,32,2048]{3,2,1,0:T(8,128)} %pad_maximum_fusion.17), channel_id=1, source_target_pairs={{0,16},{8,24},{16,0},{24,8},{1,17},{9,25},{17,1},{25,9},{2,18},{10... | collective-permute-start | bytes 1572872 | tf_op jit(solution)/shard_map/ppermute | solution.py:405
  (114 other events, 1290.0 us)
Sparse Core Ops, SparseCore 0:
  170.2 31.5 all-gather.2
  252.5 32.5 all-gather.4
  464.4 66.1 all-reduce.4

commit v5 on v4

--- a/solution.py
+++ b/solution.py
@@ -937,8 +937,14 @@
     match_matrix = jnp.dot(unit_rows, protos, preferred_element_type=jnp.float32)
 
     every = match_matrix[:IMG_DEV]
-    for mask in bits_of(devices):
-        every = jnp.concatenate([every, swap(every, "img", mask)], axis=0)
+    if devices <= 8:
+        every = jnp.concatenate([every, swap(every, "img", 1)], axis=0)
+        every = jnp.concatenate(
+            [every] + [swap(every, "img", mask) for mask in range(2, devices, 2)], axis=0
+        )
+    else:
+        for mask in bits_of(devices):
+            every = jnp.concatenate([every, swap(every, "img", mask)], axis=0)
     plan_rows = jnp.exp(every / sharpness)
     for sweep_index in range(3):
         plan_rows = plan_rows / jnp.sum(plan_rows, axis=0, keepdims=True)

time: 631 us -> 631 us (level)
  waiting for transfers between devices: 166 us -> 156 us
  starting transfers between devices: 70.1 us -> 76.6 us
    ppermute x28 -> x29, waiting for transfers between devices: 58.5 us -> 48.3 us  [swap(): return lax.ppermute(value, axis, pairs)]
    ppermute x28 -> x29, starting transfers between devices: 17.6 us -> 23.7 us  [swap(): return lax.ppermute(value, axis, pairs)]
    unnamed x124 -> x126, local copies, waits for them, and re-layouts: 15.5 us -> 16.2 us
  transfers between devices with their start and end apart: 75 -> 76, of which waited for: 40 -> 40; matrix products, arithmetic and copies ran while one was open for 19% -> 19% of each run, Pallas kernels for 19% -> 19%
where the time goes in v5:
time: 631 us; the launch traced here: 621 us
  waiting for transfers between devices  156 us (25%)
  Pallas kernels  145 us (23%)
  matrix products  96 us (15%)
  starting transfers between devices  76.6 us (12%)
  other arithmetic  68.7 us (11%)
  local copies, waits for them, and re-layouts  62.7 us (10%)
  between operations  16.3 us (3%)
    ppermute x41, waiting for transfers between devices, swap(): return plain(lax.ppermute(plain(value), axis, pairs))  105 us
    ppermute x29, waiting for transfers between devices, swap(): return lax.ppermute(value, axis, pairs)  48.3 us
    ppermute x41, starting transfers between devices, swap(): return plain(lax.ppermute(plain(value), axis, pairs))  44.1 us
    pallas_call x2, Pallas kernels, conv_wgrad(): pl.pallas_call(functools.partial(conv_kernel, wgrad_step, rows + 2 * EDGE...  35.3 us
    pallas_call x2, Pallas kernels, near_product(): pl.pallas_call(functools.partial(near_kernel, devices, width, height, low...  26.2 us
    ppermute x29, starting transfers between devices, swap(): return lax.ppermute(value, axis, pairs)  23.7 us
    pallas_call x1, Pallas kernels, conv_fwd(): pl.pallas_call(functools.partial(conv_kernel, fwd_step, rows + 2 * EDGE,...  23.6 us
    pallas_call x1, Pallas kernels, conv_dgrad(): pl.pallas_call(functools.partial(conv_kernel, dgrad_step, rows + 2 * EDGE...  23 us
  transfers between devices with their start and end apart: 76, of which 40 were waited for; matrix products, arithmetic and copies ran while one was open for 19% of the time, Pallas kernels for 19%

profile of v5, /device:TPU:0, one launch (start us, length us, event | category | flops | bytes accessed | tf_op | source)
XLA Modules:
  0.0 621.4 jit_solution(11139388057976359489)
XLA Ops:
  7.2 12.0 %fusion.91 = (f32[2016]{0:T(1024)S(1)}, f32[2016]{0:T(1024)S(1)}, f32[784,2016]{1,0:T(8,128)}) fusion(bf16[2016,2016]{1,0:T(8,128)(2,1)} %param.20, bf16[1,1,784,2016]{3,2,1,0:T(8,128)(2,1)} %param.17), kind=kOutput, calls=%fused_computation.284 | convolution fusion | flops 6377490944 | bytes 17627904 | tf_op jit(solution)/shard_map/dot_general | solution.py:893
  43.9 23.6 %conv_fwd.1 = (f32[784,2016]{1,0:T(8,128)}, f32[8,2016]{1,0:T(8,128)}) custom-call(s32[1]{0:T(128)} %bitcast.4.glob_ref, f32[784,2016]{1,0:T(8,128)} %get-tuple-element.456.refs_0_.refs_1_.refs_2_.refs_3_.refs_4_.refs_5_, f32[784,2016]{1,0:T(8,128)} %get-tuple-element.456.refs_0_.refs_1_.refs_2_.refs_3_.refs_4_.refs_5_, ...), custom_call_target="tpu_custom_call" | custom-call | flops 20000000 | bytes 20000 | tf_op jit(solution)/shard_map/conv_fwd/pallas_call | solution.py:300
  93.8 8.8 %fusion.90 = (f32[2016]{0:T(1024)S(1)}, f32[2016]{0:T(1024)S(1)}, f32[784,2016]{1,0:T(8,128)}) fusion(bf16[784,2016]{1,0:T(8,128)(2,1)S(1)} %get-tuple-element.202.left_ref, bf16[2016,2016]{1,0:T(8,128)(2,1)S(1)} %bitcast.305), kind=kOutput, calls=%fused_computation.283 | convolution fusion | flops 6377490944 | bytes 17627904 | tf_op jit(solution)/shard_map/dot_general | solution.py:919
  124.0 7.9 %multiply_reduce_fusion.5 = (f32[16]{0:T(128)S(1)}, f32[16,3000]{1,0:T(8,128)S(1)}) fusion(bf16[2016,3000]{0,1:T(8,128)(2,1)} %param.33, f32[16,2016]{1,0:T(8,128)S(1)} %broadcast_multiply_fusion), kind=kOutput, calls=%fused_computation.164 | convolution fusion | flops 193664240 | bytes 12417088 | tf_op jit(solution)/shard_map/dot_general | solution.py:937
  161.7 6.5 %multiply_reduce_fusion.6 = (f32[16]{0:T(128)S(1)}, f32[16,2016]{1,0:T(8,128)S(1)}) fusion(f32[16,2016]{1,0:T(8,128)S(1)} %get-tuple-element.462, bf16[2016,3000]{0,1:T(8,128)(2,1)} %param.33, f32[16,3000]{1,0:T(8,128)S(1)} %subtract_multiply_fusion.2), kind=kOutput, calls=%fused_computation.180 | convolution fusion | flops 193648496 | bytes 12546112 | tf_op jit(solution)/shard_map/sk,wk->sw/dot_general | solution.py:977
  169.3 8.4 %fusion.89 = (f32[2016]{0:T(1024)S(1)}, f32[2016]{0:T(1024)S(1)}, f32[784,2016]{1,0:T(8,128)}) fusion(f32[2016]{0:T(1024)S(1)} %bitcast.239, f32[784,2016]{1,0:T(8,128)} %get-tuple-element.460, f32[2016]{0:T(1024)S(1)} %bitcast.251, f32[2016]{0:T(1024)S(1)} %copy-done.44, f32[2016]{0:T(1024)S(1)} %copy-done.41, bf16[1,1,784,2016]{3,2,1,0:T(8,128)(2,1)} %param.17, ...), kind=kOutput, calls=%fused_computation.282 | convolution fusion | flops 179253312 | bytes 16059904 | tf_op jit(solution)/shard_map/dot_general | solution.py:431
  193.6 6.5 %multiply_convert_fusion.3.right_ref = bf16[784,2016]{1,0:T(8,128)(2,1)S(1)} fusion(f32[784,2016]{1,0:T(8,128)} %get-tuple-element.467, f32[784,2016]{1,0:T(8,128)} %get-tuple-element.460, f32[2016]{0:T(1024)S(1)} %bitcast.283, f32[2016]{0:T(1024)S(1)} %bitcast.282, f32[2016]{0:T(1024)S(1)} %bitcast.241, f32[2016]{0:T(1024)S(1)} %bitcast.252, f32[2016]{0:T(1024)S(1)} %mul.299), kind=kLoop, calls=%fused_computation.5 | loop fusion | flops 11063808 | bytes 15845760 | tf_op jit(solution)/shard_map/convert_element_type | solution.py:989
  200.1 11.5 %fusion.102 = f32[784,2016]{1,0:T(8,128)} fusion(bf16[784,2016]{1,0:T(8,128)(2,1)S(1)} %multiply_convert_fusion.3.right_ref, bf16[2016,2016]{1,0:T(8,128)(2,1)} %param.26), kind=kOutput, calls=%fused_computation.293 | convolution fusion | flops 6372753408 | bytes 17611776 | tf_op jit(solution)/shard_map/rv,wv->rw/dot_general | solution.py:1017
  239.8 8.6 %far_product.2 = f32[4,256,2048]{2,1,0:T(8,128)} custom-call(s32[4]{0:T(128)S(1)} %add_add_fusion.2.place_ref, bf16[784,2016]{1,0:T(8,128)(2,1)S(1)} %copy-done.8, bf16[784,2016]{1,0:T(8,128)(2,1)S(1)} %copy-done.5), custom_call_target="tpu_custom_call" | custom-call | flops 9000000 | bytes 9000 | tf_op jit(solution)/shard_map/far_product/pallas_call | solution.py:544
  261.2 8.1 %multiply_convert_fusion.1.refs_0_.refs_1_.refs_2_ = bf16[784,2016]{1,0:T(8,128)(2,1)} fusion(f32[784,2016]{1,0:T(8,128)} %get-tuple-element.472, f32[784,2016]{1,0:T(8,128)} %get-tuple-element.194, f32[2016]{0:T(1024)S(1)} %bitcast.281, f32[2016]{0:T(1024)S(1)} %bitcast.280, f32[2016]{0:T(1024)S(1)} %mul.340, f32[2016]{0:T(1024)S(1)} %bitcast.260, ...), kind=kLoop, calls=%fused_computation.1 | loop fusion | flops 11063808 | bytes 15845760 | tf_op jit(solution)/shard_map/convert_element_type | solution.py:1072
  269.5 13.2 %near_product.2 = (f32[2,4,32,2048]{3,2,1,0:T(8,128)S(1)}, f32[2,4,32,2048]{3,2,1,0:T(8,128)}, f32[2,4,32,2048]{3,2,1,0:T(8,128)}, f32[2,4,32,2048]{3,2,1,0:T(8,128)}) custom-call(s32[4]{0:T(128)S(1)} %add_add_fusion.1.place_ref, bf16[784,2016]{1,0:T(8,128)(2,1)} %copy-done.7, bf16[784,2016]{1,0:T(8,128)(2,1)} %copy-done.4, ...), custom_call_target="tpu_custom_call" | custom-call | flops 13000000 | bytes 13000 | tf_op jit(solution)/shard_map/near_product/pallas_call | solution.py:571
  287.9 23.0 %conv_dgrad.1 = (f32[784,2016]{1,0:T(8,128)}, f32[8,2016]{1,0:T(8,128)}) custom-call(s32[1]{0:T(128)} %bitcast.4.glob_ref, bf16[784,2016]{1,0:T(8,128)(2,1)} %multiply_convert_fusion.1.refs_0_.refs_1_.refs_2_, bf16[784,2016]{1,0:T(8,128)(2,1)} %multiply_convert_fusion.1.refs_0_.refs_1_.refs_2_, ...), custom_call_target="tpu_custom_call" | custom-call | flops 20000000 | bytes 20000 | tf_op jit(solution)/shard_map/conv_dgrad/pallas_call | solution.py:323
  313.7 16.0 %conv_wgrad.2.refs_10_ = f32[9,9,56,256]{3,2,1,0:T(8,128)} custom-call(s32[2]{0:T(128)} %pad_add_fusion.1.glob_ref, bf16[784,2016]{1,0:T(8,128)(2,1)} %multiply_convert_fusion.1.refs_0_.refs_1_.refs_2_, bf16[784,2016]{1,0:T(8,128)(2,1)} %multiply_convert_fusion.1.refs_0_.refs_1_.refs_2_, bf16[784,2016]{1,0:T(8,128)(2,1)} %multiply_convert_fusion.1.refs_0_.refs_1_.refs_2_, ...), custom_call_target="tpu_custom_call" | custom-call | flops 8000000 | bytes 8000 | tf_op jit(solution)/shard_map/conv_wgrad/pallas_call | solution.py:348
  359.0 6.6 %multiply_convert_fusion.right_ref = bf16[784,2016]{1,0:T(8,128)(2,1)S(1)} fusion(f32[784,2016]{1,0:T(8,128)} %get-tuple-element.456.refs_0_.refs_1_.refs_2_.refs_3_.refs_4_.refs_5_, f32[784,2016]{1,0:T(8,128)} %get-tuple-element.252, f32[2016]{0:T(1024)S(1)} %bitcast.285, f32[2016]{0:T(1024)S(1)} %bitcast.253, f32[2016]{0:T(1024)S(1)} %bitcast.262, ...), kind=kLoop, calls=%fused_computation | loop fusion | flops 11063808 | bytes 15845760 | tf_op jit(solution)/shard_map/convert_element_type | solution.py:1120
  365.6 8.6 %far_product.3 = f32[4,256,2048]{2,1,0:T(8,128)} custom-call(s32[4]{0:T(128)S(1)} %add_add_fusion.2.place_ref, bf16[784,2016]{1,0:T(8,128)(2,1)S(1)} %bitcast.227, bf16[784,2016]{1,0:T(8,128)(2,1)S(1)} %multiply_convert_fusion.right_ref), custom_call_target="tpu_custom_call" | custom-call | flops 9000000 | bytes 9000 | tf_op jit(solution)/shard_map/far_product/pallas_call | solution.py:544
  386.4 7.5 %collective-permute-done.43.refs_0_ = f32[4,256,2048]{2,1,0:T(8,128)} collective-permute-done((f32[4,256,2048]{2,1,0:T(8,128)}, f32[4,256,2048]{2,1,0:T(8,128)}, u32[]{:S(2)}, u32[]{:S(2)}) %collective-permute-start.43) | collective-permute-done | bytes 8388640 | tf_op jit(solution)/shard_map/ppermute | solution.py:405
  393.8 13.0 %near_product.3 = (f32[2,4,32,2048]{3,2,1,0:T(8,128)S(1)}, f32[2,4,32,2048]{3,2,1,0:T(8,128)}, f32[2,4,32,2048]{3,2,1,0:T(8,128)}, f32[2,4,32,2048]{3,2,1,0:T(8,128)}) custom-call(s32[4]{0:T(128)S(1)} %add_add_fusion.1.place_ref, bf16[784,2016]{1,0:T(8,128)(2,1)} %bitcast.226, bf16[784,2016]{1,0:T(8,128)(2,1)} %copy-done.6, ...), custom_call_target="tpu_custom_call" | custom-call | flops 13000000 | bytes 13000 | tf_op jit(solution)/shard_map/near_product/pallas_call | solution.py:571
  409.8 19.2 %conv_wgrad.3 = f32[9,9,56,256]{3,2,1,0:T(8,128)} custom-call(s32[2]{0:T(128)} %pad_add_fusion.2.glob_ref, bf16[784,2016]{1,0:T(8,128)(2,1)} %multiply_convert_fusion.1.refs_0_.refs_1_.refs_2_, bf16[784,2016]{1,0:T(8,128)(2,1)} %multiply_convert_fusion.1.refs_0_.refs_1_.refs_2_, ...), custom_call_target="tpu_custom_call", output_to_operand_aliasing={{}: (11, {})} | custom-call | flops 10000000 | bytes 10000 | tf_op jit(solution)/shard_map/conv_wgrad/pallas_call | solution.py:348
  442.3 13.8 %collective-permute-done.44 = f32[2,4,32,2048]{3,2,1,0:T(8,128)} collective-permute-done((f32[2,4,32,2048]{3,2,1,0:T(8,128)}, f32[2,4,32,2048]{3,2,1,0:T(8,128)}, u32[]{:S(2)}, u32[]{:S(2)}) %collective-permute-start.44) | collective-permute-done | bytes 2097184 | tf_op jit(solution)/shard_map/ppermute | solution.py:405
  467.8 13.8 %convolution_add_fusion = f32[784,2016]{1,0:T(8,128)} fusion(f32[784,2016]{1,0:T(8,128)} %get-tuple-element.467, bf16[784,2016]{1,0:T(8,128)(2,1)} %copy-done.6, bf16[2016,2016]{1,0:T(8,128)(2,1)} %param.20), kind=kOutput, calls=%fused_computation.19 | convolution fusion | flops 6374333952 | bytes 23933952 | tf_op jit(solution)/shard_map/rv,wv->rw/dot_general | solution.py:1151
  481.6 19.2 %collective-permute-done.51 = f32[4,32,2048]{2,1,0:T(8,128)S(1)} collective-permute-done((f32[4,32,2048]{2,1,0:T(8,128)}, f32[4,32,2048]{2,1,0:T(8,128)S(1)}, u32[]{:S(2)}, u32[]{:S(2)}) %collective-permute-start.51) | collective-permute-done | bytes 1048608 | tf_op jit(solution)/shard_map/ppermute | solution.py:405
  511.2 17.2 %collective-permute-done.53 = f32[2,4,88,256]{3,2,1,0:T(8,128)S(1)} collective-permute-done((f32[2,4,88,256]{3,2,1,0:T(8,128)S(1)}, f32[2,4,88,256]{3,2,1,0:T(8,128)S(1)}, u32[]{:S(2)}, u32[]{:S(2)}) %collective-permute-start.53) | collective-permute-done | bytes 720928 | tf_op jit(solution)/shard_map/ppermute | solution.py:405
  547.9 13.0 %collective-permute-done.56 = f32[1,64,2048]{2,1,0:T(8,128)S(1)} collective-permute-done((f32[1,64,2048]{2,1,0:T(8,128)S(1)}, f32[1,64,2048]{2,1,0:T(8,128)S(1)}, u32[]{:S(2)}, u32[]{:S(2)}) %collective-permute-start.56) | collective-permute-done | bytes 524320 | tf_op jit(solution)/shard_map/ppermute | solution.py:405
  585.1 10.2 %collective-permute-done.67 = f32[1,88,256]{2,1,0:T(8,128)S(1)} collective-permute-done((f32[1,88,256]{2,1,0:T(8,128)S(1)}, f32[1,88,256]{2,1,0:T(8,128)S(1)}, u32[]{:S(2)}, u32[]{:S(2)}) %collective-permute-start.67) | collective-permute-done | bytes 90144 | tf_op jit(solution)/shard_map/ppermute | solution.py:405
  (478 shorter events, 309.1 us)
Async XLA Ops:
  7.2 206.0 %all-gather.3.cloned.1.call-start = ((), (), s32[]{:S(2)}) async-start(), calls=%async_computation | async-start | bytes 2949120 | tf_op jit(solution)/shard_map/all_gather | solution.py:1003
  169.2 172.3 %all-gather.5.cloned.1.call-start = ((), (), s32[]{:S(2)}) async-start(), calls=%async_computation.1 | async-start | bytes 2949120 | tf_op jit(solution)/shard_map/all_gather | solution.py:1054
  252.2 279.7 %all-reduce.5.cloned.1.call-start = ((), (), s32[]{:S(2)}) async-start(), calls=%async_computation.2 | async-start | bytes 2080768 | tf_op jit(solution)/shard_map/psum | solution.py:1124
  284.0 48.9 %collective-permute-start.32 = (f32[2,4,32,2048]{3,2,1,0:T(8,128)}, f32[2,4,32,2048]{3,2,1,0:T(8,128)}, u32[]{:S(2)}, u32[]{:S(2)}) collective-permute-start(f32[2,4,32,2048]{3,2,1,0:T(8,128)} %get-tuple-element.227), channel_id=1, source_target_pairs={{0,8},{8,0},{16,24},{24,16},{1,9},{9,1},{17,25},{25,17},{2,10},{10... | collective-permute-start | bytes 6291464 | tf_op jit(solution)/shard_map/ppermute | solution.py:405
  285.3 48.9 %collective-permute-start.33 = (f32[2,4,32,2048]{3,2,1,0:T(8,128)}, f32[2,4,32,2048]{3,2,1,0:T(8,128)}, u32[]{:S(2)}, u32[]{:S(2)}) collective-permute-start(f32[2,4,32,2048]{3,2,1,0:T(8,128)} %get-tuple-element.228), channel_id=1, source_target_pairs={{0,16},{8,24},{16,0},{24,8},{1,17},{9,25},{17,1},{25,9},{2,18},{10... | collective-permute-start | bytes 6291464 | tf_op jit(solution)/shard_map/ppermute | solution.py:405
  310.9 30.5 %collective-permute-start.35 = (f32[1,32,3072]{2,1,0:T(8,128)S(1)}, f32[1,32,3072]{2,1,0:T(8,128)}, u32[]{:S(2)}, u32[]{:S(2)}) collective-permute-start(f32[1,32,3072]{2,1,0:T(8,128)S(1)} %bitcast_add_fusion.3), channel_id=1, source_target_pairs={{0,16},{8,24},{16,0},{24,8},{1,17},{9,25},{17,1},{25,9},{2,18},{10... | collective-permute-start | bytes 1179656 | tf_op jit(solution)/shard_map/ppermute | solution.py:405
  312.9 28.6 %collective-permute-start.36 = (f32[1,32,3072]{2,1,0:T(8,128)S(1)}, f32[1,32,3072]{2,1,0:T(8,128)S(1)}, u32[]{:S(2)}, u32[]{:S(2)}) collective-permute-start(f32[1,32,3072]{2,1,0:T(8,128)S(1)} %bitcast_add_fusion.2), channel_id=1, source_target_pairs={{0,8},{8,0},{16,24},{24,16},{1,9},{9,1},{17,25},{25,17},{2,10},{10... | collective-permute-start | bytes 1179656 | tf_op jit(solution)/shard_map/ppermute | solution.py:405
  354.7 24.2 %collective-permute-start.41 = (f32[4,32,2048]{2,1,0:T(8,128)}, f32[4,32,2048]{2,1,0:T(8,128)S(1)}, u32[]{:S(2)}, u32[]{:S(2)}) collective-permute-start(f32[4,32,2048]{2,1,0:T(8,128)} %get-tuple-element.250), channel_id=1, source_target_pairs={{0,16},{8,24},{16,0},{24,8},{1,17},{9,25},{17,1},{25,9},{2,18},{10... | collective-permute-start | bytes 3145736 | tf_op jit(solution)/shard_map/ppermute | solution.py:405
  356.3 24.0 %collective-permute-start.42 = (f32[4,32,2048]{2,1,0:T(8,128)}, f32[4,32,2048]{2,1,0:T(8,128)S(1)}, u32[]{:S(2)}, u32[]{:S(2)}) collective-permute-start(f32[4,32,2048]{2,1,0:T(8,128)} %get-tuple-element.251), channel_id=1, source_target_pairs={{0,8},{8,0},{16,24},{24,16},{1,9},{9,1},{17,25},{25,17},{2,10},{10... | collective-permute-start | bytes 3145736 | tf_op jit(solution)/shard_map/ppermute | solution.py:405
  380.7 48.3 %collective-permute-start.48 = (f32[2,64,2048]{2,1,0:T(8,128)S(1)}, f32[2,64,2048]{2,1,0:T(8,128)S(1)}, u32[]{:S(2)}, u32[]{:S(2)}) collective-permute-start(f32[2,64,2048]{2,1,0:T(8,128)S(1)} %pad_maximum_fusion.6), channel_id=1, source_target_pairs={{0,2},{1,3},{2,0},{3,1},{4,6},{5,7},{6,4},{7,5},{8,10},{9,11},{10,... | collective-permute-start | bytes 3145736 | tf_op jit(solution)/shard_map/ppermute | solution.py:405
  382.9 47.4 %collective-permute-start.46 = (f32[1,2,32,3072]{3,2,1,0:T(8,128)S(1)}, f32[1,2,32,3072]{3,2,1,0:T(8,128)S(1)}, u32[]{:S(2)}, u32[]{:S(2)}) collective-permute-start(f32[1,2,32,3072]{3,2,1,0:T(8,128)S(1)} %pad_maximum_fusion.11), channel_id=1, source_target_pairs={{0,8},{8,0},{16,24},{24,16},{1,9},{9,1},{17,25},{25,17},{2,10},{10... | collective-permute-start | bytes 2359304 | tf_op jit(solution)/shard_map/ppermute | solution.py:405
  384.4 45.9 %collective-permute-start.47 = (f32[1,2,32,3072]{3,2,1,0:T(8,128)S(1)}, f32[1,2,32,3072]{3,2,1,0:T(8,128)S(1)}, u32[]{:S(2)}, u32[]{:S(2)}) collective-permute-start(f32[1,2,32,3072]{3,2,1,0:T(8,128)S(1)} %copy-done.22), channel_id=1, source_target_pairs={{0,16},{8,24},{16,0},{24,8},{1,17},{9,25},{17,1},{25,9},{2,18},{10... | collective-permute-start | bytes 2359304 | tf_op jit(solution)/shard_map/ppermute | solution.py:405
  408.1 48.0 %collective-permute-start.44 = (f32[2,4,32,2048]{3,2,1,0:T(8,128)}, f32[2,4,32,2048]{3,2,1,0:T(8,128)}, u32[]{:S(2)}, u32[]{:S(2)}) collective-permute-start(f32[2,4,32,2048]{3,2,1,0:T(8,128)} %get-tuple-element.262), channel_id=1, source_target_pairs={{0,8},{8,0},{16,24},{24,16},{1,9},{9,1},{17,25},{25,17},{2,10},{10... | collective-permute-start | bytes 6291464 | tf_op jit(solution)/shard_map/ppermute | solution.py:405
  409.4 47.7 %collective-permute-start.45 = (f32[2,4,32,2048]{3,2,1,0:T(8,128)}, f32[2,4,32,2048]{3,2,1,0:T(8,128)}, u32[]{:S(2)}, u32[]{:S(2)}) collective-permute-start(f32[2,4,32,2048]{3,2,1,0:T(8,128)} %get-tuple-element.263), channel_id=1, source_target_pairs={{0,16},{8,24},{16,0},{24,8},{1,17},{9,25},{17,1},{25,9},{2,18},{10... | collective-permute-start | bytes 6291464 | tf_op jit(solution)/shard_map/ppermute | solution.py:405
  464.1 37.4 %collective-permute-start.49 = (f32[4,704,256]{2,1,0:T(8,128)}, f32[4,704,256]{2,1,0:T(8,128)}, u32[]{:S(2)}, u32[]{:S(2)}) collective-permute-start(f32[4,704,256]{2,1,0:T(8,128)} %units.2), channel_id=1, source_target_pairs={{0,1},{1,0},{2,3},{3,2},{4,5},{5,4},{6,7},{7,6},{8,9},{9,8},{10,11... | collective-permute-start | bytes 8650760 | tf_op jit(solution)/shard_map/ppermute | solution.py:405
  464.1 44.3 %collective-permute-start.55 = (f32[1,64,2048]{2,1,0:T(8,128)}, f32[1,64,2048]{2,1,0:T(8,128)S(1)}, u32[]{:S(2)}, u32[]{:S(2)}) collective-permute-start(f32[1,64,2048]{2,1,0:T(8,128)} %get-tuple-element.302), channel_id=1, source_target_pairs={{0,4},{1,5},{2,6},{3,7},{4,0},{5,1},{6,2},{7,3},{8,12},{9,13},{10,... | collective-permute-start | bytes 1572872 | tf_op jit(solution)/shard_map/ppermute | solution.py:405
  466.7 34.0 %collective-permute-start.51 = (f32[4,32,2048]{2,1,0:T(8,128)}, f32[4,32,2048]{2,1,0:T(8,128)S(1)}, u32[]{:S(2)}, u32[]{:S(2)}) collective-permute-start(f32[4,32,2048]{2,1,0:T(8,128)} %get-tuple-element.295), channel_id=1, source_target_pairs={{0,8},{8,0},{16,24},{24,16},{1,9},{9,1},{17,25},{25,17},{2,10},{10... | collective-permute-start | bytes 3145736 | tf_op jit(solution)/shard_map/ppermute | solution.py:405
  467.6 33.7 %collective-permute-start.50 = (f32[4,32,2048]{2,1,0:T(8,128)}, f32[4,32,2048]{2,1,0:T(8,128)S(1)}, u32[]{:S(2)}, u32[]{:S(2)}) collective-permute-start(f32[4,32,2048]{2,1,0:T(8,128)} %get-tuple-element.293), channel_id=1, source_target_pairs={{0,16},{8,24},{16,0},{24,8},{1,17},{9,25},{17,1},{25,9},{2,18},{10... | collective-permute-start | bytes 3145736 | tf_op jit(solution)/shard_map/ppermute | solution.py:405
  504.9 23.5 %collective-permute-start.53 = (f32[2,4,88,256]{3,2,1,0:T(8,128)S(1)}, f32[2,4,88,256]{3,2,1,0:T(8,128)S(1)}, u32[]{:S(2)}, u32[]{:S(2)}) collective-permute-start(f32[2,4,88,256]{3,2,1,0:T(8,128)S(1)} %get-tuple-element.299), channel_id=1, source_target_pairs={{0,8},{8,0},{16,24},{24,16},{1,9},{9,1},{17,25},{25,17},{2,10},{10... | collective-permute-start | bytes 2162696 | tf_op jit(solution)/shard_map/ppermute | solution.py:405
  507.5 28.3 %collective-permute-start.52 = (f32[2,64,2048]{2,1,0:T(8,128)}, f32[2,64,2048]{2,1,0:T(8,128)}, u32[]{:S(2)}, u32[]{:S(2)}) collective-permute-start(f32[2,64,2048]{2,1,0:T(8,128)} %get-tuple-element.361), channel_id=1, source_target_pairs={{0,2},{1,3},{2,0},{3,1},{4,6},{5,7},{6,4},{7,5},{8,10},{9,11},{10,... | collective-permute-start | bytes 3145736 | tf_op jit(solution)/shard_map/ppermute | solution.py:405
  537.1 23.7 %collective-permute-start.56 = (f32[1,64,2048]{2,1,0:T(8,128)S(1)}, f32[1,64,2048]{2,1,0:T(8,128)S(1)}, u32[]{:S(2)}, u32[]{:S(2)}) collective-permute-start(f32[1,64,2048]{2,1,0:T(8,128)S(1)} %slice.336), channel_id=1, source_target_pairs={{0,4},{1,5},{2,6},{3,7},{4,0},{5,1},{6,2},{7,3},{8,12},{9,13},{10,... | collective-permute-start | bytes 1572872 | tf_op jit(solution)/shard_map/ppermute | solution.py:405
  544.5 25.8 %collective-permute-start.63 = (f32[2,176,256]{2,1,0:T(8,128)}, f32[2,176,256]{2,1,0:T(8,128)S(1)}, u32[]{:S(2)}, u32[]{:S(2)}) collective-permute-start(f32[2,176,256]{2,1,0:T(8,128)} %get-tuple-element.397), channel_id=1, source_target_pairs={{0,2},{1,3},{2,0},{3,1},{4,6},{5,7},{6,4},{7,5},{8,10},{9,11},{10,... | collective-permute-start | bytes 1081352 | tf_op jit(solution)/shard_map/ppermute | solution.py:405
  572.6 33.9 %collective-permute-start.64 = (f32[1,2,32,2048]{3,2,1,0:T(8,128)}, f32[1,2,32,2048]{3,2,1,0:T(8,128)}, u32[]{:S(2)}, u32[]{:S(2)}) collective-permute-start(f32[1,2,32,2048]{3,2,1,0:T(8,128)} %pad_maximum_fusion.16), channel_id=1, source_target_pairs={{0,8},{8,0},{16,24},{24,16},{1,9},{9,1},{17,25},{25,17},{2,10},{10... | collective-permute-start | bytes 1572872 | tf_op jit(solution)/shard_map/ppermute | solution.py:405
  574.5 31.9 %collective-permute-start.65 = (f32[1,2,32,2048]{3,2,1,0:T(8,128)}, f32[1,2,32,2048]{3,2,1,0:T(8,128)}, u32[]{:S(2)}, u32[]{:S(2)}) collective-permute-start(f32[1,2,32,2048]{3,2,1,0:T(8,128)} %pad_maximum_fusion.17), channel_id=1, source_target_pairs={{0,16},{8,24},{16,0},{24,8},{1,17},{9,25},{17,1},{25,9},{2,18},{10... | collective-permute-start | bytes 1572872 | tf_op jit(solution)/shard_map/ppermute | solution.py:405
  (116 other events, 1198.6 us)
Sparse Core Ops, SparseCore 0:
  169.3 31.7 all-gather.2
  252.4 32.7 all-gather.4
  464.2 66.1 all-reduce.4
